TPU v7x, 32 devices: a whole 2x2x4 slice. The times are simulated.
32 devices in a mesh: groups: 2 (over y), dp: 16 (over z, x, core).
Axes of the slice: x: 2, y: 2, z: 4, core: 2. Of those that a mesh axis runs over, the one named last changes fastest.
Arguments:
- acts: bfloat16 [4096, 8192], P(('groups', 'dp')), parts along dimension 0, may hold values from -6 to 6
- grad_out: bfloat16 [4096, 1024], P(('groups', 'dp')), parts along dimension 0, may hold values from -6 to 6
- row_adapter: int32 [4096, 1], P(('groups', 'dp')), parts along dimension 0, may hold values from 0 to 63; in each aligned block of 128 rows (0 to 127, 128 to 255, ...) at most 4 rows name the same one
- ranks: int32 [64], replicated, may hold values from 8 to 64
- owner_map: int32 [128], replicated, may hold values from 0 to 127, each once
- down_slots: float32 [256, 32, 8192], P(('groups', 'dp')), parts along dimension 0, may hold values from -0.0625 to 0.0625
- up_slots: float32 [256, 32, 1024], P(('groups', 'dp')), parts along dimension 0, may hold values from -0.1875 to 0.1875
- down_first: float32 [256, 32, 8192], P(('groups', 'dp')), parts along dimension 0, may hold values from -0.0029296875 to 0.0029296875
- down_second: float32 [256, 32, 8192], P(('groups', 'dp')), parts along dimension 0, may hold values from 1e-09 to 1e-07
- up_first: float32 [256, 32, 1024], P(('groups', 'dp')), parts along dimension 0, may hold values from -0.0029296875 to 0.0029296875
- up_second: float32 [256, 32, 1024], P(('groups', 'dp')), parts along dimension 0, may hold values from 1e-09 to 1e-07
Outputs:
- input_grad: bfloat16 [4096, 8192], P(('groups', 'dp')), parts along dimension 0
- new_down: float32 [256, 32, 8192], P(('groups', 'dp')), parts along dimension 0
- new_up: float32 [256, 32, 1024], P(('groups', 'dp')), parts along dimension 0
- new_down_first: float32 [256, 32, 8192], P(('groups', 'dp')), parts along dimension 0
- new_down_second: float32 [256, 32, 8192], P(('groups', 'dp')), parts along dimension 0
- new_up_first: float32 [256, 32, 1024], P(('groups', 'dp')), parts along dimension 0
- new_up_second: float32 [256, 32, 1024], P(('groups', 'dp')), parts along dimension 0
There are 2 independent parts, one for each index of `groups`. A program takes and returns all parts, laid end to end along the dimension named above; an argument that names none is the same for every part. Nothing has to cross between parts.
Inputs may be any that keep to these rules, and one draw needn't show every extreme that they name: `row_adapter`: within the rows of one device no adapter appears on more than 4 rows, and some adapter on exactly 4. `owner_map`: A permutation of the slots; slot s lies on device s // 8 of dp, as entry s % 8 of its share.
All inputs are finite; a program needn't handle non-finite values.
Results may differ from a plain program's by a relative error of at most 0.0067.
Values may be sent and summed in bfloat16 or wider, within the bound.
No kernel may reach another device: no remote copies, remote signals or barrier semaphores. Data moves between devices by JAX's collectives and lax.ppermute only.
A program may use at most 192 MiB of HBM per device.

v0:
```python
import jax
import jax.numpy as jnp
from jax import lax
from jax.sharding import PartitionSpec as P

adapter_alpha_value = 16.0
clip_limit = 1.0
norm_eps = 1e-06
beta_one = 0.9
beta_two = 0.999
bias_one = 0.9999734386011124
bias_two = 0.0952078528862904
learn_rate = 0.0002
decay_rate = 0.01
adam_eps = 1e-08


def adamw_update(params, moment, second, gradient, clip_factor):
    clipped = clip_factor * gradient
    moment = beta_one * moment + (1.0 - beta_one) * clipped
    second = beta_two * second + (1.0 - beta_two) * clipped * clipped
    params = params - learn_rate * (
        moment / bias_one / (jnp.sqrt(second / bias_two) + adam_eps) + decay_rate * params
    )
    return (params, moment, second)


def send_back(piece_list, slots_total, model_width):
    returned = lax.all_to_all(piece_list, "dp", split_axis=1, concat_axis=1, tiled=True)
    return returned.reshape(slots_total, model_width)


def on_device(
    acts,
    grad_out,
    row_adapter,
    ranks,
    owner_map,
    down_slots,
    up_slots,
    down_first,
    down_second,
    up_first,
    up_second,
):
    tok_rows, model_width = acts.shape
    out_width = grad_out.shape[1]
    slot_depth = tok_rows // 32
    dev_count = lax.axis_size("dp")
    own_slots = down_slots.shape[0]
    half_width = down_slots.shape[1]
    device_index = lax.axis_index("dp")
    row_ids = row_adapter[:, 0]
    adapter_labels = jnp.arange(ranks.shape[0], dtype=jnp.int32)
    unit_labels = jnp.arange(owner_map.shape[0], dtype=jnp.int32)
    one_hot = (row_ids[:, None] == adapter_labels[None, :]).astype(jnp.int32)
    earlier = jnp.sum((jnp.cumsum(one_hot, axis=0) - one_hot) * one_hot, axis=1)
    slots_total = own_slots * dev_count * slot_depth
    positions = []
    for half_idx in range(2):
        unit_id = 2 * row_ids + half_idx
        slot_id = jnp.sum(
            jnp.where(unit_id[:, None] == unit_labels[None, :], owner_map[None, :], 0), axis=1
        )
        positions.append(
            (slot_id % own_slots * dev_count + slot_id // own_slots) * slot_depth + earlier
        )
    row_index = jnp.arange(tok_rows, dtype=jnp.int32)
    flat_index = jnp.concatenate(positions)
    source_row = (
        jnp.zeros((slots_total,), jnp.int32)
        .at[flat_index]
        .set(jnp.concatenate([row_index, row_index]))
    )
    filled = jnp.zeros((slots_total,), jnp.bool_).at[flat_index].set(True)
    acts_send = jnp.where(
        filled[:, None], jnp.take(acts, source_row, axis=0), jnp.zeros((), acts.dtype)
    )
    grads_send = jnp.where(
        filled[:, None], jnp.take(grad_out, source_row, axis=0), jnp.zeros((), grad_out.dtype)
    )
    acts_send = acts_send.reshape(own_slots, dev_count, slot_depth, model_width)
    grads_send = grads_send.reshape(own_slots, dev_count, slot_depth, out_width)
    my_slots = device_index * own_slots + jnp.arange(own_slots, dtype=jnp.int32)
    unit_here = jnp.sum(
        jnp.where(owner_map[None, :] == my_slots[:, None], unit_labels[None, :], 0), axis=1
    )
    adapter_here = unit_here // 2
    half_here = unit_here % 2
    local_rank_value = jnp.sum(
        jnp.where(adapter_labels[None, :] == adapter_here[:, None], ranks[None, :], 0), axis=1
    )
    rank_keep = (
        half_here[:, None] * half_width + jnp.arange(half_width, dtype=jnp.int32)[None, :]
        < local_rank_value[:, None]
    )
    adapter_scale_factor = adapter_alpha_value / local_rank_value.astype(jnp.float32)
    down_weight_bf16 = jnp.where(rank_keep[:, :, None], down_slots, 0.0).astype(jnp.bfloat16)
    up_weight_bf16 = jnp.where(rank_keep[:, :, None], up_slots, 0.0).astype(jnp.bfloat16)
    acts_recv, grads_recv = (
        lax.all_to_all(acts_send, "dp", split_axis=1, concat_axis=1, tiled=True),
        lax.all_to_all(grads_send, "dp", split_axis=1, concat_axis=1, tiled=True),
    )
    incoming_rows = acts_recv.reshape(own_slots, dev_count * slot_depth, model_width)
    incoming_gradients = grads_recv.reshape(own_slots, dev_count * slot_depth, out_width)
    hidden_state = jnp.einsum(
        "bus,bns->bun", incoming_rows, down_weight_bf16, preferred_element_type=jnp.float32
    ).astype(jnp.bfloat16)
    lowrank_gradient = jnp.einsum(
        "xpv,xev->xpe", incoming_gradients, up_weight_bf16, preferred_element_type=jnp.float32
    ).astype(jnp.bfloat16)
    down_gradient = adapter_scale_factor[:, None, None] * jnp.einsum(
        "kxa,kxo->kao", lowrank_gradient, incoming_rows, preferred_element_type=jnp.float32
    )
    up_gradient = adapter_scale_factor[:, None, None] * jnp.einsum(
        "doa,dop->dap", hidden_state, incoming_gradients, preferred_element_type=jnp.float32
    )
    squares_sum = lax.psum(
        jnp.sum(down_gradient * down_gradient) + jnp.sum(up_gradient * up_gradient), "dp"
    )
    clip_factor = jnp.minimum(1.0, clip_limit / (jnp.sqrt(squares_sum) + norm_eps))
    down_new = adamw_update(down_slots, down_first, down_second, down_gradient, clip_factor)
    up_new = adamw_update(up_slots, up_first, up_second, up_gradient, clip_factor)
    down_new, up_new = (down_new, up_new)
    matrix_product = jnp.einsum(
        "cpe,cez->cpz", lowrank_gradient, down_weight_bf16, preferred_element_type=jnp.float32
    )
    piece_list = (adapter_scale_factor[:, None, None] * matrix_product).astype(jnp.bfloat16)
    returned = send_back(
        piece_list.reshape(own_slots, dev_count, slot_depth, model_width), slots_total, model_width
    )
    first_share = jnp.take(returned, positions[0], axis=0).astype(jnp.float32)
    second_share = jnp.take(returned, positions[1], axis=0).astype(jnp.float32)
    input_grad = (first_share + second_share).astype(jnp.bfloat16)
    return (input_grad, down_new[0], up_new[0], down_new[1], down_new[2], up_new[1], up_new[2])


def solution(mesh):
    return jax.shard_map(
        on_device,
        mesh=mesh,
        in_specs=(
            P(("groups", "dp"), None),
            P(("groups", "dp"), None),
            P(("groups", "dp"), None),
            P(),
            P(),
            P(("groups", "dp"), None, None),
            P(("groups", "dp"), None, None),
            P(("groups", "dp"), None, None),
            P(("groups", "dp"), None, None),
            P(("groups", "dp"), None, None),
            P(("groups", "dp"), None, None),
        ),
        out_specs=(
            P(("groups", "dp"), None),
            P(("groups", "dp"), None, None),
            P(("groups", "dp"), None, None),
            P(("groups", "dp"), None, None),
            P(("groups", "dp"), None, None),
            P(("groups", "dp"), None, None),
            P(("groups", "dp"), None, None),
        ),
        check_vma=False,
    )
```

profile of v0, /device:TPU:15, one launch (start us, length us, event | category | flops | bytes accessed | tf_op | source)
XLA Modules:
  0.0 515.2 jit_solution(12532746587048643033)
XLA Ops:
  0.6 0.0 copy-start
  0.6 0.8 add_bitcast_fusion
  1.5 0.7 fusion.8
  2.2 0.2 reduce_window_sum.11
  2.4 0.8 select_reduce_fusion.1
  3.2 0.8 select_reduce_fusion.2
  4.1 1.4 scatter_custom_fusion.1
  5.5 3.7 gather_fusion
  9.3 1.2 gather.16
  10.5 0.1 broadcast_in_dim.168
  10.6 1.5 scatter_custom_fusion
  12.1 0.1 broadcast_in_dim.165
  12.3 2.7 fusion.5
  15.0 6.6 %all-to-all-start = ((bf16[8,16,4,1024]{3,2,0,1:T(4,128)(2,1)}), bf16[8,16,4,1024]{3,2,0,1:T(4,128)(2,1)S(1)}, u32[]{:S(2)}, u32[]{:S(2)}) async-start(bf16[8,16,4,1024]{3,2,0,1:T(4,128)(2,1)} %fusion.5), calls=%async_computation | async-start | bytes 2097152 | tf_op jit(solution)/shard_map/all_to_all | solution.py:102
  21.5 0.0 copy-done
  21.5 7.9 %gather_fusion.1 = bf16[512,8192]{1,0:T(8,128)(2,1)} fusion(bf16[128,8192]{1,0:T(8,128)(2,1)S(1)} %copy-done, s32[1024]{0:T(1024)S(1)} %pad_clamp_fusion.2), kind=kCustom, calls=%fused_computation.3 | custom fusion | bytes 16779264 | tf_op jit(solution)/shard_map/jit(_take)/gather | solution.py:77
  29.4 13.0 %gather.18 = bf16[8,16,4,8192]{3,2,1,0:T(4,128)(2,1)} reshape(bf16[512,8192]{1,0:T(8,128)(2,1)} %gather_fusion.1) | data formatting | bytes 16777216 | tf_op jit(solution)/shard_map/jit(_take)/gather | solution.py:77
  42.4 8.5 %fusion.1 = bf16[8,16,4,8192]{3,2,0,1:T(4,128)(2,1)} fusion(bf16[8,16,4,8192]{3,2,1,0:T(4,128)(2,1)} %gather.18, pred[8,16,4]{2,0,1:T(8,128)(4,1)S(1)} %copy.29, pred[8,16,4]{2,0,1:T(8,128)(4,1)S(1)} %copy.28), kind=kLoop, calls=%fused_computation.11 | loop fusion | flops 8388608 | bytes 16778240 | tf_op jit(solution)/shard_map/jit(_where)/select_n | solution.py:76
  50.9 0.0 all-to-all-done
  50.9 6.2 %all-to-all-start.2 = ((bf16[8,16,4,8192]{3,2,0,1:T(4,128)(2,1)}), bf16[8,16,4,8192]{3,2,0,1:T(4,128)(2,1)}, u32[]{:S(2)}, u32[]{:S(2)}) async-start(bf16[8,16,4,8192]{3,2,0,1:T(4,128)(2,1)} %fusion.1), calls=%async_computation.2 | async-start | bytes 16777216 | tf_op jit(solution)/shard_map/all_to_all | solution.py:101
  57.1 0.0 copy-done.3
  57.1 0.2 select_reduce_fusion.4
  57.3 0.0 copy-done.4
  57.3 0.2 select_reduce_fusion.3
  57.5 0.1 add_compare_fusion
  57.6 0.4 copy.31
  58.0 0.3 reshape.196
  58.3 1.7 convolution_convert_fusion
  60.0 9.2 %multiply_convert_fusion = bf16[8,64,8192]{2,1,0:T(8,128)(2,1)} fusion(bf16[8,64,32]{1,2,0:T(8,128)(2,1)S(1)} %convolution_convert_fusion, f32[8]{0:T(128)S(1)} %convert_divide_fusion, f32[8,32,8192]{2,1,0:T(8,128)} %param.18, pred[8,32]{1,0:T(8,128)(4,1)S(1)} %add_compare_fusion), kind=kOutput, calls=%fused_computation.6 | convolution fusion | flops 278921216 | bytes 16810272 | tf_op jit(solution)/shard_map/cpe,cez->cpz/dot_general | solution.py:125
  69.2 13.0 %reshape.197 = bf16[8,16,4,8192]{3,2,1,0:T(4,128)(2,1)} reshape(bf16[8,64,8192]{2,1,0:T(8,128)(2,1)} %multiply_convert_fusion) | data formatting | bytes 16777216 | tf_op jit(solution)/shard_map/reshape | solution.py:130
  82.2 8.1 %copy.32 = bf16[8,16,4,8192]{3,2,0,1:T(4,128)(2,1)} copy(bf16[8,16,4,8192]{3,2,1,0:T(4,128)(2,1)} %reshape.197) | data formatting | bytes 16777216 | tf_op jit(solution)/shard_map/reshape | solution.py:130
  90.4 149.1 %all-to-all-done.2 = bf16[8,16,4,8192]{3,2,0,1:T(4,128)(2,1)} async-done(((bf16[8,16,4,8192]{3,2,0,1:T(4,128)(2,1)}), bf16[8,16,4,8192]{3,2,0,1:T(4,128)(2,1)}, u32[]{:S(2)}, u32[]{:S(2)}) %all-to-all-start.2) | async-done | bytes 8388640 | tf_op jit(solution)/shard_map/all_to_all | solution.py:101
  239.4 4.9 all-to-all-start.1
  244.4 8.1 %copy.37 = bf16[8,16,4,8192]{3,2,1,0:T(4,128)(2,1)} copy(bf16[8,16,4,8192]{3,2,0,1:T(4,128)(2,1)} %all-to-all-done.2) | data formatting | bytes 16777216 | tf_op jit(solution)/shard_map/all_to_all | solution.py:101
  252.5 12.4 %reshape.199 = bf16[8,64,8192]{2,1,0:T(8,128)(2,1)} reshape(bf16[8,16,4,8192]{3,2,1,0:T(4,128)(2,1)} %copy.37) | data formatting | bytes 16777216 | tf_op jit(solution)/shard_map/reshape | solution.py:104
  265.0 9.7 %multiply_reduce_fusion = (f32[]{:T(128)}, f32[8,32,8192]{2,1,0:T(8,128)}) fusion(bf16[8,64,32]{1,2,0:T(8,128)(2,1)S(1)} %convolution_convert_fusion, bf16[8,64,8192]{2,1,0:T(8,128)(2,1)} %reshape.199, f32[8]{0:T(128)S(1)} %convert_divide_fusion), kind=kOutput, calls=%fused_computation.14 | convolution fusion | flops 274726912 | bytes 16810020 | tf_op jit(solution)/shard_map/kxa,kxo->kao/dot_general | solution.py:112
  274.7 8.0 %multiply_reduce_fusion.1 = (f32[]{:T(128)}, f32[8,32,1024]{2,1,0:T(8,128)S(1)}) fusion(bf16[8,64,1024]{2,1,0:T(8,128)(2,1)S(1)} %reshape.196, bf16[8,64,8192]{2,1,0:T(8,128)(2,1)} %reshape.199, f32[8,32,8192]{2,1,0:T(8,128)} %param.18, pred[8,32]{1,0:T(8,128)(4,1)S(1)} %add_compare_fusion, f32[8]{0:T(128)S(1)} %convert_divide_fusion), kind=kOutput, calls=%fused_computation.27 | convolution fusion | flops 304889856 | bytes 18874660 | tf_op jit(solution)/shard_map/doa,dop->dap/dot_general | solution.py:115
  284.0 159.8 %psum.7 = f32[]{:T(128)} all-reduce(f32[]{:T(128)S(6)} %add.254), channel_id=1, replica_groups=mesh['groups'=2,'dp'=16] {'dp'}, use_global_device_ids=true, to_apply=%region_10.12 | all-reduce | flops 1 | bytes 8 | tf_op jit(solution)/shard_map/psum | solution.py:118
  444.5 0.0 copy-done.2
  444.5 3.9 multiply_subtract_fusion.1
  448.4 22.3 %multiply_subtract_fusion = (f32[8,32,8192]{2,1,0:T(8,128)}, f32[8,32,8192]{2,1,0:T(8,128)}, f32[8,32,8192]{2,1,0:T(8,128)}) fusion(f32[8,32,8192]{2,1,0:T(8,128)} %param.18, f32[8,32,8192]{2,1,0:T(8,128)} %get-tuple-element.27, f32[]{:T(128)S(6)} %min.3, f32[8,32,8192]{2,1,0:T(8,128)} %param.20, f32[8,32,8192]{2,1,0:T(8,128)} %param.21), kind=kLoop, calls=%fused_computation.12 | loop fusion | flops 33554432 | bytes 58720260 | tf_op jit(solution)/shard_map/sub | solution.py:22
  470.6 0.0 all-to-all-done.1
  470.6 8.2 %copy.33 = bf16[8,16,4,8192]{3,2,1,0:T(4,128)(2,1)} copy(bf16[8,16,4,8192]{3,2,0,1:T(4,128)(2,1)} %all-to-all-done.1) | data formatting | bytes 16777216 | tf_op jit(solution)/shard_map/all_to_all | solution.py:29
  478.8 12.5 %reshape.198 = bf16[512,8192]{1,0:T(8,128)(2,1)} reshape(bf16[8,16,4,8192]{3,2,1,0:T(4,128)(2,1)} %copy.33) | data formatting | bytes 16777216 | tf_op jit(solution)/shard_map/reshape | solution.py:30
  491.3 9.7 %gather_fusion.3 = bf16[128,8192]{1,0:T(8,128)(2,1)} fusion(bf16[512,8192]{1,0:T(8,128)(2,1)} %reshape.198, s32[1024]{0:T(1024)S(1)} %pad_clamp_fusion), kind=kCustom, calls=%fused_computation.1.clone | custom fusion | bytes 4194816 | tf_op jit(solution)/shard_map/jit(_take)/gather | solution.py:133
  501.0 9.6 %gather_fusion.2 = bf16[128,8192]{1,0:T(8,128)(2,1)} fusion(bf16[512,8192]{1,0:T(8,128)(2,1)} %reshape.198, s32[1024]{0:T(1024)S(1)} %pad_clamp_fusion.1), kind=kCustom, calls=%fused_computation.clone | custom fusion | bytes 4194816 | tf_op jit(solution)/shard_map/jit(_take)/gather | solution.py:132
  510.6 4.5 add_convert_fusion
  515.2 0.0 copy-done.1
  (20 shorter events, 0.1 us)
Async XLA Ops:
  0.6 20.9 %copy-start = (bf16[128,8192]{1,0:T(8,128)(2,1)S(1)}, bf16[128,8192]{1,0:T(8,128)(2,1)}, u32[]{:S(2)}) copy-start(bf16[128,8192]{1,0:T(8,128)(2,1)} %param.13) | copy-start | bytes 6291460
  15.0 36.0 %all-to-all-start = ((bf16[8,16,4,1024]{3,2,0,1:T(4,128)(2,1)}), bf16[8,16,4,1024]{3,2,0,1:T(4,128)(2,1)S(1)}, u32[]{:S(2)}, u32[]{:S(2)}) async-start(bf16[8,16,4,1024]{3,2,0,1:T(4,128)(2,1)} %fusion.5), calls=%async_computation | async-start | bytes 2097152 | tf_op jit(solution)/shard_map/all_to_all | solution.py:102
  50.9 6.2 %copy-start.3 = (s32[128]{0:T(128)S(1)}, s32[128]{0:T(128)}, u32[]{:S(2)}) copy-start(s32[128]{0:T(128)} %param.17) | copy-start | bytes 1540
  50.9 6.4 %copy-start.4 = (s32[64]{0:T(128)S(1)}, s32[64]{0:T(128)}, u32[]{:S(2)}) copy-start(s32[64]{0:T(128)} %param.16) | copy-start | bytes 772
  50.9 188.5 %all-to-all-start.2 = ((bf16[8,16,4,8192]{3,2,0,1:T(4,128)(2,1)}), bf16[8,16,4,8192]{3,2,0,1:T(4,128)(2,1)}, u32[]{:S(2)}, u32[]{:S(2)}) async-start(bf16[8,16,4,8192]{3,2,0,1:T(4,128)(2,1)} %fusion.1), calls=%async_computation.2 | async-start | bytes 16777216 | tf_op jit(solution)/shard_map/all_to_all | solution.py:101
  239.4 231.2 %all-to-all-start.1 = ((bf16[8,16,4,8192]{3,2,0,1:T(4,128)(2,1)}), bf16[8,16,4,8192]{3,2,0,1:T(4,128)(2,1)}, u32[]{:S(2)}, u32[]{:S(2)}) async-start(bf16[8,16,4,8192]{3,2,0,1:T(4,128)(2,1)} %copy.32), calls=%async_computation.1 | async-start | bytes 16777216 | tf_op jit(solution)/shard_map/all_to_all | solution.py:29
  274.7 169.8 %copy-start.2 = (f32[8,32,1024]{2,1,0:T(8,128)S(1)}, f32[8,32,1024]{2,1,0:T(8,128)}, u32[]{:S(2)}) copy-start(f32[8,32,1024]{2,1,0:T(8,128)} %param.19) | copy-start | bytes 3145732
  491.3 23.8 %copy-start.1 = (bf16[128,8192]{1,0:T(8,128)(2,1)S(1)}, bf16[128,8192]{1,0:T(8,128)(2,1)}, u32[]{:S(2)}) copy-start(bf16[128,8192]{1,0:T(8,128)(2,1)} %param.13) | copy-start | bytes 6291460
where the time goes:
time: 519 us; the launch traced here: 515 us
  blocking collectives  160 us (31%)
  waiting for transfers between devices  149 us (29%)
  local copies, waits for them, and re-layouts  111 us (21%)
  other arithmetic  45.7 us (9%)
  matrix products  28.6 us (6%)
  starting transfers between devices  17.6 us (3%)
    psum x1, blocking collectives, on_device(): lax.psum(jnp.sum(down_gradient * down_gradient) + jnp.sum(up_gradient * u...  160 us
    all_to_all x1, waiting for transfers between devices, on_device(): lax.all_to_all(acts_send, 'dp', split_axis=1, concat_axis=1, tiled=True)  149 us
    sub x2, other arithmetic, adamw_update(): params - learn_rate * (moment / bias_one / (jnp.sqrt(second / bias_two) +...  26.1 us
    reshape x2, local copies, waits for them, and re-layouts, on_device(): piece_list.reshape(own_slots, dev_count, slot_depth, model_width)  21.2 us
    gather x2, local copies, waits for them, and re-layouts, on_device(): jnp.take(acts, source_row, axis=0)  20.9 us
    reshape x1, local copies, waits for them, and re-layouts, send_back(): return returned.reshape(slots_total, model_width)  12.5 us
    reshape x1, local copies, waits for them, and re-layouts, on_device(): acts_recv.reshape(own_slots, dev_count * slot_depth, model_width)  12.4 us
  transfers between devices with their start and end apart: 3, of which 1 were waited for; matrix products, arithmetic and copies ran while one was open for 25% of the time, Pallas kernels for 0%

commit v1 on v0

v1 whole, which is shorter than its diff:
```python
import jax
import jax.numpy as jnp
from jax import lax
from jax.sharding import PartitionSpec as P

adapter_alpha_value = 16.0
clip_limit = 1.0
norm_eps = 1e-06
beta_one = 0.9
beta_two = 0.999
bias_one = 0.9999734386011124
bias_two = 0.0952078528862904
learn_rate = 0.0002
decay_rate = 0.01
adam_eps = 1e-08


def adamw_update(params, moment, second, gradient, clip_factor):
    clipped = clip_factor * gradient
    moment = beta_one * moment + (1.0 - beta_one) * clipped
    second = beta_two * second + (1.0 - beta_two) * clipped * clipped
    params = params - learn_rate * (
        moment / bias_one / (jnp.sqrt(second / bias_two) + adam_eps) + decay_rate * params
    )
    return (params, moment, second)


def on_device(
    acts,
    grad_out,
    row_adapter,
    ranks,
    owner_map,
    down_slots,
    up_slots,
    down_first,
    down_second,
    up_first,
    up_second,
):
    rows, width = acts.shape
    out_width = grad_out.shape[1]
    devices = lax.axis_size("dp")
    own, depth = down_slots.shape[0], down_slots.shape[1]
    slots = owner_map.shape[0]
    halves = 2
    team = devices // halves
    cut = width // team
    out_cut = out_width // team
    half_slots = own * team
    cols = half_slots * depth
    all_rows = devices * rows
    groups = [[h * team + j for j in range(team)] for h in range(halves)]
    me = lax.axis_index("dp")
    f32, bf16 = jnp.float32, jnp.bfloat16

    unit_labels = jnp.arange(slots, dtype=jnp.int32)
    adapter_labels = jnp.arange(ranks.shape[0], dtype=jnp.int32)

    def describe(first_slot, count):
        here = first_slot + jnp.arange(count, dtype=jnp.int32)
        unit = jnp.sum(jnp.where(owner_map[None, :] == here[:, None], unit_labels[None, :], 0), axis=1)
        rank = jnp.sum(
            jnp.where(adapter_labels[None, :] == (unit // 2)[:, None], ranks[None, :], 0), axis=1
        )
        return unit, rank

    own_unit, own_rank = describe(me * own, own)
    keep = (own_unit % 2)[:, None] * depth + jnp.arange(depth, dtype=jnp.int32)[None, :] < own_rank[:, None]
    keep = keep.reshape(own * depth, 1)
    down_flat = down_slots.reshape(own * depth, width)
    up16 = jnp.where(keep, up_slots.reshape(own * depth, out_width), 0.0).astype(bf16)
    seat = me % team
    team_perms = [[(i, i ^ b) for i in range(devices)] for b in range(team)]

    def sliced(array, pieces):
        return array.reshape(array.shape[0], pieces, -1).transpose(1, 0, 2)

    def to_team(array):
        return lax.all_to_all(array, "dp", split_axis=0, concat_axis=0, axis_index_groups=groups, tiled=True)

    def to_all(array):
        return lax.all_to_all(array, "dp", split_axis=0, concat_axis=0, tiled=True)

    def swap(blocks):
        return [blocks[0]] + [lax.ppermute(blocks[b], "dp", team_perms[b]) for b in range(1, team)]

    def double(array, span, wide):
        step = 1
        while step < span:
            sent = array if wide or step == 1 else array.astype(bf16)
            got = lax.ppermute(sent, "dp", [(i, i ^ step) for i in range(devices)])
            array = sent.astype(f32) + got.astype(f32)
            step *= 2
        return array

    id_rows = -(-rows // out_cut)
    id_block = jnp.pad(row_adapter[:, 0], (0, id_rows * out_cut - rows)).astype(bf16)
    id_block = jnp.pad(id_block.reshape(id_rows, out_cut), ((0, -id_rows % 16), (0, 0)))
    g_send = jnp.concatenate(
        [sliced(grad_out, team), jnp.broadcast_to(id_block, (team,) + id_block.shape)], axis=1
    )
    g_got = to_all(jnp.tile(g_send, (halves, 1, 1)))
    g_cut = g_got[:, :rows].reshape(all_rows, out_cut)
    ids = g_got[:, rows : rows + id_rows].reshape(devices, -1)[:, :rows].reshape(all_rows)
    ids = ids.astype(f32).astype(jnp.int32)
    b_cut = to_team(sliced(up16, team)).reshape(cols, out_cut)
    acts_now, _, _ = lax.optimization_barrier((acts, g_got, b_cut))
    x_cut = to_all(jnp.tile(sliced(acts_now, team), (halves, 1, 1))).reshape(all_rows, cut)
    a_blocks = []
    for b in range(team):
        part = lax.dynamic_slice_in_dim(down_flat, (seat ^ b) * cut, cut, axis=1)
        a_blocks.append(jnp.where(keep, part, 0.0).astype(bf16))
    a_cut = jnp.concatenate(swap(a_blocks), axis=0)

    half_unit, half_rank = describe(me // team * half_slots, half_slots)
    seats = jnp.arange(team, dtype=jnp.int32) ^ seat

    def columns(reorder):
        unit, rank = half_unit, half_rank
        if reorder:
            unit = jnp.take(unit.reshape(team, own), seats, axis=0).reshape(-1)
            rank = jnp.take(rank.reshape(team, own), seats, axis=0).reshape(-1)
        unit = jnp.repeat(unit, depth)
        scale = adapter_alpha_value / jnp.repeat(rank, depth).astype(f32)
        lane = unit % 2 * depth + jnp.arange(cols, dtype=jnp.int32) % depth
        fold = (lane[None, :] == jnp.arange(2 * depth, dtype=jnp.int32)[:, None]).astype(bf16)
        match = ids[:, None] == (unit // 2)[None, :]
        return scale, fold, match

    b_side, a_side = columns(False), columns(True)

    def narrow(left, right, side):
        _, fold, match = side
        product = lax.dot_general(left, right, (((1,), (1,)), ((), ())), preferred_element_type=f32)
        masked = jnp.where(match, product, 0.0).astype(bf16)
        part = lax.dot_general(fold, masked, (((1,), (1,)), ((), ())), preferred_element_type=f32)
        return double(part, team, False).astype(bf16)

    def widen(lanes, side):
        _, fold, match = side
        spread = lax.dot_general(lanes, fold, (((0,), (0,)), ((), ())), preferred_element_type=f32)
        return jnp.where(match, spread, 0.0).astype(bf16)

    low = widen(narrow(g_cut, b_cut, b_side), a_side)
    piece = jnp.dot(low, a_cut, preferred_element_type=f32).astype(bf16)
    back = to_all(piece.reshape(devices, rows, cut)).astype(f32)

    x_late, _ = lax.optimization_barrier((x_cut, piece))
    hidden = widen(narrow(x_late, a_cut, a_side), b_side)
    down_parts, squares = [], jnp.zeros((), f32)
    for b in range(team):
        span = slice(b * own * depth, (b + 1) * own * depth)
        part = a_side[0][span, None] * lax.dot_general(
            low[:, span], x_late, (((0,), (0,)), ((), ())), preferred_element_type=f32
        )
        squares = squares + jnp.sum(part * part)
        down_parts.append(part.astype(bf16))
    down_parts = swap(down_parts)
    up_grad = b_side[0][:, None] * lax.dot_general(
        hidden, g_cut, (((0,), (0,)), ((), ())), preferred_element_type=f32
    )
    squares = double(squares + jnp.sum(up_grad * up_grad), devices, True)
    clip_factor = jnp.minimum(1.0, clip_limit / (jnp.sqrt(squares) + norm_eps))
    up_parts = swap(
        [
            lax.dynamic_slice_in_dim(up_grad.astype(bf16), (seat ^ b) * own * depth, own * depth, axis=0)
            for b in range(team)
        ]
    )

    def home(parts, part_width, whole_width):
        grad = jnp.zeros((own * depth, whole_width), bf16)
        for b in range(team):
            grad = lax.dynamic_update_slice_in_dim(grad, parts[b], (seat ^ b) * part_width, axis=1)
        return grad.reshape(own, depth, whole_width).astype(f32)

    down_new = adamw_update(down_slots, down_first, down_second, home(down_parts, cut, width), clip_factor)
    up_new = adamw_update(up_slots, up_first, up_second, home(up_parts, out_cut, out_width), clip_factor)

    row_rank = jnp.sum(jnp.where(row_adapter == adapter_labels[None, :], ranks[None, :], 0), axis=1)
    row_scale = adapter_alpha_value / row_rank.astype(f32)
    joined = (back[:team] + back[team:]).transpose(1, 0, 2).reshape(rows, width)
    input_grad = (row_scale[:, None] * joined).astype(bf16)
    return (input_grad, down_new[0], up_new[0], down_new[1], down_new[2], up_new[1], up_new[2])


def solution(mesh):
    two = P(("groups", "dp"), None)
    three = P(("groups", "dp"), None, None)
    return jax.shard_map(
        on_device,
        mesh=mesh,
        in_specs=(two, two, two, P(), P(), three, three, three, three, three, three),
        out_specs=(two, three, three, three, three, three, three),
        check_vma=False,
    )
```

time: 519 us -> 393 us (0.76)
  blocking collectives: 160 us -> 21.7 us
  local copies, waits for them, and re-layouts: 111 us -> 31 us
  matrix products: 28.6 us -> 82.8 us
  starting transfers between devices: 17.6 us -> 60.4 us
  waiting for transfers between devices: 149 us -> 132 us
  between operations: 2.88 us -> 9.87 us
    psum x1 -> x0, blocking collectives: 160 us -> none  [on_device(): lax.psum(jnp.sum(down_gradient * down_gradient) + jnp.sum(up_gradient * u...]
    all_to_all x3, waiting for transfers between devices: 149 us -> 6.69 us  [the longest x1 6.68 us: to_team(): lax.all_to_all(array, 'dp', split_axis=0, concat_axis=0, axis_index_group...]
    ppermute x0 -> x31, waiting for transfers between devices: none -> 126 us  [the longest x21 120 us: swap(): lax.ppermute(blocks[b], 'dp', team_perms[b])]
    dot_general x4 -> x13, matrix products: 28.6 us -> 82.8 us  [the longest x8 41.3 us: on_device(): lax.dot_general(low[:, span], x_late, (((0,), (0,)), ((), ())), preferred...]
    reshape x5 -> x6, local copies, waits for them, and re-layouts: 46.4 us -> 0.69 us  [the longest x1 0.31 us: on_device(): joined = (back[:team] + back[team:]).transpose(1, 0, 2).reshape(rows, width)]
    gather x6 -> x2, local copies, waits for them, and re-layouts: 45.1 us -> 1.13 us  [the longest x1 0.57 us: columns(): rank = jnp.take(rank.reshape(team, own), seats, axis=0).reshape(-1)]
    ppermute x0 -> x31, starting transfers between devices: none -> 42.8 us  [the longest x21 30.1 us: swap(): lax.ppermute(blocks[b], 'dp', team_perms[b])]
    all_to_all x0 -> x1, blocking collectives: none -> 21.7 us  [to_all(): return lax.all_to_all(array, 'dp', split_axis=0, concat_axis=0, tiled=True)]
  transfers between devices with their start and end apart: 3 -> 34, of which waited for: 1 -> 17; matrix products, arithmetic and copies ran while one was open for 25% -> 36% of each run, Pallas kernels for 0% -> 0%
where the time goes in v1:
time: 393 us; the launch traced here: 387 us
  waiting for transfers between devices  132 us (34%)
  matrix products  82.8 us (21%)
  starting transfers between devices  60.4 us (15%)
  other arithmetic  48.8 us (12%)
  local copies, waits for them, and re-layouts  31 us (8%)
  blocking collectives  21.7 us (6%)
  between operations  9.87 us (3%)
    ppermute x21, waiting for transfers between devices, swap(): lax.ppermute(blocks[b], 'dp', team_perms[b])  120 us
    dot_general x8, matrix products, on_device(): lax.dot_general(low[:, span], x_late, (((0,), (0,)), ((), ())), preferred...  41.3 us
    ppermute x21, starting transfers between devices, swap(): lax.ppermute(blocks[b], 'dp', team_perms[b])  30.1 us
    sub x2, other arithmetic, adamw_update(): params - learn_rate * (moment / bias_one / (jnp.sqrt(second / bias_two) +...  25.8 us
    all_to_all x1, blocking collectives, to_all(): return lax.all_to_all(array, 'dp', split_axis=0, concat_axis=0, tiled=True)  21.7 us
    dot_general x2, matrix products, narrow(): lax.dot_general(fold, masked, (((1,), (1,)), ((), ())), preferred_element...  20.1 us
    all_to_all x2, starting transfers between devices, to_all(): return lax.all_to_all(array, 'dp', split_axis=0, concat_axis=0, tiled=True)  13.2 us
    ppermute x10, starting transfers between devices, double(): got = lax.ppermute(sent, 'dp', [(i, i ^ step) for i in range(devices)])  12.7 us
  transfers between devices with their start and end apart: 34, of which 17 were waited for; matrix products, arithmetic and copies ran while one was open for 36% of the time, Pallas kernels for 0%

profile of v1, /device:TPU:15, one launch (start us, length us, event | category | flops | bytes accessed | tf_op | source)
XLA Modules:
  0.0 387.0 jit_solution(16071247590270534932)
XLA Ops:
  5.4 4.5 %all-to-all-start.1 = ((bf16[8,256,128]{2,1,0:T(8,128)(2,1)}), bf16[8,256,128]{2,1,0:T(8,128)(2,1)S(1)}, u32[]{:S(2)}, u32[]{:S(2)}) async-start(bf16[8,256,128]{2,1,0:T(8,128)(2,1)} %copy.33), calls=%async_computation.1 | async-start | bytes 1048576 | tf_op jit(solution)/shard_map/all_to_all | solution.py:80
  10.1 6.7 %all-to-all-done.1 = bf16[8,256,128]{2,1,0:T(8,128)(2,1)S(1)} async-done(((bf16[8,256,128]{2,1,0:T(8,128)(2,1)}), bf16[8,256,128]{2,1,0:T(8,128)(2,1)S(1)}, u32[]{:S(2)}, u32[]{:S(2)}) %all-to-all-start.1) | async-done | bytes 524320 | tf_op jit(solution)/shard_map/all_to_all | solution.py:80
  16.9 21.7 %all_to_all.20 = bf16[16,144,128]{2,1,0:T(8,128)(2,1)S(1)} all-to-all(bf16[16,144,128]{2,1,0:T(8,128)(2,1)S(1)} %bitcast.71), channel_id=1, replica_groups=mesh['groups'=2,'dp'=16] {'dp'}, dimensions={0} | all-to-all | bytes 1179648 | tf_op jit(solution)/shard_map/all_to_all | solution.py:83
  41.1 2.5 tile.20
  43.6 7.2 %all-to-all-start.3 = ((bf16[16,128,1024]{2,1,0:T(8,128)(2,1)}), bf16[16,128,1024]{2,1,0:T(8,128)(2,1)}, u32[]{:S(2)}, u32[]{:S(2)}) async-start(bf16[16,128,1024]{2,1,0:T(8,128)(2,1)} %bitcast.65), calls=%async_computation.3 | async-start | bytes 8388608 | tf_op jit(solution)/shard_map/all_to_all | solution.py:83
  50.9 6.1 %select_convert_fusion = (bf16[256,1024]{1,0:T(8,128)(2,1)}, bf16[256,1024]{1,0:T(8,128)(2,1)}, bf16[256,1024]{1,0:T(8,128)(2,1)}, bf16[256,1024]{1,0:T(8,128)(2...) fusion(f32[256,8192]{1,0:T(8,128)} %bitcast.64, ...), kind=kLoop, calls=%fused_computation.58 | loop fusion | flops 2097151 | bytes 8388896 | tf_op jit(solution)/shard_map/convert_element_type | solution.py:113
  61.7 4.8 %fusion.13 = f32[64,2048]{1,0:T(8,128)S(1)} fusion(bf16[2048,128]{1,0:T(8,128)(2,1)S(1)} %bitcast.75, bf16[2048,128]{1,0:T(8,128)(2,1)S(1)} %bitcast.77, s32[2048]{0:T(1024)S(1)} %get-tuple-element.53, s32[2048]{0:T(1024)S(1)} %bitcast.79, s32[2048]{0:T(1024)S(1)} %get-tuple-element.52), kind=kOutput, calls=%fused_computation.25 | convolution fusion | flops 1623326720 | bytes 1597440 | tf_op jit(solution)/shard_map/dot_general | solution.py:137
  68.3 1.9 constant_dynamic-update-slice_fusion.6
  70.3 15.3 %collective-permute-done.4 = bf16[256,1024]{1,0:T(8,128)(2,1)S(1)} collective-permute-done((bf16[256,1024]{1,0:T(8,128)(2,1)}, bf16[256,1024]{1,0:T(8,128)(2,1)S(1)}, u32[]{:S(2)}, u32[]{:S(2)}) %collective-permute-start.4) | collective-permute-done | bytes 524320 | tf_op jit(solution)/shard_map/ppermute | solution.py:86
  86.4 17.1 %collective-permute-done.5 = bf16[256,1024]{1,0:T(8,128)(2,1)S(1)} collective-permute-done((bf16[256,1024]{1,0:T(8,128)(2,1)}, bf16[256,1024]{1,0:T(8,128)(2,1)S(1)}, u32[]{:S(2)}, u32[]{:S(2)}) %collective-permute-start.5) | collective-permute-done | bytes 524320 | tf_op jit(solution)/shard_map/ppermute | solution.py:86
  103.5 10.4 %collective-permute-start.9 = (bf16[256,1024]{1,0:T(8,128)(2,1)}, bf16[256,1024]{1,0:T(8,128)(2,1)S(1)}, u32[]{:S(2)}, u32[]{:S(2)}) collective-permute-start(bf16[256,1024]{1,0:T(8,128)(2,1)} %get-tuple-element.18), channel_id=1, source_target_pairs={{0,7},{1,6},{2,5},{3,4},{4,3},{5,2},{6,1},{7,0},{8,15},{9,14},{10,... | collective-permute-start | bytes 1572872 | tf_op jit(solution)/shard_map/ppermute | solution.py:86
  114.8 17.0 %collective-permute-done.6 = bf16[256,1024]{1,0:T(8,128)(2,1)S(1)} collective-permute-done((bf16[256,1024]{1,0:T(8,128)(2,1)}, bf16[256,1024]{1,0:T(8,128)(2,1)S(1)}, u32[]{:S(2)}, u32[]{:S(2)}) %collective-permute-start.6) | collective-permute-done | bytes 524320 | tf_op jit(solution)/shard_map/ppermute | solution.py:86
  132.7 11.2 %collective-permute-done.7 = bf16[256,1024]{1,0:T(8,128)(2,1)S(1)} collective-permute-done((bf16[256,1024]{1,0:T(8,128)(2,1)}, bf16[256,1024]{1,0:T(8,128)(2,1)S(1)}, u32[]{:S(2)}, u32[]{:S(2)}) %collective-permute-start.7) | collective-permute-done | bytes 524320 | tf_op jit(solution)/shard_map/ppermute | solution.py:86
  144.7 9.5 %collective-permute-done.8 = bf16[256,1024]{1,0:T(8,128)(2,1)S(1)} collective-permute-done((bf16[256,1024]{1,0:T(8,128)(2,1)}, bf16[256,1024]{1,0:T(8,128)(2,1)S(1)}, u32[]{:S(2)}, u32[]{:S(2)}) %collective-permute-start.8) | collective-permute-done | bytes 524320 | tf_op jit(solution)/shard_map/ppermute | solution.py:86
  155.1 10.7 %collective-permute-done.9 = bf16[256,1024]{1,0:T(8,128)(2,1)S(1)} collective-permute-done((bf16[256,1024]{1,0:T(8,128)(2,1)}, bf16[256,1024]{1,0:T(8,128)(2,1)S(1)}, u32[]{:S(2)}, u32[]{:S(2)}) %collective-permute-start.9) | collective-permute-done | bytes 524320 | tf_op jit(solution)/shard_map/ppermute | solution.py:86
  166.6 4.4 %collective-permute-done.2 = bf16[64,2048]{1,0:T(8,128)(2,1)S(1)} collective-permute-done((bf16[64,2048]{1,0:T(8,128)(2,1)S(1)}, bf16[64,2048]{1,0:T(8,128)(2,1)S(1)}, u32[]{:S(2)}, u32[]{:S(2)}) %collective-permute-start.2) | collective-permute-done | bytes 262176 | tf_op jit(solution)/shard_map/ppermute | solution.py:92
  171.1 2.6 fusion
  173.7 3.4 copy-done.8
  177.1 10.4 %convolution_convert_fusion = bf16[2048,1024]{1,0:T(8,128)(2,1)} fusion(bf16[2048,2048]{1,0:T(8,128)(2,1)S(1)} %fusion, bf16[2048,1024]{1,0:T(8,128)(2,1)S(1)} %copy-done.4), kind=kOutput, calls=%fused_computation.23 | convolution fusion | flops 8592031744 | bytes 16777216 | tf_op jit(solution)/shard_map/dot_general | solution.py:146
  187.5 6.0 %all-to-all-start.2 = ((bf16[16,128,1024]{2,1,0:T(8,128)(2,1)}), bf16[16,128,1024]{2,1,0:T(8,128)(2,1)}, u32[]{:S(2)}, u32[]{:S(2)}) async-start(bf16[16,128,1024]{2,1,0:T(8,128)(2,1)} %bitcast.70), calls=%async_computation.2 | async-start | bytes 8388608 | tf_op jit(solution)/shard_map/all_to_all | solution.py:83
  195.0 5.3 %multiply_reduce_fusion.7 = (f32[]{:T(128)}, bf16[256,1024]{1,0:T(8,128)(2,1)}) fusion(bf16[2048,1024]{1,0:T(8,128)(2,1)} %bitcast.14, bf16[2048,2048]{1,0:T(8,128)(2,1)} %copy-done.8, f32[256]{0:T(256)S(1)} %slice.126), kind=kOutput, calls=%fused_computation.56 | convolution fusion | flops 1074790400 | bytes 5768196 | tf_op jit(solution)/shard_map/dot_general | solution.py:154
  200.7 5.2 %multiply_reduce_fusion.6 = (f32[]{:T(128)}, bf16[256,1024]{1,0:T(8,128)(2,1)}) fusion(bf16[2048,1024]{1,0:T(8,128)(2,1)} %bitcast.14, bf16[2048,2048]{1,0:T(8,128)(2,1)} %copy-done.8, f32[256]{0:T(256)S(1)} %slice.130), kind=kOutput, calls=%fused_computation.55 | convolution fusion | flops 1074790400 | bytes 5768196 | tf_op jit(solution)/shard_map/dot_general | solution.py:154
  206.2 5.2 %multiply_reduce_fusion.5 = (f32[]{:T(128)}, bf16[256,1024]{1,0:T(8,128)(2,1)}) fusion(bf16[2048,1024]{1,0:T(8,128)(2,1)} %bitcast.14, bf16[2048,2048]{1,0:T(8,128)(2,1)} %copy-done.8, f32[256]{0:T(256)S(1)} %slice.134), kind=kOutput, calls=%fused_computation.54 | convolution fusion | flops 1074790400 | bytes 5768196 | tf_op jit(solution)/shard_map/dot_general | solution.py:154
  212.9 5.2 %multiply_reduce_fusion.4 = (f32[]{:T(128)}, bf16[256,1024]{1,0:T(8,128)(2,1)}) fusion(bf16[2048,1024]{1,0:T(8,128)(2,1)} %bitcast.14, bf16[2048,2048]{1,0:T(8,128)(2,1)} %copy-done.8, f32[256]{0:T(256)S(1)} %slice.138), kind=kOutput, calls=%fused_computation.53 | convolution fusion | flops 1074790400 | bytes 5768196 | tf_op jit(solution)/shard_map/dot_general | solution.py:154
  218.4 15.3 %fusion.5 = f32[64,2048]{1,0:T(8,128)S(1)} fusion(bf16[2048,1024]{1,0:T(8,128)(2,1)} %bitcast.14, bf16[2048,1024]{1,0:T(8,128)(2,1)} %constant_dynamic-update-slice_fusion, s32[2048]{0:T(1024)S(1)} %get-tuple-element.51, s32[2048]{0:T(1024)S(1)} %bitcast.81, s32[2048]{0:T(1024)S(1)} %get-tuple-element.50), kind=kOutput, calls=%fused_computation.12 | convolution fusion | flops 9139519488 | bytes 8937472 | tf_op jit(solution)/shard_map/dot_general | solution.py:137
  234.1 5.3 %multiply_reduce_fusion.3 = (f32[]{:T(128)}, bf16[256,1024]{1,0:T(8,128)(2,1)}) fusion(bf16[2048,1024]{1,0:T(8,128)(2,1)} %bitcast.14, bf16[2048,2048]{1,0:T(8,128)(2,1)} %copy-done.8, f32[256]{0:T(256)S(1)} %slice.142), kind=kOutput, calls=%fused_computation.52 | convolution fusion | flops 1074790400 | bytes 5768196 | tf_op jit(solution)/shard_map/dot_general | solution.py:154
  239.4 5.3 %multiply_reduce_fusion.2 = (f32[]{:T(128)}, bf16[256,1024]{1,0:T(8,128)(2,1)}) fusion(bf16[2048,1024]{1,0:T(8,128)(2,1)} %bitcast.14, bf16[2048,2048]{1,0:T(8,128)(2,1)} %copy-done.8, f32[256]{0:T(256)S(1)} %slice.146), kind=kOutput, calls=%fused_computation.51 | convolution fusion | flops 1074790400 | bytes 5768196 | tf_op jit(solution)/shard_map/dot_general | solution.py:154
  244.7 5.2 %multiply_reduce_fusion.1 = (f32[]{:T(128)}, bf16[256,1024]{1,0:T(8,128)(2,1)}) fusion(bf16[2048,1024]{1,0:T(8,128)(2,1)} %bitcast.14, bf16[2048,2048]{1,0:T(8,128)(2,1)} %copy-done.8, f32[256]{0:T(256)S(1)} %slice.150), kind=kOutput, calls=%fused_computation.50 | convolution fusion | flops 1074790400 | bytes 5768196 | tf_op jit(solution)/shard_map/dot_general | solution.py:154
  249.9 2.5 broadcast_in_dim.221
  252.4 4.6 %convert_dynamic-update-slice_fusion = (bf16[256,8192]{1,0:T(8,128)(2,1)}, f32[256,1024]{1,0:T(8,128)S(1)}) fusion(bf16[256,8192]{1,0:T(8,128)(2,1)} %broadcast_in_dim.221, s32[]{:T(128)S(6)} %select_n.252, bf16[2048,1024]{1,0:T(8,128)(2,1)} %bitcast.14, bf16[2048,2048]{1,0:T(8,128)(2,1)} %copy-done.8, f32[256]{0:T(256)S(1)} %slice.122), kind=kOutput, calls=%fused_computation.67 | convolution fusion | flops 1074266112 | bytes 6816772 | tf_op jit(solution)/shard_map/dot_general | solution.py:154
  264.5 1.9 constant_dynamic-update-slice_fusion.20
  266.4 2.8 collective-permute-start.23
  271.1 3.3 collective-permute-done.20
  275.2 11.4 %collective-permute-done.21 = bf16[256,1024]{1,0:T(8,128)(2,1)S(1)} collective-permute-done((bf16[256,1024]{1,0:T(8,128)(2,1)}, bf16[256,1024]{1,0:T(8,128)(2,1)S(1)}, u32[]{:S(2)}, u32[]{:S(2)}) %collective-permute-start.21) | collective-permute-done | bytes 524320 | tf_op jit(solution)/shard_map/ppermute | solution.py:86
  287.4 9.6 %collective-permute-done.22 = bf16[256,1024]{1,0:T(8,128)(2,1)S(1)} collective-permute-done((bf16[256,1024]{1,0:T(8,128)(2,1)}, bf16[256,1024]{1,0:T(8,128)(2,1)S(1)}, u32[]{:S(2)}, u32[]{:S(2)}) %collective-permute-start.22) | collective-permute-done | bytes 524320 | tf_op jit(solution)/shard_map/ppermute | solution.py:86
  297.8 10.4 %collective-permute-done.23 = bf16[256,1024]{1,0:T(8,128)(2,1)S(1)} collective-permute-done((bf16[256,1024]{1,0:T(8,128)(2,1)}, bf16[256,1024]{1,0:T(8,128)(2,1)S(1)}, u32[]{:S(2)}, u32[]{:S(2)}) %collective-permute-start.23) | collective-permute-done | bytes 524320 | tf_op jit(solution)/shard_map/ppermute | solution.py:86
  310.5 3.2 convert_element_type.215
  315.5 1.7 multiply_convert_fusion
  317.1 8.3 %fusion.49 = (bf16[2048,128]{1,0:T(8,128)(2,1)S(1)}, f32[]{:T(128)}) fusion(bf16[2048,128]{1,0:T(8,128)(2,1)S(1)} %bitcast.76, s32[2048]{0:T(1024)S(1)} %get-tuple-element.53, s32[2048]{0:T(1024)S(1)} %bitcast.82, bf16[64,2048]{1,0:T(8,128)(2,1)S(1)} %collective-permute-done.12, bf16[64,2048]{1,0:T(8,128)(2,1)S(1)} %add_convert_fusion.1, ...), kind=kOutput, calls=%fused_computation.178 | convolution fusion | flops 1624899584 | bytes 1605636 | tf_op jit(solution)/shard_map/dot_general | solution.py:160
  326.1 1.8 collective-permute-start.13
  332.2 2.0 collective-permute-start.14
  338.3 4.7 %collective-permute-start.16 = (f32[]{:T(128)}, f32[]{:T(128)}, u32[]{:S(2)}, u32[]{:S(2)}) collective-permute-start(f32[]{:T(128)} %add.334), channel_id=1, source_target_pairs={{0,8},{1,9},{2,10},{3,11},{4,12},{5,13},{6,14},{7,15},{8,0},{9,1},... | collective-permute-start | bytes 20 | tf_op jit(solution)/shard_map/ppermute | solution.py:92
  343.2 4.4 %collective-permute-start.28 = (bf16[256,128]{1,0:T(8,128)(2,1)S(1)}, bf16[256,128]{1,0:T(8,128)(2,1)S(1)}, u32[]{:S(2)}, u32[]{:S(2)}) collective-permute-start(bf16[256,128]{1,0:T(8,128)(2,1)S(1)} %get-tuple-element.44), channel_id=1, source_target_pairs={{0,5},{1,4},{2,7},{3,6},{4,1},{5,0},{6,3},{7,2},{8,13},{9,12},{10,... | collective-permute-start | bytes 196616 | tf_op jit(solution)/shard_map/ppermute | solution.py:86
  348.3 6.6 %convert_multiply_fusion = f32[256,8192]{1,0:T(8,128)} fusion(bf16[256,8192]{1,0:T(8,128)(2,1)} %constant_dynamic-update-slice_fusion.14, f32[]{:T(128)S(6)} %min.3), kind=kLoop, calls=%fused_computation.16 | loop fusion | flops 4194304 | bytes 12582916 | tf_op jit(solution)/shard_map/mul | solution.py:19
  354.8 22.4 %multiply_subtract_fusion = (f32[8,32,8192]{2,1,0:T(8,128)}, f32[8,32,8192]{2,1,0:T(8,128)}, f32[8,32,8192]{2,1,0:T(8,128)}) fusion(f32[8,32,8192]{2,1,0:T(8,128)} %param.18, f32[8,32,8192]{2,1,0:T(8,128)} %bitcast.63, f32[8,32,8192]{2,1,0:T(8,128)} %param.20, f32[8,32,8192]{2,1,0:T(8,128)} %param.21), kind=kLoop, calls=%fused_computation.14 | loop fusion | flops 31457280 | bytes 58720256 | tf_op jit(solution)/shard_map/sub | solution.py:22
  378.7 2.6 collective-permute-done.29
  381.3 1.9 collective-permute-done.30
  383.4 3.5 multiply_subtract_fusion.1
  (152 shorter events, 42.3 us)
Async XLA Ops:
  0.6 9.3 %copy-start.3 = (bf16[128,1024]{1,0:T(8,128)(2,1)S(1)}, bf16[128,1024]{1,0:T(8,128)(2,1)}, u32[]{:S(2)}) copy-start(bf16[128,1024]{1,0:T(8,128)(2,1)} %param.14) | copy-start | bytes 786436
  0.6 9.3 %copy-start.6 = (s32[128,1]{0,1:T(1,128)S(1)}, s32[128,1]{0,1:T(1,128)}, u32[]{:S(2)}) copy-start(s32[128,1]{0,1:T(1,128)} %param.15) | copy-start | bytes 1540
  0.7 37.8 %copy-start.1 = (bf16[128,8192]{1,0:T(8,128)(2,1)S(1)}, bf16[128,8192]{1,0:T(8,128)(2,1)}, u32[]{:S(2)}) copy-start(bf16[128,8192]{1,0:T(8,128)(2,1)} %param.13) | copy-start | bytes 6291460
  5.4 11.4 %all-to-all-start.1 = ((bf16[8,256,128]{2,1,0:T(8,128)(2,1)}), bf16[8,256,128]{2,1,0:T(8,128)(2,1)S(1)}, u32[]{:S(2)}, u32[]{:S(2)}) async-start(bf16[8,256,128]{2,1,0:T(8,128)(2,1)} %copy.33), calls=%async_computation.1 | async-start | bytes 1048576 | tf_op jit(solution)/shard_map/all_to_all | solution.py:80
  43.6 143.9 %all-to-all-start.3 = ((bf16[16,128,1024]{2,1,0:T(8,128)(2,1)}), bf16[16,128,1024]{2,1,0:T(8,128)(2,1)}, u32[]{:S(2)}, u32[]{:S(2)}) async-start(bf16[16,128,1024]{2,1,0:T(8,128)(2,1)} %bitcast.65), calls=%async_computation.3 | async-start | bytes 8388608 | tf_op jit(solution)/shard_map/all_to_all | solution.py:83
  50.8 8.6 %copy-start.5 = (s32[128]{0:T(128)S(1)}, s32[128]{0:T(128)}, u32[]{:S(2)}) copy-start(s32[128]{0:T(128)} %param.17) | copy-start | bytes 1540
  50.8 9.9 %copy-start.7 = (s32[64]{0:T(128)S(1)}, s32[64]{0:T(128)}, u32[]{:S(2)}) copy-start(s32[64]{0:T(128)} %param.16) | copy-start | bytes 772
  57.0 10.0 %collective-permute-start.3 = (bf16[256,1024]{1,0:T(8,128)(2,1)}, bf16[256,1024]{1,0:T(8,128)(2,1)}, u32[]{:S(2)}, u32[]{:S(2)}) collective-permute-start(bf16[256,1024]{1,0:T(8,128)(2,1)} %get-tuple-element.24), channel_id=1, source_target_pairs={{0,1},{1,0},{2,3},{3,2},{4,5},{5,4},{6,7},{7,6},{8,9},{9,8},{10,11... | collective-permute-start | bytes 1572872 | tf_op jit(solution)/shard_map/ppermute | solution.py:86
  57.3 28.3 %collective-permute-start.4 = (bf16[256,1024]{1,0:T(8,128)(2,1)}, bf16[256,1024]{1,0:T(8,128)(2,1)S(1)}, u32[]{:S(2)}, u32[]{:S(2)}) collective-permute-start(bf16[256,1024]{1,0:T(8,128)(2,1)} %get-tuple-element.23), channel_id=1, source_target_pairs={{0,2},{1,3},{2,0},{3,1},{4,6},{5,7},{6,4},{7,5},{8,10},{9,11},{10,... | collective-permute-start | bytes 1572872 | tf_op jit(solution)/shard_map/ppermute | solution.py:86
  57.6 45.9 %collective-permute-start.5 = (bf16[256,1024]{1,0:T(8,128)(2,1)}, bf16[256,1024]{1,0:T(8,128)(2,1)S(1)}, u32[]{:S(2)}, u32[]{:S(2)}) collective-permute-start(bf16[256,1024]{1,0:T(8,128)(2,1)} %get-tuple-element.22), channel_id=1, source_target_pairs={{0,3},{1,2},{2,1},{3,0},{4,7},{5,6},{6,5},{7,4},{8,11},{9,10},{10,... | collective-permute-start | bytes 1572872 | tf_op jit(solution)/shard_map/ppermute | solution.py:86
  59.1 72.6 %collective-permute-start.6 = (bf16[256,1024]{1,0:T(8,128)(2,1)}, bf16[256,1024]{1,0:T(8,128)(2,1)S(1)}, u32[]{:S(2)}, u32[]{:S(2)}) collective-permute-start(bf16[256,1024]{1,0:T(8,128)(2,1)} %get-tuple-element.21), channel_id=1, source_target_pairs={{0,4},{1,5},{2,6},{3,7},{4,0},{5,1},{6,2},{7,3},{8,12},{9,13},{10,... | collective-permute-start | bytes 1572872 | tf_op jit(solution)/shard_map/ppermute | solution.py:86
  66.5 3.6 collective-permute-start
  67.0 77.0 %collective-permute-start.7 = (bf16[256,1024]{1,0:T(8,128)(2,1)}, bf16[256,1024]{1,0:T(8,128)(2,1)S(1)}, u32[]{:S(2)}, u32[]{:S(2)}) collective-permute-start(bf16[256,1024]{1,0:T(8,128)(2,1)} %get-tuple-element.20), channel_id=1, source_target_pairs={{0,5},{1,4},{2,7},{3,6},{4,1},{5,0},{6,3},{7,2},{8,13},{9,12},{10,... | collective-permute-start | bytes 1572872 | tf_op jit(solution)/shard_map/ppermute | solution.py:86
  70.2 84.1 %collective-permute-start.8 = (bf16[256,1024]{1,0:T(8,128)(2,1)}, bf16[256,1024]{1,0:T(8,128)(2,1)S(1)}, u32[]{:S(2)}, u32[]{:S(2)}) collective-permute-start(bf16[256,1024]{1,0:T(8,128)(2,1)} %get-tuple-element.19), channel_id=1, source_target_pairs={{0,6},{1,7},{2,4},{3,5},{4,2},{5,3},{6,0},{7,1},{8,14},{9,15},{10,... | collective-permute-start | bytes 1572872 | tf_op jit(solution)/shard_map/ppermute | solution.py:86
  85.6 47.0 %collective-permute-start.1 = (bf16[64,2048]{1,0:T(8,128)(2,1)S(1)}, bf16[64,2048]{1,0:T(8,128)(2,1)S(1)}, u32[]{:S(2)}, u32[]{:S(2)}) collective-permute-start(bf16[64,2048]{1,0:T(8,128)(2,1)S(1)} %add_convert_fusion.5), channel_id=1, source_target_pairs={{0,2},{1,3},{2,0},{3,1},{4,6},{5,7},{6,4},{7,5},{8,10},{9,11},{10,... | collective-permute-start | bytes 786440 | tf_op jit(solution)/shard_map/ppermute | solution.py:92
  103.5 62.3 %collective-permute-start.9 = (bf16[256,1024]{1,0:T(8,128)(2,1)}, bf16[256,1024]{1,0:T(8,128)(2,1)S(1)}, u32[]{:S(2)}, u32[]{:S(2)}) collective-permute-start(bf16[256,1024]{1,0:T(8,128)(2,1)} %get-tuple-element.18), channel_id=1, source_target_pairs={{0,7},{1,6},{2,5},{3,4},{4,3},{5,2},{6,1},{7,0},{8,15},{9,14},{10,... | collective-permute-start | bytes 1572872 | tf_op jit(solution)/shard_map/ppermute | solution.py:86
  132.6 38.4 %collective-permute-start.2 = (bf16[64,2048]{1,0:T(8,128)(2,1)S(1)}, bf16[64,2048]{1,0:T(8,128)(2,1)S(1)}, u32[]{:S(2)}, u32[]{:S(2)}) collective-permute-start(bf16[64,2048]{1,0:T(8,128)(2,1)S(1)} %add_convert_fusion.4), channel_id=1, source_target_pairs={{0,4},{1,5},{2,6},{3,7},{4,0},{5,1},{6,2},{7,3},{8,12},{9,13},{10,... | collective-permute-start | bytes 786440 | tf_op jit(solution)/shard_map/ppermute | solution.py:92
  171.1 6.0 %copy-start.4 = (bf16[2048,1024]{1,0:T(8,128)(2,1)S(1)}, bf16[2048,1024]{1,0:T(8,128)(2,1)}, u32[]{:S(2)}) copy-start(bf16[2048,1024]{1,0:T(8,128)(2,1)} %constant_dynamic-update-slice_fusion) | copy-start | bytes 12582916
  173.7 3.4 copy-start.8
  187.5 123.1 %all-to-all-start.2 = ((bf16[16,128,1024]{2,1,0:T(8,128)(2,1)}), bf16[16,128,1024]{2,1,0:T(8,128)(2,1)}, u32[]{:S(2)}, u32[]{:S(2)}) async-start(bf16[16,128,1024]{2,1,0:T(8,128)(2,1)} %bitcast.70), calls=%async_computation.2 | async-start | bytes 8388608 | tf_op jit(solution)/shard_map/all_to_all | solution.py:83
  200.3 64.1 %collective-permute-start.17 = (bf16[256,1024]{1,0:T(8,128)(2,1)}, bf16[256,1024]{1,0:T(8,128)(2,1)}, u32[]{:S(2)}, u32[]{:S(2)}) collective-permute-start(bf16[256,1024]{1,0:T(8,128)(2,1)} %get-tuple-element.41), channel_id=1, source_target_pairs={{0,1},{1,0},{2,3},{3,2},{4,5},{5,4},{6,7},{7,6},{8,9},{9,8},{10,11... | collective-permute-start | bytes 1572872 | tf_op jit(solution)/shard_map/ppermute | solution.py:86
  205.9 60.5 %collective-permute-start.18 = (bf16[256,1024]{1,0:T(8,128)(2,1)}, bf16[256,1024]{1,0:T(8,128)(2,1)S(1)}, u32[]{:S(2)}, u32[]{:S(2)}) collective-permute-start(bf16[256,1024]{1,0:T(8,128)(2,1)} %get-tuple-element.39), channel_id=1, source_target_pairs={{0,2},{1,3},{2,0},{3,1},{4,6},{5,7},{6,4},{7,5},{8,10},{9,11},{10,... | collective-permute-start | bytes 1572872 | tf_op jit(solution)/shard_map/ppermute | solution.py:86
  211.4 58.6 %collective-permute-start.19 = (bf16[256,1024]{1,0:T(8,128)(2,1)}, bf16[256,1024]{1,0:T(8,128)(2,1)S(1)}, u32[]{:S(2)}, u32[]{:S(2)}) collective-permute-start(bf16[256,1024]{1,0:T(8,128)(2,1)} %get-tuple-element.37), channel_id=1, source_target_pairs={{0,3},{1,2},{2,1},{3,0},{4,7},{5,6},{6,5},{7,4},{8,11},{9,10},{10,... | collective-permute-start | bytes 1572872 | tf_op jit(solution)/shard_map/ppermute | solution.py:86
  218.1 56.3 %collective-permute-start.20 = (bf16[256,1024]{1,0:T(8,128)(2,1)}, bf16[256,1024]{1,0:T(8,128)(2,1)S(1)}, u32[]{:S(2)}, u32[]{:S(2)}) collective-permute-start(bf16[256,1024]{1,0:T(8,128)(2,1)} %get-tuple-element.35), channel_id=1, source_target_pairs={{0,4},{1,5},{2,6},{3,7},{4,0},{5,1},{6,2},{7,3},{8,12},{9,13},{10,... | collective-permute-start | bytes 1572872 | tf_op jit(solution)/shard_map/ppermute | solution.py:86
  233.7 29.3 %collective-permute-start.10 = (f32[64,2048]{1,0:T(8,128)S(1)}, f32[64,2048]{1,0:T(8,128)S(1)}, u32[]{:S(2)}, u32[]{:S(2)}) collective-permute-start(f32[64,2048]{1,0:T(8,128)S(1)} %fusion.5), channel_id=1, source_target_pairs={{0,1},{1,0},{2,3},{3,2},{4,5},{5,4},{6,7},{7,6},{8,9},{9,8},{10,11... | collective-permute-start | bytes 1572872 | tf_op jit(solution)/shard_map/ppermute | solution.py:92
  263.0 23.6 %collective-permute-start.21 = (bf16[256,1024]{1,0:T(8,128)(2,1)}, bf16[256,1024]{1,0:T(8,128)(2,1)S(1)}, u32[]{:S(2)}, u32[]{:S(2)}) collective-permute-start(bf16[256,1024]{1,0:T(8,128)(2,1)} %get-tuple-element.33), channel_id=1, source_target_pairs={{0,5},{1,4},{2,7},{3,6},{4,1},{5,0},{6,3},{7,2},{8,13},{9,12},{10,... | collective-permute-start | bytes 1572872 | tf_op jit(solution)/shard_map/ppermute | solution.py:86
  264.4 32.7 %collective-permute-start.22 = (bf16[256,1024]{1,0:T(8,128)(2,1)}, bf16[256,1024]{1,0:T(8,128)(2,1)S(1)}, u32[]{:S(2)}, u32[]{:S(2)}) collective-permute-start(bf16[256,1024]{1,0:T(8,128)(2,1)} %get-tuple-element.31), channel_id=1, source_target_pairs={{0,6},{1,7},{2,4},{3,5},{4,2},{5,3},{6,0},{7,1},{8,14},{9,15},{10,... | collective-permute-start | bytes 1572872 | tf_op jit(solution)/shard_map/ppermute | solution.py:86
  266.4 41.9 %collective-permute-start.23 = (bf16[256,1024]{1,0:T(8,128)(2,1)}, bf16[256,1024]{1,0:T(8,128)(2,1)S(1)}, u32[]{:S(2)}, u32[]{:S(2)}) collective-permute-start(bf16[256,1024]{1,0:T(8,128)(2,1)} %get-tuple-element.29), channel_id=1, source_target_pairs={{0,7},{1,6},{2,5},{3,4},{4,3},{5,2},{6,1},{7,0},{8,15},{9,14},{10,... | collective-permute-start | bytes 1572872 | tf_op jit(solution)/shard_map/ppermute | solution.py:86
  270.0 39.1 %collective-permute-start.11 = (bf16[64,2048]{1,0:T(8,128)(2,1)S(1)}, bf16[64,2048]{1,0:T(8,128)(2,1)S(1)}, u32[]{:S(2)}, u32[]{:S(2)}) collective-permute-start(bf16[64,2048]{1,0:T(8,128)(2,1)S(1)} %add_convert_fusion.2), channel_id=1, source_target_pairs={{0,2},{1,3},{2,0},{3,1},{4,6},{5,7},{6,4},{7,5},{8,10},{9,11},{10,... | collective-permute-start | bytes 786440 | tf_op jit(solution)/shard_map/ppermute | solution.py:92
  309.1 8.0 %collective-permute-start.12 = (bf16[64,2048]{1,0:T(8,128)(2,1)S(1)}, bf16[64,2048]{1,0:T(8,128)(2,1)S(1)}, u32[]{:S(2)}, u32[]{:S(2)}) collective-permute-start(bf16[64,2048]{1,0:T(8,128)(2,1)S(1)} %add_convert_fusion.1), channel_id=1, source_target_pairs={{0,4},{1,5},{2,6},{3,7},{4,0},{5,1},{6,2},{7,3},{8,12},{9,13},{10,... | collective-permute-start | bytes 786440 | tf_op jit(solution)/shard_map/ppermute | solution.py:92
  326.1 5.5 %collective-permute-start.13 = (f32[]{:T(128)}, f32[]{:T(128)}, u32[]{:S(2)}, u32[]{:S(2)}) collective-permute-start(f32[]{:T(128)} %add.331), channel_id=1, source_target_pairs={{0,1},{1,0},{2,3},{3,2},{4,5},{5,4},{6,7},{7,6},{8,9},{9,8},{10,11... | collective-permute-start | bytes 20 | tf_op jit(solution)/shard_map/ppermute | solution.py:92
  328.0 49.2 %collective-permute-start.24 = (bf16[256,128]{1,0:T(8,128)(2,1)S(1)}, bf16[256,128]{1,0:T(8,128)(2,1)S(1)}, u32[]{:S(2)}, u32[]{:S(2)}) collective-permute-start(bf16[256,128]{1,0:T(8,128)(2,1)S(1)} %get-tuple-element.48), channel_id=1, source_target_pairs={{0,1},{1,0},{2,3},{3,2},{4,5},{5,4},{6,7},{7,6},{8,9},{9,8},{10,11... | collective-permute-start | bytes 196616 | tf_op jit(solution)/shard_map/ppermute | solution.py:86
  328.1 50.0 %collective-permute-start.25 = (bf16[256,128]{1,0:T(8,128)(2,1)S(1)}, bf16[256,128]{1,0:T(8,128)(2,1)S(1)}, u32[]{:S(2)}, u32[]{:S(2)}) collective-permute-start(bf16[256,128]{1,0:T(8,128)(2,1)S(1)} %get-tuple-element.47), channel_id=1, source_target_pairs={{0,2},{1,3},{2,0},{3,1},{4,6},{5,7},{6,4},{7,5},{8,10},{9,11},{10,... | collective-permute-start | bytes 196616 | tf_op jit(solution)/shard_map/ppermute | solution.py:86
  329.4 49.2 %collective-permute-start.26 = (bf16[256,128]{1,0:T(8,128)(2,1)S(1)}, bf16[256,128]{1,0:T(8,128)(2,1)S(1)}, u32[]{:S(2)}, u32[]{:S(2)}) collective-permute-start(bf16[256,128]{1,0:T(8,128)(2,1)S(1)} %get-tuple-element.46), channel_id=1, source_target_pairs={{0,3},{1,2},{2,1},{3,0},{4,7},{5,6},{6,5},{7,4},{8,11},{9,10},{10,... | collective-permute-start | bytes 196616 | tf_op jit(solution)/shard_map/ppermute | solution.py:86
  330.3 48.4 %collective-permute-start.27 = (bf16[256,128]{1,0:T(8,128)(2,1)S(1)}, bf16[256,128]{1,0:T(8,128)(2,1)S(1)}, u32[]{:S(2)}, u32[]{:S(2)}) collective-permute-start(bf16[256,128]{1,0:T(8,128)(2,1)S(1)} %get-tuple-element.45), channel_id=1, source_target_pairs={{0,4},{1,5},{2,6},{3,7},{4,0},{5,1},{6,2},{7,3},{8,12},{9,13},{10,... | collective-permute-start | bytes 196616 | tf_op jit(solution)/shard_map/ppermute | solution.py:86
  332.2 2.4 collective-permute-start.14
  335.2 2.4 collective-permute-start.15
  338.3 4.9 %collective-permute-start.16 = (f32[]{:T(128)}, f32[]{:T(128)}, u32[]{:S(2)}, u32[]{:S(2)}) collective-permute-start(f32[]{:T(128)} %add.334), channel_id=1, source_target_pairs={{0,8},{1,9},{2,10},{3,11},{4,12},{5,13},{6,14},{7,15},{8,0},{9,1},... | collective-permute-start | bytes 20 | tf_op jit(solution)/shard_map/ppermute | solution.py:92
  343.2 35.5 %collective-permute-start.28 = (bf16[256,128]{1,0:T(8,128)(2,1)S(1)}, bf16[256,128]{1,0:T(8,128)(2,1)S(1)}, u32[]{:S(2)}, u32[]{:S(2)}) collective-permute-start(bf16[256,128]{1,0:T(8,128)(2,1)S(1)} %get-tuple-element.44), channel_id=1, source_target_pairs={{0,5},{1,4},{2,7},{3,6},{4,1},{5,0},{6,3},{7,2},{8,13},{9,12},{10,... | collective-permute-start | bytes 196616 | tf_op jit(solution)/shard_map/ppermute | solution.py:86
  354.8 28.5 %copy-start = (f32[8,32,1024]{2,1,0:T(8,128)S(1)}, f32[8,32,1024]{2,1,0:T(8,128)}, u32[]{:S(2)}) copy-start(f32[8,32,1024]{2,1,0:T(8,128)} %param.19) | copy-start | bytes 3145732
  354.8 28.5 %copy-start.2 = (f32[8,32,1024]{2,1,0:T(8,128)S(1)}, f32[8,32,1024]{2,1,0:T(8,128)}, u32[]{:S(2)}) copy-start(f32[8,32,1024]{2,1,0:T(8,128)} %param.22) | copy-start | bytes 3145732
  377.2 4.1 %collective-permute-start.29 = (bf16[256,128]{1,0:T(8,128)(2,1)S(1)}, bf16[256,128]{1,0:T(8,128)(2,1)S(1)}, u32[]{:S(2)}, u32[]{:S(2)}) collective-permute-start(bf16[256,128]{1,0:T(8,128)(2,1)S(1)} %get-tuple-element.43), channel_id=1, source_target_pairs={{0,6},{1,7},{2,4},{3,5},{4,2},{5,3},{6,0},{7,1},{8,14},{9,15},{10,... | collective-permute-start | bytes 196616 | tf_op jit(solution)/shard_map/ppermute | solution.py:86
  378.2 5.0 %collective-permute-start.30 = (bf16[256,128]{1,0:T(8,128)(2,1)S(1)}, bf16[256,128]{1,0:T(8,128)(2,1)S(1)}, u32[]{:S(2)}, u32[]{:S(2)}) collective-permute-start(bf16[256,128]{1,0:T(8,128)(2,1)S(1)} %get-tuple-element.42), channel_id=1, source_target_pairs={{0,7},{1,6},{2,5},{3,4},{4,3},{5,2},{6,1},{7,0},{8,15},{9,14},{10,... | collective-permute-start | bytes 196616 | tf_op jit(solution)/shard_map/ppermute | solution.py:86

commit v2 on v1

v2 whole, which is shorter than its diff:
```python
import jax
import jax.numpy as jnp
from jax import lax
from jax.experimental import pallas as pl
from jax.experimental.pallas import tpu as pltpu
from jax.sharding import PartitionSpec as P

adapter_alpha_value = 16.0
clip_limit = 1.0
norm_eps = 1e-06
beta_one = 0.9
beta_two = 0.999
bias_one = 0.9999734386011124
bias_two = 0.0952078528862904
learn_rate = 0.0002
decay_rate = 0.01
adam_eps = 1e-08


def adamw_update(params, moment, second, gradient, clip_factor):
    clipped = clip_factor * gradient
    moment = beta_one * moment + (1.0 - beta_one) * clipped
    second = beta_two * second + (1.0 - beta_two) * clipped * clipped
    params = params - learn_rate * (
        moment / bias_one / (jnp.sqrt(second / bias_two) + adam_eps) + decay_rate * params
    )
    return (params, moment, second)


ROOM = pltpu.CompilerParams(vmem_limit_bytes=28 * 1024 * 1024)
NT = (((1,), (1,)), ((), ()))
TN = (((0,), (0,)), ((), ()))


def whole(array):
    return pl.BlockSpec(array.shape, lambda *_: (0,) * array.ndim)


def cost(flops, size):
    return pl.CostEstimate(flops=flops // 4096, bytes_accessed=size // 4096, transcendentals=0)


def narrow(units, ids, left, stacks, places, depth):
    rows, span = left.shape
    size = stacks[0].shape[1]
    tile = min(rows, 256)

    def kernel(units_ref, ids_ref, left_ref, *refs):
        out_ref = refs[-1]
        twice = 2 * ids_ref[...]
        first = jnp.zeros((depth, tile), jnp.float32)
        second = first
        for c, (stack, place) in enumerate(places):
            product = lax.dot_general(refs[stack][place], left_ref[...], NT, preferred_element_type=jnp.float32)
            for k in range(size // depth):
                unit = units_ref[c * (size // depth) + k]
                lanes = product[k * depth : (k + 1) * depth]
                first = first + jnp.where(twice == unit, lanes, 0.0)
                second = second + jnp.where(twice + 1 == unit, lanes, 0.0)
        out_ref[:depth, :] = first
        out_ref[depth:, :] = second

    return pl.pallas_call(
        kernel,
        grid_spec=pltpu.PrefetchScalarGridSpec(
            num_scalar_prefetch=1,
            grid=(rows // tile,),
            in_specs=[
                pl.BlockSpec((1, tile), lambda i, _: (0, i)),
                pl.BlockSpec((tile, span), lambda i, _: (i, 0)),
            ]
            + [whole(stack) for stack in stacks],
            out_specs=pl.BlockSpec((2 * depth, tile), lambda i, _: (0, i)),
        ),
        out_shape=jax.ShapeDtypeStruct((2 * depth, rows), jnp.float32),
        compiler_params=ROOM,
        cost_estimate=cost(2 * rows * size * len(places) * span, 2 * rows * span),
        name="narrow",
    )(units, ids, left, *stacks)


def spread(unit, twice, lanes, depth):
    second = jnp.where(twice + 1 == unit, lanes[depth:], 0.0)
    return jnp.where(twice == unit, lanes[:depth], second).astype(jnp.bfloat16)


def pieces_of(units, ids, lanes, stacks, places, depth):
    rows = lanes.shape[1]
    _, size, span = stacks[0].shape
    tile = min(rows, 256)

    def kernel(units_ref, ids_ref, lanes_ref, *refs):
        out_ref, wide = refs[-2:]
        twice = 2 * ids_ref[...]
        total = jnp.zeros((tile, span), jnp.float32)
        for c, (stack, place) in enumerate(places):
            for k in range(size // depth):
                unit = units_ref[c * (size // depth) + k]
                wide[c, k * depth : (k + 1) * depth, :] = spread(unit, twice, lanes_ref[...], depth)
            total = total + lax.dot_general(
                wide[c], refs[stack][place], TN, preferred_element_type=jnp.float32
            )
        out_ref[...] = total.astype(out_ref.dtype)

    return pl.pallas_call(
        kernel,
        grid_spec=pltpu.PrefetchScalarGridSpec(
            num_scalar_prefetch=1,
            grid=(rows // tile,),
            in_specs=[
                pl.BlockSpec((1, tile), lambda i, _: (0, i)),
                pl.BlockSpec((2 * depth, tile), lambda i, _: (0, i)),
            ]
            + [whole(stack) for stack in stacks],
            out_specs=pl.BlockSpec((tile, span), lambda i, _: (i, 0)),
            scratch_shapes=[pltpu.VMEM((len(places), size, tile), jnp.bfloat16)],
        ),
        out_shape=jax.ShapeDtypeStruct((rows, span), jnp.bfloat16),
        compiler_params=ROOM,
        cost_estimate=cost(2 * rows * size * len(places) * span, 2 * rows * span),
        name="pieces",
    )(units, ids, lanes, *stacks)


def gradient(units, ids, lanes, right, scale, parts, depth):
    rows, span = right.shape
    cols = scale.shape[0]
    size = cols // parts

    def kernel(units_ref, ids_ref, lanes_ref, right_ref, scale_ref, out_ref, square_ref, wide):
        b = pl.program_id(0)
        twice = 2 * ids_ref[...]
        for u in range(size // depth):
            wide[u * depth : (u + 1) * depth, :] = spread(
                units_ref[b * (size // depth) + u], twice, lanes_ref[...], depth
            )
        grad = scale_ref[...] * jnp.dot(wide[...], right_ref[...], preferred_element_type=jnp.float32)
        out_ref[0] = grad.astype(out_ref.dtype)

        @pl.when(b == 0)
        def _():
            square_ref[...] = jnp.zeros_like(square_ref)

        square_ref[...] += jnp.sum(grad * grad, axis=0, keepdims=True)

    return pl.pallas_call(
        kernel,
        grid_spec=pltpu.PrefetchScalarGridSpec(
            num_scalar_prefetch=1,
            grid=(parts,),
            in_specs=[
                whole(ids),
                whole(lanes),
                whole(right),
                pl.BlockSpec((size, 1), lambda i, _: (i, 0)),
            ],
            out_specs=[
                pl.BlockSpec((1, size, span), lambda i, _: (i, 0, 0)),
                pl.BlockSpec((1, span), lambda i, _: (0, 0)),
            ],
            scratch_shapes=[pltpu.VMEM((size, rows), jnp.bfloat16)],
        ),
        out_shape=[
            jax.ShapeDtypeStruct((parts, size, span), jnp.bfloat16),
            jax.ShapeDtypeStruct((1, span), jnp.float32),
        ],
        compiler_params=ROOM,
        cost_estimate=cost(2 * rows * cols * span, 2 * (rows + cols) * span),
        name="gradient",
    )(units, ids, lanes, right, scale.reshape(cols, 1))


def update_slots(params, moment, second, stacks, places, columns, clip_factor):
    count = len(places)
    _, rows, cut = stacks[0].shape
    width = count * cut
    tile = min(rows, max(16, 131072 // cut))

    def kernel(columns_ref, clip_ref, p_ref, m_ref, v_ref, *refs):
        new_p_ref, new_m_ref, new_v_ref, grad = refs[-4:]
        c, i = pl.program_id(0), pl.program_id(1)
        start = pl.multiple_of(i * tile, tile)
        for k, (stack, place) in enumerate(places):

            @pl.when(c == k)
            def _():
                grad[...] = refs[stack][place, pl.ds(start, tile), :].astype(jnp.float32)

        new = adamw_update(p_ref[...], m_ref[...], v_ref[...], grad[...], clip_ref[0, 0])
        new_p_ref[...], new_m_ref[...], new_v_ref[...] = new

    block = pl.BlockSpec((tile, cut), lambda c, i, columns_ref: (i, columns_ref[c]))
    shape = jax.ShapeDtypeStruct((rows, width), jnp.float32)
    new = pl.pallas_call(
        kernel,
        grid_spec=pltpu.PrefetchScalarGridSpec(
            num_scalar_prefetch=1,
            grid=(count, rows // tile),
            in_specs=[pl.BlockSpec(memory_space=pltpu.SMEM)] + [block] * 3 + [whole(stack) for stack in stacks],
            out_specs=[block] * 3,
            scratch_shapes=[pltpu.VMEM((tile, cut), jnp.float32)],
        ),
        out_shape=[shape] * 3,
        compiler_params=ROOM,
        cost_estimate=cost(20 * rows * width, 26 * rows * width),
        name="update",
    )(columns, clip_factor.reshape(1, 1), *[a.reshape(rows, width) for a in (params, moment, second)], *stacks)
    return [a.reshape(params.shape) for a in new]


def join(back, scale, team):
    _, rows, cut = back.shape

    def kernel(one_ref, two_ref, scale_ref, out_ref):
        total = one_ref[0].astype(jnp.float32) + two_ref[0].astype(jnp.float32)
        out_ref[...] = (scale_ref[...] * total).astype(out_ref.dtype)

    return pl.pallas_call(
        kernel,
        grid=(team,),
        in_specs=[
            pl.BlockSpec((1, rows, cut), lambda j: (j, 0, 0)),
            pl.BlockSpec((1, rows, cut), lambda j: (team + j, 0, 0)),
            pl.BlockSpec((rows, 1), lambda j: (0, 0)),
        ],
        out_specs=pl.BlockSpec((rows, cut), lambda j: (0, j)),
        out_shape=jax.ShapeDtypeStruct((rows, team * cut), back.dtype),
        compiler_params=ROOM,
        cost_estimate=cost(3 * rows * team * cut, 6 * rows * team * cut),
        name="join",
    )(back, back, scale)


def on_device(
    acts,
    grad_out,
    row_adapter,
    ranks,
    owner_map,
    down_slots,
    up_slots,
    down_first,
    down_second,
    up_first,
    up_second,
):
    rows, width = acts.shape
    out_width = grad_out.shape[1]
    devices = lax.axis_size("dp")
    own, depth = down_slots.shape[0], down_slots.shape[1]
    slots = owner_map.shape[0]
    halves = 2
    team = devices // halves
    cut = width // team
    out_cut = out_width // team
    half_slots = own * team
    all_rows = devices * rows
    span = own * depth
    me = lax.axis_index("dp")
    seat = me % team
    f32, bf16 = jnp.float32, jnp.bfloat16

    unit_labels = jnp.arange(slots, dtype=jnp.int32)
    adapter_labels = jnp.arange(ranks.shape[0], dtype=jnp.int32)

    def describe(first_slot, count):
        here = first_slot + jnp.arange(count, dtype=jnp.int32)
        unit = jnp.sum(jnp.where(owner_map[None, :] == here[:, None], unit_labels[None, :], 0), axis=1)
        rank = jnp.sum(
            jnp.where(adapter_labels[None, :] == (unit // 2)[:, None], ranks[None, :], 0), axis=1
        )
        return unit, rank

    own_unit, own_rank = describe(me * own, own)
    keep = (own_unit % 2)[:, None] * depth + jnp.arange(depth, dtype=jnp.int32)[None, :] < own_rank[:, None]
    keep = keep.reshape(span, 1)
    down_flat = down_slots.reshape(span, width)
    up16 = jnp.where(keep, up_slots.reshape(span, out_width), 0.0).astype(bf16)

    def sliced(array, pieces):
        return array.reshape(array.shape[0], pieces, -1).transpose(1, 0, 2)

    def to_all(array):
        return lax.all_to_all(array, "dp", split_axis=0, concat_axis=0, tiled=True)

    core = seat % 2
    order = list(range(0, team, 2)) + list(range(1, team, 2))
    peers = [seat ^ b for b in order]

    def to_team(array):
        groups = [[h * team + j for j in range(team)] for h in range(halves)]
        return lax.all_to_all(array, "dp", split_axis=0, concat_axis=0, axis_index_groups=groups, tiled=True)

    def send(array, apart):
        return lax.ppermute(array, "dp", [(i, i ^ apart) for i in range(devices)])

    def swap(blocks, beside, packed=False):
        count = team // 2
        got, beside = lax.optimization_barrier((send(jnp.stack(blocks[count:]), 1), beside))
        pairs = [jnp.stack([blocks[k], got[k]]) for k in range(1, count)]
        if packed:
            pairs, beside = lax.optimization_barrier((pairs, beside))
        return beside, [blocks[0][None], got] + [send(pair, b) for pair, b in zip(pairs, order[1:])]

    def swap_back(parts):
        count = team // 2
        pairs = [send(parts[2 * k : 2 * k + 2], 2 * k) for k in range(1, count)]
        got = send(jnp.stack([parts[1]] + [pair[1] for pair in pairs]), 1)
        return [parts[:1]] + pairs + [got]

    places = [(0, 0)] + [(k + 1, 0) for k in range(1, team // 2)]
    places = places + [(1, 0)] + [(k + 1, 1) for k in range(1, team // 2)]

    def chip_sum(part):
        return part + send(part, 1)

    def team_sum(chip, beside):
        half = chip.shape[1] // 2
        mine = lax.dynamic_slice_in_dim(chip, core * half, half, axis=1)
        step = 2
        while step < team:
            other, beside = lax.optimization_barrier((send(mine.astype(bf16), step), beside))
            mine = mine + other.astype(f32)
            step *= 2
        mine = mine.astype(bf16)
        other = send(mine, 1)
        even = core == 0
        both = [jnp.where(even, mine, other), jnp.where(even, other, mine)]
        return jnp.concatenate(both, axis=1).astype(f32), beside

    def double(array):
        step = 1
        while step < devices:
            array = array + send(array, step)
            step *= 2
        return array

    def columns_of(array, peer, size):
        return lax.dynamic_slice_in_dim(array, peer * size, size, axis=1)

    id_rows = -(-rows // out_cut)
    id_block = jnp.pad(row_adapter[:, 0], (0, id_rows * out_cut - rows)).astype(bf16)
    id_block = jnp.pad(id_block.reshape(id_rows, out_cut), ((0, -id_rows % 16), (0, 0)))
    tall = rows + id_block.shape[0]
    g_and_b = jnp.concatenate([grad_out, jnp.tile(id_block, (1, team)), up16], axis=0)
    _, stacks = swap([columns_of(g_and_b, peer, out_cut) for peer in peers], ())
    blocks = [stacks[stack][place] for stack, place in places]
    mine = jnp.zeros((team * tall, out_cut), bf16)
    for peer, block in zip(peers, blocks):
        mine = lax.dynamic_update_slice_in_dim(mine, block[:tall], peer * tall, axis=0)
    b_cut = jnp.stack([block[tall:] for block in blocks])
    theirs = lax.ppermute(mine, "dp", [(i, (i + team) % devices) for i in range(devices)])
    lower = me < team
    g_got = jnp.concatenate([jnp.where(lower, mine, theirs), jnp.where(lower, theirs, mine)], axis=0)
    g_got = g_got.reshape(devices, tall, out_cut)
    g_cut = g_got[:, :rows].reshape(all_rows, out_cut)
    ids = g_got[:, rows : rows + id_rows].reshape(devices, -1)[:, :rows].reshape(1, all_rows)
    ids = ids.astype(f32).astype(jnp.int32)

    half_unit, half_rank = describe(me // team * half_slots, half_slots)
    seats = jnp.stack(peers)
    units = jnp.take(half_unit.reshape(team, own), seats, axis=0).reshape(-1)
    unit_rank = jnp.take(half_rank.reshape(team, own), seats, axis=0).reshape(-1)
    col_scale = adapter_alpha_value / jnp.repeat(unit_rank, depth).astype(f32)
    pair_seats = jnp.arange(team, dtype=jnp.int32) ^ seat
    pair_units = jnp.take(half_unit.reshape(team, own), pair_seats, axis=0).reshape(-1)
    pair_rank = jnp.take(half_rank.reshape(team, own), pair_seats, axis=0).reshape(-1)
    pair_scale = adapter_alpha_value / jnp.repeat(pair_rank, depth).astype(f32)
    half_scale = adapter_alpha_value / jnp.repeat(half_rank, depth).astype(f32)

    acts_send = jnp.tile(sliced(acts, team), (halves, 1, 1))
    acts_send, g_cut = lax.optimization_barrier((acts_send, g_cut))
    x_cut = to_all(acts_send).reshape(all_rows, cut)
    alone = [(0, k) for k in range(team)]
    low_chip = chip_sum(narrow(units, ids, g_cut, [b_cut], alone, depth))
    low_chip, down_late = lax.optimization_barrier((low_chip, down_flat))
    a_blocks = [jnp.where(keep, columns_of(down_late, peer, cut), 0.0).astype(bf16) for peer in peers]
    low_chip, a_stacks = swap(a_blocks, low_chip)
    low, _ = team_sum(low_chip, ids)
    down_parts, down_squares = gradient(pair_units, ids, low, x_cut, pair_scale, team, depth)
    down_stacks = swap_back(down_parts)
    down_places = [(k, 0) for k in range(team // 2)] + [(team // 2, k) for k in range(team // 2)]
    x_late, a_stacks, _ = lax.optimization_barrier((x_cut, a_stacks, down_parts))
    hidden_part = narrow(units, ids, x_late, a_stacks, places, depth)
    hidden_chip, a_stacks = lax.optimization_barrier((chip_sum(hidden_part), a_stacks))
    piece = pieces_of(units, ids, low, a_stacks, places, depth)
    hidden, piece = team_sum(hidden_chip, piece)
    up_parts, up_squares = gradient(half_unit, ids, hidden, g_cut, half_scale, team, depth)
    up_home = to_team(up_parts)
    squares = double(jnp.sum(down_squares) + jnp.sum(up_squares))
    clip_factor = jnp.minimum(1.0, clip_limit / (jnp.sqrt(squares) + norm_eps))
    piece, _, down_stacks, up_home = lax.optimization_barrier((piece, squares, down_stacks, up_home))
    back = to_all(piece.reshape(devices, rows, cut))
    columns = jnp.stack(peers)
    down_new = update_slots(down_slots, down_first, down_second, down_stacks, down_places, columns, clip_factor)
    up_grad = up_home.transpose(1, 0, 2).reshape(own, depth, out_width).astype(f32)
    up_new = adamw_update(up_slots, up_first, up_second, up_grad, clip_factor)

    row_rank = jnp.sum(jnp.where(row_adapter == adapter_labels[None, :], ranks[None, :], 0), axis=1)
    input_grad = join(back, (adapter_alpha_value / row_rank.astype(f32))[:, None], team)
    return (input_grad, down_new[0], up_new[0], down_new[1], down_new[2], up_new[1], up_new[2])


def solution(mesh):
    two = P(("groups", "dp"), None)
    three = P(("groups", "dp"), None, None)
    return jax.shard_map(
        on_device,
        mesh=mesh,
        in_specs=(two, two, two, P(), P(), three, three, three, three, three, three),
        out_specs=(two, three, three, three, three, three, three),
        check_vma=False,
    )
```

time: 393 us -> 363 us (0.924); the launches traced: 387 us -> 361 us
  matrix products: 82.8 us -> 0 us
  Pallas kernels: 0 us -> 76.4 us
  waiting for transfers between devices: 132 us -> 177 us
  other arithmetic: 48.8 us -> 25.4 us
  blocking collectives: 21.7 us -> 0 us
  starting transfers between devices: 60.4 us -> 48.8 us
  between operations: 9.87 us -> 5.41 us
    dot_general x13 -> x0, matrix products: 82.8 us -> none  [the longest x8 41.3 us: on_device(): lax.dot_general(low[:, span], x_late, (((0,), (0,)), ((), ())), preferred...]
    pallas_call x0 -> x7, Pallas kernels: none -> 76.4 us  [the longest x2 20.4 us: narrow(): pl.pallas_call(kernel, grid_spec=pltpu.PrefetchScalarGridSpec(num_scalar_...]
    all_to_all x2, waiting for transfers between devices: 0.01 us -> 61.5 us  [to_all(): return lax.all_to_all(array, 'dp', split_axis=0, concat_axis=0, tiled=True)]
    sub x2 -> x1, other arithmetic: 25.8 us -> 3.88 us  [adamw_update(): params - learn_rate * (moment / bias_one / (jnp.sqrt(second / bias_two) +...]
    all_to_all x1 -> x0, blocking collectives: 21.7 us -> none  [to_all(): return lax.all_to_all(array, 'dp', split_axis=0, concat_axis=0, tiled=True)]
    ppermute x31 -> x25, starting transfers between devices: 42.8 us -> 27.3 us  [the longest x24 24.9 us: send(): return lax.ppermute(array, 'dp', [(i, i ^ apart) for i in range(devices)])]
    another operation x0 -> x10, other arithmetic: none -> 13.4 us  [the longest x7 9.12 us: swap(): pairs = [jnp.stack([blocks[k], got[k]]) for k in range(1, count)]]
    ppermute x31 -> x25, waiting for transfers between devices: 126 us -> 116 us  [the longest x24 103 us: send(): return lax.ppermute(array, 'dp', [(i, i ^ apart) for i in range(devices)])]
  transfers between devices with their start and end apart: 34 -> 28, of which waited for: 17 -> 14; matrix products, arithmetic and copies ran while one was open for 36% -> 8% of each run, Pallas kernels for 0% -> 19%
where the time goes in v2:
time: 363 us; the launch traced here: 361 us
  waiting for transfers between devices  177 us (49%)
  Pallas kernels  76.4 us (21%)
  starting transfers between devices  48.8 us (13%)
  local copies, waits for them, and re-layouts  28 us (8%)
  other arithmetic  25.4 us (7%)
  between operations  5.41 us (1%)
    ppermute x24, waiting for transfers between devices, send(): return lax.ppermute(array, 'dp', [(i, i ^ apart) for i in range(devices)])  103 us
    all_to_all x2, waiting for transfers between devices, to_all(): return lax.all_to_all(array, 'dp', split_axis=0, concat_axis=0, tiled=True)  61.5 us
    ppermute x24, starting transfers between devices, send(): return lax.ppermute(array, 'dp', [(i, i ^ apart) for i in range(devices)])  24.9 us
    pallas_call x2, Pallas kernels, narrow(): pl.pallas_call(kernel, grid_spec=pltpu.PrefetchScalarGridSpec(num_scalar_...  20.4 us
    pallas_call x2, Pallas kernels, gradient(): pl.pallas_call(kernel, grid_spec=pltpu.PrefetchScalarGridSpec(num_scalar_...  19.3 us
    pallas_call x1, Pallas kernels, update_slots(): pl.pallas_call(kernel, grid_spec=pltpu.PrefetchScalarGridSpec(num_scalar_...  17.6 us
    all_to_all x2, starting transfers between devices, to_all(): return lax.all_to_all(array, 'dp', split_axis=0, concat_axis=0, tiled=True)  17.3 us
    unnamed x67, local copies, waits for them, and re-layouts  13.8 us
  transfers between devices with their start and end apart: 28, of which 14 were waited for; matrix products, arithmetic and copies ran while one was open for 8% of the time, Pallas kernels for 19%

profile of v2, /device:TPU:15, one launch (start us, length us, event | category | flops | bytes accessed | tf_op | source)
XLA Modules:
  0.0 361.1 jit_solution(5295392674813928312)
XLA Ops:
  3.2 1.4 fusion.1
  4.7 1.2 pad_maximum_fusion.5
  7.5 1.4 copy.31
  8.9 1.2 copy.25
  12.0 2.3 collective-permute-start.3
  14.3 3.9 %collective-permute-done.1 = bf16[2,400,128]{2,1,0:T(8,128)(2,1)S(1)} collective-permute-done((bf16[2,400,128]{2,1,0:T(8,128)(2,1)S(1)}, bf16[2,400,128]{2,1,0:T(8,128)(2,1)S(1)}, u32[]{:S(2)}, u32[]{:S(2)}) %collective-permute-start.1) | collective-permute-done | bytes 204832 | tf_op jit(solution)/shard_map/ppermute | solution.py:295
  18.2 5.3 %collective-permute-done.3 = bf16[2,400,128]{2,1,0:T(8,128)(2,1)S(1)} collective-permute-done((bf16[2,400,128]{2,1,0:T(8,128)(2,1)S(1)}, bf16[2,400,128]{2,1,0:T(8,128)(2,1)S(1)}, u32[]{:S(2)}, u32[]{:S(2)}) %collective-permute-start.3) | collective-permute-done | bytes 204832 | tf_op jit(solution)/shard_map/ppermute | solution.py:295
  24.4 2.4 collective-permute-start.4
  26.8 12.9 %collective-permute-done.4 = bf16[1152,128]{1,0:T(8,128)(2,1)S(1)} collective-permute-done((bf16[1152,128]{1,0:T(8,128)(2,1)S(1)}, bf16[1152,128]{1,0:T(8,128)(2,1)S(1)}, u32[]{:S(2)}, u32[]{:S(2)}) %collective-permute-start.4) | collective-permute-done | bytes 294944 | tf_op jit(solution)/shard_map/ppermute | solution.py:352
  40.7 2.6 tile.20
  43.3 7.3 %all-to-all-start = ((bf16[16,128,1024]{2,1,0:T(8,128)(2,1)}), bf16[16,128,1024]{2,1,0:T(8,128)(2,1)}, u32[]{:S(2)}, u32[]{:S(2)}) async-start(bf16[16,128,1024]{2,1,0:T(8,128)(2,1)} %bitcast.109), calls=%async_computation | async-start | bytes 8388608 | tf_op jit(solution)/shard_map/all_to_all | solution.py:284
  53.4 5.6 %narrow.2 = f32[64,2048]{1,0:T(8,128)S(1)} custom-call(s32[64]{0:T(128)S(1)} %reshape.272.units_ref, s32[1,2048]{1,0:T(1,128)S(1)} %fusion.21.ids_ref, bf16[2048,128]{1,0:T(8,128)(2,1)S(1)} %bitcast.107, bf16[8,256,128]{2,1,0:T(8,128)(2,1)S(1)} %slice_dynamic-update-slice_fusion.refs_0_), custom_call_target="tpu_custom_call" | custom-call | flops 262144 | bytes 128 | tf_op jit(solution)/shard_map/narrow/pallas_call | solution.py:63
  59.5 1.5 collective-permute-done.5
  61.1 5.9 %fusion.9 = (bf16[1,256,1024]{2,1,0:T(8,128)(2,1)}, bf16[1,256,1024]{2,1,0:T(8,128)(2,1)}, bf16[1,256,1024]{2,1,0:T(8,128)(2,1)}, bf16[1,256,1024]{2,1,0:T(8,128...) fusion(f32[256,8192]{1,0:T(8,128)} %bitcast.103, ...), kind=kLoop, calls=%fused_computation.32 | loop fusion | flops 2097152 | bytes 8388896 | tf_op jit(solution)/shard_map/stack | solution.py:300
  66.9 1.6 pad_maximum_fusion
  70.4 2.5 collective-permute-done.6.refs_1_
  74.4 1.2 collective-permute-start.10
  77.0 45.0 %collective-permute-done.10 = bf16[64,1024]{1,0:T(8,128)(2,1)S(1)} collective-permute-done((bf16[64,1024]{1,0:T(8,128)(2,1)S(1)}, bf16[64,1024]{1,0:T(8,128)(2,1)S(1)}, u32[]{:S(2)}, u32[]{:S(2)}) %collective-permute-start.10) | collective-permute-done | bytes 131104 | tf_op jit(solution)/shard_map/ppermute | solution.py:295
  122.2 1.1 pad_maximum_fusion.4
  123.2 3.5 collective-permute-start.9
  126.7 19.2 %collective-permute-done.11 = bf16[64,1024]{1,0:T(8,128)(2,1)S(1)} collective-permute-done((bf16[64,1024]{1,0:T(8,128)(2,1)S(1)}, bf16[64,1024]{1,0:T(8,128)(2,1)S(1)}, u32[]{:S(2)}, u32[]{:S(2)}) %collective-permute-start.11) | collective-permute-done | bytes 131104 | tf_op jit(solution)/shard_map/ppermute | solution.py:295
  146.0 1.3 collective-permute-start.12
  147.6 2.1 div.116.scale_ref
  149.8 1.2 copy-done.4
  151.0 13.9 %gradient.2 = (bf16[8,256,1024]{2,1,0:T(8,128)(2,1)S(1)}, f32[1,1024]{1,0:T(1,128)S(1)}) custom-call(s32[64]{0:T(128)S(1)} %reshape.279.units_ref, s32[1,2048]{1,0:T(1,128)S(1)} %fusion.21.ids_ref, f32[64,2048]{1,0:T(8,128)S(1)} %maximum_convert_fusion.lanes_ref, bf16[2048,1024]{1,0:T(8,128)(2,1)} %bitcast.29.right_ref.left_ref, f32[2048,1]{1,0:T(8,128)S(1)} %copy-done.4), custom_call_target="tpu_custom_call" | custom-call | flops 2097152 | bytes 2048 | tf_op jit(solution)/shard_map/gradient/pallas_call | solution.py:146
  165.7 2.5 collective-permute-start.21
  168.2 14.8 %narrow.3 = f32[64,2048]{1,0:T(8,128)S(1)} custom-call(s32[64]{0:T(128)S(1)} %reshape.272.units_ref, s32[1,2048]{1,0:T(1,128)S(1)} %fusion.21.ids_ref, bf16[2048,1024]{1,0:T(8,128)(2,1)} %bitcast.29.right_ref.left_ref, bf16[1,256,1024]{2,1,0:T(8,128)(2,1)S(1)} %copy-done.3, bf16[4,256,1024]{2,1,0:T(8,128)(2,1)S(1)} %collective-permute-done.6.refs_1_, ...), custom_call_target="tpu_custom_call" | custom-call | flops 2097152 | bytes 1024 | tf_op jit(solution)/shard_map/narrow/pallas_call | solution.py:63
  183.9 1.5 collective-permute-done.13
  185.5 2.0 collective-permute-start.14
  188.3 12.8 %pieces.1 = bf16[2048,1024]{1,0:T(8,128)(2,1)S(1)} custom-call(s32[64]{0:T(128)S(1)} %reshape.272.units_ref, s32[1,2048]{1,0:T(1,128)S(1)} %fusion.21.ids_ref, f32[64,2048]{1,0:T(8,128)S(1)} %maximum_convert_fusion.lanes_ref, bf16[1,256,1024]{2,1,0:T(8,128)(2,1)S(1)} %copy-done.3, bf16[4,256,1024]{2,1,0:T(8,128)(2,1)S(1)} %collective-permute-done.6.refs_1_, ...), custom_call_target="tpu_custom_call" | custom-call | flops 2097152 | bytes 1024 | tf_op jit(solution)/shard_map/pieces/pallas_call | solution.py:105
  201.2 15.6 %collective-permute-done.14 = bf16[64,1024]{1,0:T(8,128)(2,1)S(1)} collective-permute-done((bf16[64,1024]{1,0:T(8,128)(2,1)S(1)}, bf16[64,1024]{1,0:T(8,128)(2,1)S(1)}, u32[]{:S(2)}, u32[]{:S(2)}) %collective-permute-start.14) | collective-permute-done | bytes 131104 | tf_op jit(solution)/shard_map/ppermute | solution.py:295
  217.0 1.8 pad_maximum_fusion.1
  219.8 5.0 %collective-permute-done.15 = bf16[64,1024]{1,0:T(8,128)(2,1)S(1)} collective-permute-done((bf16[64,1024]{1,0:T(8,128)(2,1)S(1)}, bf16[64,1024]{1,0:T(8,128)(2,1)S(1)}, u32[]{:S(2)}, u32[]{:S(2)}) %collective-permute-start.15) | collective-permute-done | bytes 131104 | tf_op jit(solution)/shard_map/ppermute | solution.py:295
  225.8 1.1 div.117.scale_ref
  227.0 5.4 %gradient.3 = (bf16[8,256,128]{2,1,0:T(8,128)(2,1)}, f32[1,128]{1,0:T(1,128)S(1)}) custom-call(s32[64]{0:T(128)S(1)} %select_reduce_fusion.2.units_ref, s32[1,2048]{1,0:T(1,128)S(1)} %fusion.21.ids_ref, f32[64,2048]{1,0:T(8,128)S(1)} %maximum_convert_fusion.1.lanes_ref, bf16[2048,128]{1,0:T(8,128)(2,1)S(1)} %bitcast.108, f32[2048,1]{1,0:T(8,128)S(1)} %div.117.scale_ref), custom_call_target="tpu_custom_call" | custom-call | flops 262144 | bytes 256 | tf_op jit(solution)/shard_map/gradient/pallas_call | solution.py:146
  232.4 4.2 %all-to-all-start.1 = ((bf16[8,256,128]{2,1,0:T(8,128)(2,1)}), bf16[8,256,128]{2,1,0:T(8,128)(2,1)S(1)}, u32[]{:S(2)}, u32[]{:S(2)}) async-start(bf16[8,256,128]{2,1,0:T(8,128)(2,1)} %get-tuple-element.71), calls=%async_computation.1 | async-start | bytes 1048576 | tf_op jit(solution)/shard_map/all_to_all | solution.py:292
  239.1 1.4 collective-permute-start.17
  241.1 1.4 collective-permute-start.18
  242.5 1.3 collective-permute-done.18
  245.4 1.5 collective-permute-done.19
  247.6 3.1 collective-permute-start.20
  252.3 10.0 %all-to-all-start.2 = ((bf16[16,128,1024]{2,1,0:T(8,128)(2,1)}), bf16[16,128,1024]{2,1,0:T(8,128)(2,1)}, u32[]{:S(2)}, u32[]{:S(2)}) async-start(bf16[16,128,1024]{2,1,0:T(8,128)(2,1)} %bitcast.105), calls=%async_computation.2 | async-start | bytes 8388608 | tf_op jit(solution)/shard_map/all_to_all | solution.py:284
  262.7 3.4 copy-done
  266.1 3.4 copy-done.2
  270.5 17.6 %update.1 = (f32[256,8192]{1,0:T(8,128)}, f32[256,8192]{1,0:T(8,128)}, f32[256,8192]{1,0:T(8,128)}) custom-call(s32[8]{0:T(128)S(1)} %stack.126.columns_ref, f32[1,1]{1,0:T(1,128)} %bitcast.43.clip_ref, f32[256,8192]{1,0:T(8,128)S(1)} %bitcast.104, f32[256,8192]{1,0:T(8,128)S(1)} %bitcast.106, f32[256,8192]{1,0:T(8,128)} %bitcast.110, ...), custom_call_target="tpu_custom_call" | custom-call | flops 10240 | bytes 13312 | tf_op jit(solution)/shard_map/update/pallas_call | solution.py:194
  289.4 3.9 %multiply_subtract_fusion = (f32[8,32,1024]{2,1,0:T(8,128)}, f32[8,32,1024]{2,1,0:T(8,128)}, f32[8,32,1024]{2,1,0:T(8,128)}) fusion(f32[8,32,1024]{2,1,0:T(8,128)S(1)} %copy-done.12, f32[8,32,1024]{2,1,0:T(8,128)S(1)} %mul.174, f32[8,32,1024]{2,1,0:T(8,128)} %param.22, f32[8,32,1024]{2,1,0:T(8,128)} %param.23), kind=kLoop, calls=%fused_computation.12 | loop fusion | flops 3932160 | bytes 7340032 | tf_op jit(solution)/shard_map/sub | solution.py:24
  293.3 61.5 %all-to-all-done.2.one_ref.two_ref = bf16[16,128,1024]{2,1,0:T(8,128)(2,1)} async-done(((bf16[16,128,1024]{2,1,0:T(8,128)(2,1)}), bf16[16,128,1024]{2,1,0:T(8,128)(2,1)}, u32[]{:S(2)}, u32[]{:S(2)}) %all-to-all-start.2) | async-done | bytes 4194336 | tf_op jit(solution)/shard_map/all_to_all | solution.py:284
  354.8 6.3 %join.1 = bf16[128,8192]{1,0:T(8,128)(2,1)} custom-call(bf16[16,128,1024]{2,1,0:T(8,128)(2,1)} %all-to-all-done.2.one_ref.two_ref, bf16[16,128,1024]{2,1,0:T(8,128)(2,1)} %all-to-all-done.2.one_ref.two_ref, f32[128,1]{1,0:T(8,128)S(1)} %copy.28.scale_ref), custom_call_target="tpu_custom_call" | custom-call | flops 768 | bytes 1536 | tf_op jit(solution)/shard_map/join/pallas_call | solution.py:218
  (173 shorter events, 26.8 us)
Async XLA Ops:
  4.6 2.9 copy-start.14
  6.8 3.5 collective-permute-start
  11.4 6.8 %collective-permute-start.1 = (bf16[2,400,128]{2,1,0:T(8,128)(2,1)S(1)}, bf16[2,400,128]{2,1,0:T(8,128)(2,1)S(1)}, u32[]{:S(2)}, u32[]{:S(2)}) collective-permute-start(bf16[2,400,128]{2,1,0:T(8,128)(2,1)S(1)} %pad_maximum_fusion.8), channel_id=1, source_target_pairs={{0,2},{1,3},{2,0},{3,1},{4,6},{5,7},{6,4},{7,5},{8,10},{9,11},{10,... | collective-permute-start | bytes 614408 | tf_op jit(solution)/shard_map/ppermute | solution.py:295
  11.7 6.5 %collective-permute-start.2 = (bf16[2,400,128]{2,1,0:T(8,128)(2,1)S(1)}, bf16[2,400,128]{2,1,0:T(8,128)(2,1)S(1)}, u32[]{:S(2)}, u32[]{:S(2)}) collective-permute-start(bf16[2,400,128]{2,1,0:T(8,128)(2,1)S(1)} %pad_maximum_fusion.9), channel_id=1, source_target_pairs={{0,4},{1,5},{2,6},{3,7},{4,0},{5,1},{6,2},{7,3},{8,12},{9,13},{10,... | collective-permute-start | bytes 614408 | tf_op jit(solution)/shard_map/ppermute | solution.py:295
  12.0 11.5 %collective-permute-start.3 = (bf16[2,400,128]{2,1,0:T(8,128)(2,1)S(1)}, bf16[2,400,128]{2,1,0:T(8,128)(2,1)S(1)}, u32[]{:S(2)}, u32[]{:S(2)}) collective-permute-start(bf16[2,400,128]{2,1,0:T(8,128)(2,1)S(1)} %pad_maximum_fusion.10), channel_id=1, source_target_pairs={{0,6},{1,7},{2,4},{3,5},{4,2},{5,3},{6,0},{7,1},{8,14},{9,15},{10,... | collective-permute-start | bytes 614408 | tf_op jit(solution)/shard_map/ppermute | solution.py:295
  18.2 8.6 %copy-start.20 = (bf16[2,400,128]{2,1,0:T(8,128)(2,1)}, bf16[2,400,128]{2,1,0:T(8,128)(2,1)S(1)}, u32[]{:S(2)}) copy-start(bf16[2,400,128]{2,1,0:T(8,128)(2,1)S(1)} %collective-permute-done.1) | copy-start | bytes 614404
  18.2 8.6 %copy-start.22 = (bf16[2,400,128]{2,1,0:T(8,128)(2,1)}, bf16[2,400,128]{2,1,0:T(8,128)(2,1)S(1)}, u32[]{:S(2)}) copy-start(bf16[2,400,128]{2,1,0:T(8,128)(2,1)S(1)} %collective-permute-done.2) | copy-start | bytes 614404
  23.5 16.3 %copy-start.24 = (bf16[2,400,128]{2,1,0:T(8,128)(2,1)}, bf16[2,400,128]{2,1,0:T(8,128)(2,1)S(1)}, u32[]{:S(2)}) copy-start(bf16[2,400,128]{2,1,0:T(8,128)(2,1)S(1)} %collective-permute-done.3) | copy-start | bytes 614404
  24.4 15.3 %collective-permute-start.4 = (bf16[1152,128]{1,0:T(8,128)(2,1)S(1)}, bf16[1152,128]{1,0:T(8,128)(2,1)S(1)}, u32[]{:S(2)}, u32[]{:S(2)}) collective-permute-start(bf16[1152,128]{1,0:T(8,128)(2,1)S(1)} %fusion.13), channel_id=1, source_target_pairs={{0,8},{1,9},{2,10},{3,11},{4,12},{5,13},{6,14},{7,15},{8,0},{9,1},... | collective-permute-start | bytes 884744 | tf_op jit(solution)/shard_map/ppermute | solution.py:352
  43.3 7.3 %copy-start.26 = (s32[128]{0:T(128)S(1)}, s32[128]{0:T(128)}, u32[]{:S(2)}) copy-start(s32[128]{0:T(128)} %param.17) | copy-start | bytes 1540
  43.3 8.4 %copy-start.21 = (bf16[2,400,128]{2,1,0:T(8,128)(2,1)S(1)}, bf16[2,400,128]{2,1,0:T(8,128)(2,1)}, u32[]{:S(2)}) copy-start(bf16[2,400,128]{2,1,0:T(8,128)(2,1)} %copy-done.20) | copy-start | bytes 614404
  43.3 8.4 %copy-start.23 = (bf16[2,400,128]{2,1,0:T(8,128)(2,1)S(1)}, bf16[2,400,128]{2,1,0:T(8,128)(2,1)}, u32[]{:S(2)}) copy-start(bf16[2,400,128]{2,1,0:T(8,128)(2,1)} %copy-done.22) | copy-start | bytes 614404
  43.3 8.4 %copy-start.25 = (bf16[2,400,128]{2,1,0:T(8,128)(2,1)S(1)}, bf16[2,400,128]{2,1,0:T(8,128)(2,1)}, u32[]{:S(2)}) copy-start(bf16[2,400,128]{2,1,0:T(8,128)(2,1)} %copy-done.24) | copy-start | bytes 614404
  43.3 106.5 %all-to-all-start = ((bf16[16,128,1024]{2,1,0:T(8,128)(2,1)}), bf16[16,128,1024]{2,1,0:T(8,128)(2,1)}, u32[]{:S(2)}, u32[]{:S(2)}) async-start(bf16[16,128,1024]{2,1,0:T(8,128)(2,1)} %bitcast.109), calls=%async_computation | async-start | bytes 8388608 | tf_op jit(solution)/shard_map/all_to_all | solution.py:284
  59.0 2.0 collective-permute-start.5
  68.5 4.4 %collective-permute-start.6 = (bf16[4,256,1024]{2,1,0:T(8,128)(2,1)}, bf16[4,256,1024]{2,1,0:T(8,128)(2,1)S(1)}, u32[]{:S(2)}, u32[]{:S(2)}) collective-permute-start(bf16[4,256,1024]{2,1,0:T(8,128)(2,1)} %pad_maximum_fusion), channel_id=1, source_target_pairs={{0,1},{1,0},{2,3},{3,2},{4,5},{5,4},{6,7},{7,6},{8,9},{9,8},{10,11... | collective-permute-start | bytes 6291464 | tf_op jit(solution)/shard_map/ppermute | solution.py:295
  70.3 2.7 copy-start.19
  70.4 5.2 %copy-start.18 = (bf16[1,256,1024]{2,1,0:T(8,128)(2,1)S(1)}, bf16[1,256,1024]{2,1,0:T(8,128)(2,1)}, u32[]{:S(2)}) copy-start(bf16[1,256,1024]{2,1,0:T(8,128)(2,1)} %get-tuple-element.86) | copy-start | bytes 1572868
  73.0 49.1 %copy-start.17 = (bf16[1,256,1024]{2,1,0:T(8,128)(2,1)S(1)}, bf16[1,256,1024]{2,1,0:T(8,128)(2,1)}, u32[]{:S(2)}) copy-start(bf16[1,256,1024]{2,1,0:T(8,128)(2,1)} %get-tuple-element.85) | copy-start | bytes 1572868
  74.1 91.6 %collective-permute-start.7 = (bf16[2,256,1024]{2,1,0:T(8,128)(2,1)}, bf16[2,256,1024]{2,1,0:T(8,128)(2,1)}, u32[]{:S(2)}, u32[]{:S(2)}) collective-permute-start(bf16[2,256,1024]{2,1,0:T(8,128)(2,1)} %pad_maximum_fusion.2), channel_id=1, source_target_pairs={{0,2},{1,3},{2,0},{3,1},{4,6},{5,7},{6,4},{7,5},{8,10},{9,11},{10,... | collective-permute-start | bytes 3145736 | tf_op jit(solution)/shard_map/ppermute | solution.py:295
  74.4 47.6 %collective-permute-start.10 = (bf16[64,1024]{1,0:T(8,128)(2,1)S(1)}, bf16[64,1024]{1,0:T(8,128)(2,1)S(1)}, u32[]{:S(2)}, u32[]{:S(2)}) collective-permute-start(bf16[64,1024]{1,0:T(8,128)(2,1)S(1)} %dynamic-slice_convert_fusion.1), channel_id=1, source_target_pairs={{0,2},{1,3},{2,0},{3,1},{4,6},{5,7},{6,4},{7,5},{8,10},{9,11},{10,... | collective-permute-start | bytes 393224 | tf_op jit(solution)/shard_map/ppermute | solution.py:295
  76.7 91.4 %collective-permute-start.8 = (bf16[2,256,1024]{2,1,0:T(8,128)(2,1)}, bf16[2,256,1024]{2,1,0:T(8,128)(2,1)}, u32[]{:S(2)}, u32[]{:S(2)}) collective-permute-start(bf16[2,256,1024]{2,1,0:T(8,128)(2,1)} %pad_maximum_fusion.3), channel_id=1, source_target_pairs={{0,4},{1,5},{2,6},{3,7},{4,0},{5,1},{6,2},{7,3},{8,12},{9,13},{10,... | collective-permute-start | bytes 3145736 | tf_op jit(solution)/shard_map/ppermute | solution.py:295
  122.1 23.9 %collective-permute-start.11 = (bf16[64,1024]{1,0:T(8,128)(2,1)S(1)}, bf16[64,1024]{1,0:T(8,128)(2,1)S(1)}, u32[]{:S(2)}, u32[]{:S(2)}) collective-permute-start(bf16[64,1024]{1,0:T(8,128)(2,1)S(1)} %fusion.10), channel_id=1, source_target_pairs={{0,4},{1,5},{2,6},{3,7},{4,0},{5,1},{6,2},{7,3},{8,12},{9,13},{10,... | collective-permute-start | bytes 393224 | tf_op jit(solution)/shard_map/ppermute | solution.py:295
  123.2 44.9 %collective-permute-start.9 = (bf16[2,256,1024]{2,1,0:T(8,128)(2,1)}, bf16[2,256,1024]{2,1,0:T(8,128)(2,1)}, u32[]{:S(2)}, u32[]{:S(2)}) collective-permute-start(bf16[2,256,1024]{2,1,0:T(8,128)(2,1)} %pad_maximum_fusion.4), channel_id=1, source_target_pairs={{0,6},{1,7},{2,4},{3,5},{4,2},{5,3},{6,0},{7,1},{8,14},{9,15},{10,... | collective-permute-start | bytes 3145736 | tf_op jit(solution)/shard_map/ppermute | solution.py:295
  146.0 3.7 %collective-permute-start.12 = (bf16[64,1024]{1,0:T(8,128)(2,1)S(1)}, bf16[64,1024]{1,0:T(8,128)(2,1)S(1)}, u32[]{:S(2)}, u32[]{:S(2)}) collective-permute-start(bf16[64,1024]{1,0:T(8,128)(2,1)S(1)} %add_convert_fusion.1), channel_id=1, source_target_pairs={{0,1},{1,0},{2,3},{3,2},{4,5},{5,4},{6,7},{7,6},{8,9},{9,8},{10,11... | collective-permute-start | bytes 393224 | tf_op jit(solution)/shard_map/ppermute | solution.py:295
  164.8 3.3 copy-start.3
  165.4 51.4 %collective-permute-start.23 = (bf16[2,256,1024]{2,1,0:T(8,128)(2,1)S(1)}, bf16[2,256,1024]{2,1,0:T(8,128)(2,1)S(1)}, u32[]{:S(2)}, u32[]{:S(2)}) collective-permute-start(bf16[2,256,1024]{2,1,0:T(8,128)(2,1)S(1)} %get-tuple-element.95), channel_id=1, source_target_pairs={{0,6},{1,7},{2,4},{3,5},{4,2},{5,3},{6,0},{7,1},{8,14},{9,15},{10,... | collective-permute-start | bytes 3145736 | tf_op jit(solution)/shard_map/ppermute | solution.py:295
  165.5 51.3 %collective-permute-start.22 = (bf16[2,256,1024]{2,1,0:T(8,128)(2,1)S(1)}, bf16[2,256,1024]{2,1,0:T(8,128)(2,1)S(1)}, u32[]{:S(2)}, u32[]{:S(2)}) collective-permute-start(bf16[2,256,1024]{2,1,0:T(8,128)(2,1)S(1)} %get-tuple-element.96), channel_id=1, source_target_pairs={{0,4},{1,5},{2,6},{3,7},{4,0},{5,1},{6,2},{7,3},{8,12},{9,13},{10,... | collective-permute-start | bytes 3145736 | tf_op jit(solution)/shard_map/ppermute | solution.py:295
  165.7 51.2 %collective-permute-start.21 = (bf16[2,256,1024]{2,1,0:T(8,128)(2,1)S(1)}, bf16[2,256,1024]{2,1,0:T(8,128)(2,1)S(1)}, u32[]{:S(2)}, u32[]{:S(2)}) collective-permute-start(bf16[2,256,1024]{2,1,0:T(8,128)(2,1)S(1)} %get-tuple-element.97), channel_id=1, source_target_pairs={{0,2},{1,3},{2,0},{3,1},{4,6},{5,7},{6,4},{7,5},{8,10},{9,11},{10,... | collective-permute-start | bytes 3145736 | tf_op jit(solution)/shard_map/ppermute | solution.py:295
  182.9 2.5 collective-permute-start.13
  185.5 31.3 %collective-permute-start.14 = (bf16[64,1024]{1,0:T(8,128)(2,1)S(1)}, bf16[64,1024]{1,0:T(8,128)(2,1)S(1)}, u32[]{:S(2)}, u32[]{:S(2)}) collective-permute-start(bf16[64,1024]{1,0:T(8,128)(2,1)S(1)} %dynamic-slice_convert_fusion), channel_id=1, source_target_pairs={{0,2},{1,3},{2,0},{3,1},{4,6},{5,7},{6,4},{7,5},{8,10},{9,11},{10,... | collective-permute-start | bytes 393224 | tf_op jit(solution)/shard_map/ppermute | solution.py:295
  201.2 17.6 %copy-start.1 = (bf16[2048,1024]{1,0:T(8,128)(2,1)}, bf16[2048,1024]{1,0:T(8,128)(2,1)S(1)}, u32[]{:S(2)}) copy-start(bf16[2048,1024]{1,0:T(8,128)(2,1)S(1)} %pieces.1) | copy-start | bytes 12582916
  219.1 32.4 %collective-permute-start.24 = (bf16[4,256,1024]{2,1,0:T(8,128)(2,1)}, bf16[4,256,1024]{2,1,0:T(8,128)(2,1)}, u32[]{:S(2)}, u32[]{:S(2)}) collective-permute-start(bf16[4,256,1024]{2,1,0:T(8,128)(2,1)} %pad_maximum_fusion.1), channel_id=1, source_target_pairs={{0,1},{1,0},{2,3},{3,2},{4,5},{5,4},{6,7},{7,6},{8,9},{9,8},{10,11... | collective-permute-start | bytes 6291464 | tf_op jit(solution)/shard_map/ppermute | solution.py:295
  219.6 5.1 %collective-permute-start.15 = (bf16[64,1024]{1,0:T(8,128)(2,1)S(1)}, bf16[64,1024]{1,0:T(8,128)(2,1)S(1)}, u32[]{:S(2)}, u32[]{:S(2)}) collective-permute-start(bf16[64,1024]{1,0:T(8,128)(2,1)S(1)} %fusion.11), channel_id=1, source_target_pairs={{0,4},{1,5},{2,6},{3,7},{4,0},{5,1},{6,2},{7,3},{8,12},{9,13},{10,... | collective-permute-start | bytes 393224 | tf_op jit(solution)/shard_map/ppermute | solution.py:295
  224.8 2.1 collective-permute-start.16
  232.4 19.1 %all-to-all-start.1 = ((bf16[8,256,128]{2,1,0:T(8,128)(2,1)}), bf16[8,256,128]{2,1,0:T(8,128)(2,1)S(1)}, u32[]{:S(2)}, u32[]{:S(2)}) async-start(bf16[8,256,128]{2,1,0:T(8,128)(2,1)} %get-tuple-element.71), calls=%async_computation.1 | async-start | bytes 1048576 | tf_op jit(solution)/shard_map/all_to_all | solution.py:292
  239.1 1.4 collective-permute-start.17
  241.1 2.8 collective-permute-start.18
  244.5 2.4 collective-permute-start.19
  247.6 3.3 collective-permute-start.20
  252.3 10.0 %copy-start.28 = (s32[128,1]{0,1:T(1,128)S(1)}, s32[128,1]{0,1:T(1,128)}, u32[]{:S(2)}) copy-start(s32[128,1]{0,1:T(1,128)} %param.15) | copy-start | bytes 1540
  252.3 10.4 %copy-start.6 = (bf16[2,256,1024]{2,1,0:T(8,128)(2,1)S(1)}, bf16[2,256,1024]{2,1,0:T(8,128)(2,1)}, u32[]{:S(2)}) copy-start(bf16[2,256,1024]{2,1,0:T(8,128)(2,1)} %copy-done.5) | copy-start | bytes 3145732
  252.3 10.4 %copy-start.8 = (bf16[2,256,1024]{2,1,0:T(8,128)(2,1)S(1)}, bf16[2,256,1024]{2,1,0:T(8,128)(2,1)}, u32[]{:S(2)}) copy-start(bf16[2,256,1024]{2,1,0:T(8,128)(2,1)} %copy-done.7) | copy-start | bytes 3145732
  252.3 10.4 %copy-start.10 = (bf16[2,256,1024]{2,1,0:T(8,128)(2,1)S(1)}, bf16[2,256,1024]{2,1,0:T(8,128)(2,1)}, u32[]{:S(2)}) copy-start(bf16[2,256,1024]{2,1,0:T(8,128)(2,1)} %copy-done.9) | copy-start | bytes 3145732
  252.3 102.5 %all-to-all-start.2 = ((bf16[16,128,1024]{2,1,0:T(8,128)(2,1)}), bf16[16,128,1024]{2,1,0:T(8,128)(2,1)}, u32[]{:S(2)}, u32[]{:S(2)}) async-start(bf16[16,128,1024]{2,1,0:T(8,128)(2,1)} %bitcast.105), calls=%async_computation.2 | async-start | bytes 8388608 | tf_op jit(solution)/shard_map/all_to_all | solution.py:284
  262.7 3.4 copy-start
  266.1 3.4 copy-start.2
  270.5 17.6 %copy-start.16 = (bf16[8,256,128]{2,1,0:T(8,128)(2,1)S(1)}, bf16[8,256,128]{2,1,0:T(8,128)(2,1)}, u32[]{:S(2)}) copy-start(bf16[8,256,128]{2,1,0:T(8,128)(2,1)} %copy-done.15) | copy-start | bytes 1572868
  (9 other events, 13.9 us)

commit v3 on v2

--- a/solution.py
+++ b/solution.py
@@ -43,7 +43,7 @@
 def narrow(units, ids, left, stacks, places, depth):
     rows, span = left.shape
     size = stacks[0].shape[1]
-    tile = min(rows, 256)
+    tile = min(rows, 512)
 
     def kernel(units_ref, ids_ref, left_ref, *refs):
         out_ref = refs[-1]
@@ -87,7 +87,7 @@
 def pieces_of(units, ids, lanes, stacks, places, depth):
     rows = lanes.shape[1]
     _, size, span = stacks[0].shape
-    tile = min(rows, 256)
+    tile = min(rows, 512)
 
     def kernel(units_ref, ids_ref, lanes_ref, *refs):
         out_ref, wide = refs[-2:]
@@ -210,25 +210,26 @@
 
 def join(back, scale, team):
     _, rows, cut = back.shape
-
-    def kernel(one_ref, two_ref, scale_ref, out_ref):
-        total = one_ref[0].astype(jnp.float32) + two_ref[0].astype(jnp.float32)
-        out_ref[...] = (scale_ref[...] * total).astype(out_ref.dtype)
+    tile = min(rows, 32)
+
+    def kernel(back_ref, scale_ref, out_ref):
+        for j in range(team):
+            total = back_ref[j].astype(jnp.float32) + back_ref[team + j].astype(jnp.float32)
+            out_ref[:, j * cut : (j + 1) * cut] = (scale_ref[...] * total).astype(out_ref.dtype)
 
     return pl.pallas_call(
         kernel,
-        grid=(team,),
+        grid=(rows // tile,),
         in_specs=[
-            pl.BlockSpec((1, rows, cut), lambda j: (j, 0, 0)),
-            pl.BlockSpec((1, rows, cut), lambda j: (team + j, 0, 0)),
-            pl.BlockSpec((rows, 1), lambda j: (0, 0)),
+            pl.BlockSpec((2 * team, tile, cut), lambda i: (0, i, 0)),
+            pl.BlockSpec((tile, 1), lambda i: (i, 0)),
         ],
-        out_specs=pl.BlockSpec((rows, cut), lambda j: (0, j)),
+        out_specs=pl.BlockSpec((tile, team * cut), lambda i: (i, 0)),
         out_shape=jax.ShapeDtypeStruct((rows, team * cut), back.dtype),
         compiler_params=ROOM,
         cost_estimate=cost(3 * rows * team * cut, 6 * rows * team * cut),
         name="join",
-    )(back, back, scale)
+    )(back, scale)
 
 
 def on_device(
@@ -328,11 +329,9 @@
         both = [jnp.where(even, mine, other), jnp.where(even, other, mine)]
         return jnp.concatenate(both, axis=1).astype(f32), beside
 
-    def double(array):
-        step = 1
-        while step < devices:
+    def sum_over(array, steps):
+        for step in steps:
             array = array + send(array, step)
-            step *= 2
         return array
 
     def columns_of(array, peer, size):
@@ -342,14 +341,21 @@
     id_block = jnp.pad(row_adapter[:, 0], (0, id_rows * out_cut - rows)).astype(bf16)
     id_block = jnp.pad(id_block.reshape(id_rows, out_cut), ((0, -id_rows % 16), (0, 0)))
     tall = rows + id_block.shape[0]
-    g_and_b = jnp.concatenate([grad_out, jnp.tile(id_block, (1, team)), up16], axis=0)
+    g_mine = jnp.concatenate([grad_out, jnp.tile(id_block, (1, team))], axis=0)
+    g_other = lax.ppermute(g_mine, "dp", [(i, (i + team) % devices) for i in range(devices)])
+    g_and_b = jnp.concatenate([g_mine, g_other, up16], axis=0)
     _, stacks = swap([columns_of(g_and_b, peer, out_cut) for peer in peers], ())
+    acts_send = jnp.tile(sliced(acts, team), (halves, 1, 1))
+    acts_send, early = lax.optimization_barrier((acts_send, stacks[:3]))
+    stacks = early + stacks[3:]
+    x_cut = to_all(acts_send).reshape(all_rows, cut)
     blocks = [stacks[stack][place] for stack, place in places]
-    mine = jnp.zeros((team * tall, out_cut), bf16)
+    mine = jnp.zeros((team, tall, out_cut), bf16)
+    theirs = mine
     for peer, block in zip(peers, blocks):
-        mine = lax.dynamic_update_slice_in_dim(mine, block[:tall], peer * tall, axis=0)
-    b_cut = jnp.stack([block[tall:] for block in blocks])
-    theirs = lax.ppermute(mine, "dp", [(i, (i + team) % devices) for i in range(devices)])
+        mine = lax.dynamic_update_slice_in_dim(mine, block[None, :tall], peer, axis=0)
+        theirs = lax.dynamic_update_slice_in_dim(theirs, block[None, tall : 2 * tall], peer, axis=0)
+    b_cut = jnp.stack([block[2 * tall :] for block in blocks])
     lower = me < team
     g_got = jnp.concatenate([jnp.where(lower, mine, theirs), jnp.where(lower, theirs, mine)], axis=0)
     g_got = g_got.reshape(devices, tall, out_cut)
@@ -368,9 +374,6 @@
     pair_scale = adapter_alpha_value / jnp.repeat(pair_rank, depth).astype(f32)
     half_scale = adapter_alpha_value / jnp.repeat(half_rank, depth).astype(f32)
 
-    acts_send = jnp.tile(sliced(acts, team), (halves, 1, 1))
-    acts_send, g_cut = lax.optimization_barrier((acts_send, g_cut))
-    x_cut = to_all(acts_send).reshape(all_rows, cut)
     alone = [(0, k) for k in range(team)]
     low_chip = chip_sum(narrow(units, ids, g_cut, [b_cut], alone, depth))
     low_chip, down_late = lax.optimization_barrier((low_chip, down_flat))
@@ -387,9 +390,11 @@
     hidden, piece = team_sum(hidden_chip, piece)
     up_parts, up_squares = gradient(half_unit, ids, hidden, g_cut, half_scale, team, depth)
     up_home = to_team(up_parts)
-    squares = double(jnp.sum(down_squares) + jnp.sum(up_squares))
+    far_steps = [2**k for k in range(2, devices.bit_length() - 1)][::-1]
+    squares = sum_over(jnp.sum(down_squares) + jnp.sum(up_squares), far_steps)
+    piece, squares, down_stacks, up_home = lax.optimization_barrier((piece, squares, down_stacks, up_home))
+    squares = sum_over(squares, [1, 2])
     clip_factor = jnp.minimum(1.0, clip_limit / (jnp.sqrt(squares) + norm_eps))
-    piece, _, down_stacks, up_home = lax.optimization_barrier((piece, squares, down_stacks, up_home))
     back = to_all(piece.reshape(devices, rows, cut))
     columns = jnp.stack(peers)
     down_new = update_slots(down_slots, down_first, down_second, down_stacks, down_places, columns, clip_factor)

time: 363 us -> 345 us (0.950)
  waiting for transfers between devices: 177 us -> 152 us
  starting transfers between devices: 48.8 us -> 59.9 us
  Pallas kernels: 76.4 us -> 70.9 us
    all_to_all x2, waiting for transfers between devices: 61.5 us -> 43 us  [to_all(): return lax.all_to_all(array, 'dp', split_axis=0, concat_axis=0, tiled=True)]
    ppermute x24, starting transfers between devices: 24.9 us -> 38.7 us  [send(): return lax.ppermute(array, 'dp', [(i, i ^ apart) for i in range(devices)])]
    ppermute x1, waiting for transfers between devices: 12.9 us -> 8.65 us  [on_device(): lax.ppermute(g_mine, 'dp', [(i, (i + team) % devices) for i in range(devi...]
    unnamed x67 -> x53, local copies, waits for them, and re-layouts: 13.8 us -> 13.8 us
  transfers between devices with their start and end apart: 28 -> 28, of which waited for: 14 -> 14; matrix products, arithmetic and copies ran while one was open for 8% -> 11% of each run, Pallas kernels for 19% -> 19%
where the time goes in v3:
time: 345 us; the launch traced here: 344 us
  waiting for transfers between devices  152 us (44%)
  Pallas kernels  70.9 us (21%)
  starting transfers between devices  59.9 us (17%)
  local copies, waits for them, and re-layouts  27.8 us (8%)
  other arithmetic  27.5 us (8%)
  between operations  5.26 us (2%)
    ppermute x24, waiting for transfers between devices, send(): return lax.ppermute(array, 'dp', [(i, i ^ apart) for i in range(devices)])  100 us
    all_to_all x2, waiting for transfers between devices, to_all(): return lax.all_to_all(array, 'dp', split_axis=0, concat_axis=0, tiled=True)  43 us
    ppermute x24, starting transfers between devices, send(): return lax.ppermute(array, 'dp', [(i, i ^ apart) for i in range(devices)])  38.7 us
    pallas_call x2, Pallas kernels, gradient(): pl.pallas_call(kernel, grid_spec=pltpu.PrefetchScalarGridSpec(num_scalar_...  19.3 us
    pallas_call x1, Pallas kernels, update_slots(): pl.pallas_call(kernel, grid_spec=pltpu.PrefetchScalarGridSpec(num_scalar_...  17.6 us
    pallas_call x2, Pallas kernels, narrow(): pl.pallas_call(kernel, grid_spec=pltpu.PrefetchScalarGridSpec(num_scalar_...  17.3 us
    all_to_all x2, starting transfers between devices, to_all(): return lax.all_to_all(array, 'dp', split_axis=0, concat_axis=0, tiled=True)  14.7 us
    unnamed x53, local copies, waits for them, and re-layouts  13.8 us
  transfers between devices with their start and end apart: 28, of which 14 were waited for; matrix products, arithmetic and copies ran while one was open for 11% of the time, Pallas kernels for 19%

profile of v3, /device:TPU:15, one launch (start us, length us, event | category | flops | bytes accessed | tf_op | source)
XLA Modules:
  0.0 343.6 jit_solution(5606902949232587056)
XLA Ops:
  2.4 2.4 collective-permute-start
  7.6 1.4 fusion.1
  9.0 8.7 %collective-permute-done = bf16[144,1024]{1,0:T(8,128)(2,1)S(1)} collective-permute-done((bf16[144,1024]{1,0:T(8,128)(2,1)S(1)}, bf16[144,1024]{1,0:T(8,128)(2,1)S(1)}, u32[]{:S(2)}, u32[]{:S(2)}) %collective-permute-start) | collective-permute-done | bytes 294944 | tf_op jit(solution)/shard_map/ppermute | solution.py:345
  20.0 1.2 collective-permute-done.1
  22.4 1.4 copy.30
  23.8 1.2 copy.25
  25.8 1.1 collective-permute-start.3
  27.6 1.3 collective-permute-start.4
  28.9 1.3 collective-permute-done.2
  30.2 2.5 tile.8
  32.9 7.9 %all-to-all-start = ((bf16[16,128,1024]{2,1,0:T(8,128)(2,1)}), bf16[16,128,1024]{2,1,0:T(8,128)(2,1)}, u32[]{:S(2)}, u32[]{:S(2)}) async-start(bf16[16,128,1024]{2,1,0:T(8,128)(2,1)} %bitcast.78), calls=%async_computation | async-start | bytes 8388608 | tf_op jit(solution)/shard_map/all_to_all | solution.py:285
  44.5 4.3 %narrow.2 = f32[64,2048]{1,0:T(8,128)S(1)} custom-call(s32[64]{0:T(128)S(1)} %reshape.296.units_ref, s32[1,2048]{1,0:T(1,128)S(1)} %fusion.13.ids_ref, bf16[2048,128]{1,0:T(8,128)(2,1)S(1)} %bitcast.76, bf16[8,256,128]{2,1,0:T(8,128)(2,1)S(1)} %slice_dynamic-update-slice_fusion.refs_0_), custom_call_target="tpu_custom_call" | custom-call | flops 262144 | bytes 128 | tf_op jit(solution)/shard_map/narrow/pallas_call | solution.py:63
  49.2 1.5 collective-permute-done.5
  50.8 5.9 %fusion.9 = (bf16[1,256,1024]{2,1,0:T(8,128)(2,1)}, bf16[1,256,1024]{2,1,0:T(8,128)(2,1)}, bf16[1,256,1024]{2,1,0:T(8,128)(2,1)}, bf16[1,256,1024]{2,1,0:T(8,128...) fusion(f32[256,8192]{1,0:T(8,128)} %bitcast.72, ...), kind=kLoop, calls=%fused_computation.32 | loop fusion | flops 2097152 | bytes 8388896 | tf_op jit(solution)/shard_map/stack | solution.py:301
  56.7 1.6 pad_maximum_fusion
  60.2 2.5 collective-permute-done.6.refs_1_
  64.2 1.2 collective-permute-start.10
  67.5 44.3 %collective-permute-done.10 = bf16[64,1024]{1,0:T(8,128)(2,1)S(1)} collective-permute-done((bf16[64,1024]{1,0:T(8,128)(2,1)S(1)}, bf16[64,1024]{1,0:T(8,128)(2,1)S(1)}, u32[]{:S(2)}, u32[]{:S(2)}) %collective-permute-start.10) | collective-permute-done | bytes 131104 | tf_op jit(solution)/shard_map/ppermute | solution.py:296
  112.0 1.1 pad_maximum_fusion.5
  113.0 3.5 %collective-permute-start.9 = (bf16[2,256,1024]{2,1,0:T(8,128)(2,1)}, bf16[2,256,1024]{2,1,0:T(8,128)(2,1)}, u32[]{:S(2)}, u32[]{:S(2)}) collective-permute-start(bf16[2,256,1024]{2,1,0:T(8,128)(2,1)} %pad_maximum_fusion.5), channel_id=1, source_target_pairs={{0,6},{1,7},{2,4},{3,5},{4,2},{5,3},{6,0},{7,1},{8,14},{9,15},{10,... | collective-permute-start | bytes 3145736 | tf_op jit(solution)/shard_map/ppermute | solution.py:296
  116.5 19.6 %collective-permute-done.11 = bf16[64,1024]{1,0:T(8,128)(2,1)S(1)} collective-permute-done((bf16[64,1024]{1,0:T(8,128)(2,1)S(1)}, bf16[64,1024]{1,0:T(8,128)(2,1)S(1)}, u32[]{:S(2)}, u32[]{:S(2)}) %collective-permute-start.11) | collective-permute-done | bytes 131104 | tf_op jit(solution)/shard_map/ppermute | solution.py:296
  136.1 1.3 collective-permute-start.12
  137.8 2.1 div.116.scale_ref
  139.9 1.2 copy-done.4
  141.1 13.9 %gradient.2 = (bf16[8,256,1024]{2,1,0:T(8,128)(2,1)S(1)}, f32[1,1024]{1,0:T(1,128)S(1)}) custom-call(s32[64]{0:T(128)S(1)} %reshape.302.units_ref, s32[1,2048]{1,0:T(1,128)S(1)} %fusion.13.ids_ref, f32[64,2048]{1,0:T(8,128)S(1)} %maximum_convert_fusion.lanes_ref, bf16[2048,1024]{1,0:T(8,128)(2,1)} %bitcast.21.right_ref.left_ref, f32[2048,1]{1,0:T(8,128)S(1)} %copy-done.4), custom_call_target="tpu_custom_call" | custom-call | flops 2097152 | bytes 2048 | tf_op jit(solution)/shard_map/gradient/pallas_call | solution.py:146
  155.8 2.5 collective-permute-start.19
  158.3 13.0 %narrow.3 = f32[64,2048]{1,0:T(8,128)S(1)} custom-call(s32[64]{0:T(128)S(1)} %reshape.296.units_ref, s32[1,2048]{1,0:T(1,128)S(1)} %fusion.13.ids_ref, bf16[2048,1024]{1,0:T(8,128)(2,1)} %bitcast.21.right_ref.left_ref, bf16[1,256,1024]{2,1,0:T(8,128)(2,1)S(1)} %copy-done.3, bf16[4,256,1024]{2,1,0:T(8,128)(2,1)S(1)} %collective-permute-done.6.refs_1_, ...), custom_call_target="tpu_custom_call" | custom-call | flops 2097152 | bytes 1024 | tf_op jit(solution)/shard_map/narrow/pallas_call | solution.py:63
  172.3 1.5 collective-permute-done.13
  173.9 2.0 collective-permute-start.14
  176.7 12.3 %pieces.1 = bf16[2048,1024]{1,0:T(8,128)(2,1)S(1)} custom-call(s32[64]{0:T(128)S(1)} %reshape.296.units_ref, s32[1,2048]{1,0:T(1,128)S(1)} %fusion.13.ids_ref, f32[64,2048]{1,0:T(8,128)S(1)} %maximum_convert_fusion.lanes_ref, bf16[1,256,1024]{2,1,0:T(8,128)(2,1)S(1)} %copy-done.3, bf16[4,256,1024]{2,1,0:T(8,128)(2,1)S(1)} %collective-permute-done.6.refs_1_, ...), custom_call_target="tpu_custom_call" | custom-call | flops 2097152 | bytes 1024 | tf_op jit(solution)/shard_map/pieces/pallas_call | solution.py:105
  189.0 17.9 %collective-permute-done.14 = bf16[64,1024]{1,0:T(8,128)(2,1)S(1)} collective-permute-done((bf16[64,1024]{1,0:T(8,128)(2,1)S(1)}, bf16[64,1024]{1,0:T(8,128)(2,1)S(1)}, u32[]{:S(2)}, u32[]{:S(2)}) %collective-permute-start.14) | collective-permute-done | bytes 131104 | tf_op jit(solution)/shard_map/ppermute | solution.py:296
  207.1 1.8 pad_maximum_fusion.1
  210.0 5.0 %collective-permute-done.15 = bf16[64,1024]{1,0:T(8,128)(2,1)S(1)} collective-permute-done((bf16[64,1024]{1,0:T(8,128)(2,1)S(1)}, bf16[64,1024]{1,0:T(8,128)(2,1)S(1)}, u32[]{:S(2)}, u32[]{:S(2)}) %collective-permute-start.15) | collective-permute-done | bytes 131104 | tf_op jit(solution)/shard_map/ppermute | solution.py:296
  216.0 1.1 div.117.scale_ref
  217.2 5.4 %gradient.3 = (bf16[8,256,128]{2,1,0:T(8,128)(2,1)}, f32[1,128]{1,0:T(1,128)S(1)}) custom-call(s32[64]{0:T(128)S(1)} %select_reduce_fusion.2.units_ref, s32[1,2048]{1,0:T(1,128)S(1)} %fusion.13.ids_ref, f32[64,2048]{1,0:T(8,128)S(1)} %maximum_convert_fusion.1.lanes_ref, bf16[2048,128]{1,0:T(8,128)(2,1)S(1)} %bitcast.77, f32[2048,1]{1,0:T(8,128)S(1)} %div.117.scale_ref), custom_call_target="tpu_custom_call" | custom-call | flops 262144 | bytes 256 | tf_op jit(solution)/shard_map/gradient/pallas_call | solution.py:146
  222.6 4.2 %all-to-all-start.1 = ((bf16[8,256,128]{2,1,0:T(8,128)(2,1)}), bf16[8,256,128]{2,1,0:T(8,128)(2,1)S(1)}, u32[]{:S(2)}, u32[]{:S(2)}) async-start(bf16[8,256,128]{2,1,0:T(8,128)(2,1)} %get-tuple-element.76), calls=%async_computation.1 | async-start | bytes 1048576 | tf_op jit(solution)/shard_map/all_to_all | solution.py:293
  229.3 3.1 collective-permute-start.17
  232.4 2.9 collective-permute-done.17
  236.7 1.6 collective-permute-done.18
  239.8 6.8 %all-to-all-start.2 = ((bf16[16,128,1024]{2,1,0:T(8,128)(2,1)}), bf16[16,128,1024]{2,1,0:T(8,128)(2,1)}, u32[]{:S(2)}, u32[]{:S(2)}) async-start(bf16[16,128,1024]{2,1,0:T(8,128)(2,1)} %bitcast.74), calls=%async_computation.2 | async-start | bytes 8388608 | tf_op jit(solution)/shard_map/all_to_all | solution.py:285
  246.9 1.4 collective-permute-start.23
  248.9 14.9 %collective-permute-start.24 = (f32[]{:T(128)}, f32[]{:T(128)}, u32[]{:S(2)}, u32[]{:S(2)}) collective-permute-start(f32[]{:T(128)} %add.250), channel_id=1, source_target_pairs={{0,2},{1,3},{2,0},{3,1},{4,6},{5,7},{6,4},{7,5},{8,10},{9,11},{10,... | collective-permute-start | bytes 20 | tf_op jit(solution)/shard_map/ppermute | solution.py:296
  265.5 3.4 copy-done
  268.9 3.4 copy-done.2
  273.3 17.6 %update.1 = (f32[256,8192]{1,0:T(8,128)}, f32[256,8192]{1,0:T(8,128)}, f32[256,8192]{1,0:T(8,128)}) custom-call(s32[8]{0:T(128)S(1)} %stack.124.columns_ref, f32[1,1]{1,0:T(1,128)} %bitcast.35.clip_ref, f32[256,8192]{1,0:T(8,128)S(1)} %bitcast.73, f32[256,8192]{1,0:T(8,128)S(1)} %bitcast.75, f32[256,8192]{1,0:T(8,128)} %bitcast.79, ...), custom_call_target="tpu_custom_call" | custom-call | flops 10240 | bytes 13312 | tf_op jit(solution)/shard_map/update/pallas_call | solution.py:194
  292.2 3.9 %multiply_subtract_fusion = (f32[8,32,1024]{2,1,0:T(8,128)}, f32[8,32,1024]{2,1,0:T(8,128)}, f32[8,32,1024]{2,1,0:T(8,128)}) fusion(f32[8,32,1024]{2,1,0:T(8,128)S(1)} %copy-done.12, f32[8,32,1024]{2,1,0:T(8,128)S(1)} %mul.142, f32[8,32,1024]{2,1,0:T(8,128)} %param.22, f32[8,32,1024]{2,1,0:T(8,128)} %param.23), kind=kLoop, calls=%fused_computation.13 | loop fusion | flops 3932160 | bytes 7340032 | tf_op jit(solution)/shard_map/sub | solution.py:24
  296.1 43.0 %all-to-all-done.2.back_ref = bf16[16,128,1024]{2,1,0:T(8,128)(2,1)} async-done(((bf16[16,128,1024]{2,1,0:T(8,128)(2,1)}), bf16[16,128,1024]{2,1,0:T(8,128)(2,1)}, u32[]{:S(2)}, u32[]{:S(2)}) %all-to-all-start.2) | async-done | bytes 4194336 | tf_op jit(solution)/shard_map/all_to_all | solution.py:285
  339.1 4.4 %join.1 = bf16[128,8192]{1,0:T(8,128)(2,1)} custom-call(bf16[16,128,1024]{2,1,0:T(8,128)(2,1)} %all-to-all-done.2.back_ref, f32[128,1]{1,0:T(8,128)S(1)} %copy.28.scale_ref), custom_call_target="tpu_custom_call" | custom-call | flops 768 | bytes 1536 | tf_op jit(solution)/shard_map/join/pallas_call | solution.py:220
  (161 shorter events, 30.9 us)
Async XLA Ops:
  0.6 17.0 %copy-start.19 = (bf16[128,1024]{1,0:T(8,128)(2,1)S(1)}, bf16[128,1024]{1,0:T(8,128)(2,1)}, u32[]{:S(2)}) copy-start(bf16[128,1024]{1,0:T(8,128)(2,1)} %param.14) | copy-start | bytes 786436
  2.4 15.3 %collective-permute-start = (bf16[144,1024]{1,0:T(8,128)(2,1)S(1)}, bf16[144,1024]{1,0:T(8,128)(2,1)S(1)}, u32[]{:S(2)}, u32[]{:S(2)}) collective-permute-start(bf16[144,1024]{1,0:T(8,128)(2,1)S(1)} %pad_maximum_fusion.8), channel_id=1, source_target_pairs={{0,8},{1,9},{2,10},{3,11},{4,12},{5,13},{6,14},{7,15},{8,0},{9,1},... | collective-permute-start | bytes 884744 | tf_op jit(solution)/shard_map/ppermute | solution.py:345
  17.8 4.7 %copy-start.13 = (bf16[128,8192]{1,0:T(8,128)(2,1)S(1)}, bf16[128,8192]{1,0:T(8,128)(2,1)}, u32[]{:S(2)}) copy-start(bf16[128,8192]{1,0:T(8,128)(2,1)} %param.13) | copy-start | bytes 6291460
  19.0 2.3 collective-permute-start.1
  22.0 8.2 %collective-permute-start.2 = (bf16[2,544,128]{2,1,0:T(8,128)(2,1)}, bf16[2,544,128]{2,1,0:T(8,128)(2,1)}, u32[]{:S(2)}, u32[]{:S(2)}) collective-permute-start(bf16[2,544,128]{2,1,0:T(8,128)(2,1)} %pad_maximum_fusion.9), channel_id=1, source_target_pairs={{0,2},{1,3},{2,0},{3,1},{4,6},{5,7},{6,4},{7,5},{8,10},{9,11},{10,... | collective-permute-start | bytes 835592 | tf_op jit(solution)/shard_map/ppermute | solution.py:296
  25.8 15.8 %collective-permute-start.3 = (bf16[2,544,128]{2,1,0:T(8,128)(2,1)}, bf16[2,544,128]{2,1,0:T(8,128)(2,1)S(1)}, u32[]{:S(2)}, u32[]{:S(2)}) collective-permute-start(bf16[2,544,128]{2,1,0:T(8,128)(2,1)} %pad_maximum_fusion.10), channel_id=1, source_target_pairs={{0,4},{1,5},{2,6},{3,7},{4,0},{5,1},{6,2},{7,3},{8,12},{9,13},{10,... | collective-permute-start | bytes 835592 | tf_op jit(solution)/shard_map/ppermute | solution.py:296
  27.6 14.0 %collective-permute-start.4 = (bf16[2,544,128]{2,1,0:T(8,128)(2,1)}, bf16[2,544,128]{2,1,0:T(8,128)(2,1)S(1)}, u32[]{:S(2)}, u32[]{:S(2)}) collective-permute-start(bf16[2,544,128]{2,1,0:T(8,128)(2,1)} %pad_maximum_fusion.11), channel_id=1, source_target_pairs={{0,6},{1,7},{2,4},{3,5},{4,2},{5,3},{6,0},{7,1},{8,14},{9,15},{10,... | collective-permute-start | bytes 835592 | tf_op jit(solution)/shard_map/ppermute | solution.py:296
  32.9 107.0 %all-to-all-start = ((bf16[16,128,1024]{2,1,0:T(8,128)(2,1)}), bf16[16,128,1024]{2,1,0:T(8,128)(2,1)}, u32[]{:S(2)}, u32[]{:S(2)}) async-start(bf16[16,128,1024]{2,1,0:T(8,128)(2,1)} %bitcast.78), calls=%async_computation | async-start | bytes 8388608 | tf_op jit(solution)/shard_map/all_to_all | solution.py:285
  48.8 2.0 collective-permute-start.5
  56.7 2.5 copy-start.20
  58.3 4.4 %collective-permute-start.6 = (bf16[4,256,1024]{2,1,0:T(8,128)(2,1)}, bf16[4,256,1024]{2,1,0:T(8,128)(2,1)S(1)}, u32[]{:S(2)}, u32[]{:S(2)}) collective-permute-start(bf16[4,256,1024]{2,1,0:T(8,128)(2,1)} %pad_maximum_fusion), channel_id=1, source_target_pairs={{0,1},{1,0},{2,3},{3,2},{4,5},{5,4},{6,7},{7,6},{8,9},{9,8},{10,11... | collective-permute-start | bytes 6291464 | tf_op jit(solution)/shard_map/ppermute | solution.py:296
  60.1 2.7 copy-start.18
  60.2 5.2 %copy-start.17 = (bf16[1,256,1024]{2,1,0:T(8,128)(2,1)S(1)}, bf16[1,256,1024]{2,1,0:T(8,128)(2,1)}, u32[]{:S(2)}) copy-start(bf16[1,256,1024]{2,1,0:T(8,128)(2,1)} %get-tuple-element.92) | copy-start | bytes 1572868
  62.8 49.1 %copy-start.16 = (bf16[1,256,1024]{2,1,0:T(8,128)(2,1)S(1)}, bf16[1,256,1024]{2,1,0:T(8,128)(2,1)}, u32[]{:S(2)}) copy-start(bf16[1,256,1024]{2,1,0:T(8,128)(2,1)} %get-tuple-element.91) | copy-start | bytes 1572868
  63.9 92.0 %collective-permute-start.7 = (bf16[2,256,1024]{2,1,0:T(8,128)(2,1)}, bf16[2,256,1024]{2,1,0:T(8,128)(2,1)}, u32[]{:S(2)}, u32[]{:S(2)}) collective-permute-start(bf16[2,256,1024]{2,1,0:T(8,128)(2,1)} %pad_maximum_fusion.3), channel_id=1, source_target_pairs={{0,2},{1,3},{2,0},{3,1},{4,6},{5,7},{6,4},{7,5},{8,10},{9,11},{10,... | collective-permute-start | bytes 3145736 | tf_op jit(solution)/shard_map/ppermute | solution.py:296
  64.2 47.7 %collective-permute-start.10 = (bf16[64,1024]{1,0:T(8,128)(2,1)S(1)}, bf16[64,1024]{1,0:T(8,128)(2,1)S(1)}, u32[]{:S(2)}, u32[]{:S(2)}) collective-permute-start(bf16[64,1024]{1,0:T(8,128)(2,1)S(1)} %dynamic-slice_convert_fusion.1), channel_id=1, source_target_pairs={{0,2},{1,3},{2,0},{3,1},{4,6},{5,7},{6,4},{7,5},{8,10},{9,11},{10,... | collective-permute-start | bytes 393224 | tf_op jit(solution)/shard_map/ppermute | solution.py:296
  66.5 91.8 %collective-permute-start.8 = (bf16[2,256,1024]{2,1,0:T(8,128)(2,1)}, bf16[2,256,1024]{2,1,0:T(8,128)(2,1)}, u32[]{:S(2)}, u32[]{:S(2)}) collective-permute-start(bf16[2,256,1024]{2,1,0:T(8,128)(2,1)} %pad_maximum_fusion.4), channel_id=1, source_target_pairs={{0,4},{1,5},{2,6},{3,7},{4,0},{5,1},{6,2},{7,3},{8,12},{9,13},{10,... | collective-permute-start | bytes 3145736 | tf_op jit(solution)/shard_map/ppermute | solution.py:296
  111.9 24.2 %collective-permute-start.11 = (bf16[64,1024]{1,0:T(8,128)(2,1)S(1)}, bf16[64,1024]{1,0:T(8,128)(2,1)S(1)}, u32[]{:S(2)}, u32[]{:S(2)}) collective-permute-start(bf16[64,1024]{1,0:T(8,128)(2,1)S(1)} %fusion.10), channel_id=1, source_target_pairs={{0,4},{1,5},{2,6},{3,7},{4,0},{5,1},{6,2},{7,3},{8,12},{9,13},{10,... | collective-permute-start | bytes 393224 | tf_op jit(solution)/shard_map/ppermute | solution.py:296
  113.0 45.3 %collective-permute-start.9 = (bf16[2,256,1024]{2,1,0:T(8,128)(2,1)}, bf16[2,256,1024]{2,1,0:T(8,128)(2,1)}, u32[]{:S(2)}, u32[]{:S(2)}) collective-permute-start(bf16[2,256,1024]{2,1,0:T(8,128)(2,1)} %pad_maximum_fusion.5), channel_id=1, source_target_pairs={{0,6},{1,7},{2,4},{3,5},{4,2},{5,3},{6,0},{7,1},{8,14},{9,15},{10,... | collective-permute-start | bytes 3145736 | tf_op jit(solution)/shard_map/ppermute | solution.py:296
  136.1 3.7 %collective-permute-start.12 = (bf16[64,1024]{1,0:T(8,128)(2,1)S(1)}, bf16[64,1024]{1,0:T(8,128)(2,1)S(1)}, u32[]{:S(2)}, u32[]{:S(2)}) collective-permute-start(bf16[64,1024]{1,0:T(8,128)(2,1)S(1)} %add_convert_fusion.1), channel_id=1, source_target_pairs={{0,1},{1,0},{2,3},{3,2},{4,5},{5,4},{6,7},{7,6},{8,9},{9,8},{10,11... | collective-permute-start | bytes 393224 | tf_op jit(solution)/shard_map/ppermute | solution.py:296
  139.9 1.2 copy-start.4
  155.0 3.3 copy-start.3
  155.6 51.4 %collective-permute-start.21 = (bf16[2,256,1024]{2,1,0:T(8,128)(2,1)S(1)}, bf16[2,256,1024]{2,1,0:T(8,128)(2,1)S(1)}, u32[]{:S(2)}, u32[]{:S(2)}) collective-permute-start(bf16[2,256,1024]{2,1,0:T(8,128)(2,1)S(1)} %get-tuple-element.101), channel_id=1, source_target_pairs={{0,6},{1,7},{2,4},{3,5},{4,2},{5,3},{6,0},{7,1},{8,14},{9,15},{10,... | collective-permute-start | bytes 3145736 | tf_op jit(solution)/shard_map/ppermute | solution.py:296
  155.7 51.3 %collective-permute-start.20 = (bf16[2,256,1024]{2,1,0:T(8,128)(2,1)S(1)}, bf16[2,256,1024]{2,1,0:T(8,128)(2,1)S(1)}, u32[]{:S(2)}, u32[]{:S(2)}) collective-permute-start(bf16[2,256,1024]{2,1,0:T(8,128)(2,1)S(1)} %get-tuple-element.102), channel_id=1, source_target_pairs={{0,4},{1,5},{2,6},{3,7},{4,0},{5,1},{6,2},{7,3},{8,12},{9,13},{10,... | collective-permute-start | bytes 3145736 | tf_op jit(solution)/shard_map/ppermute | solution.py:296
  155.8 51.2 %collective-permute-start.19 = (bf16[2,256,1024]{2,1,0:T(8,128)(2,1)S(1)}, bf16[2,256,1024]{2,1,0:T(8,128)(2,1)S(1)}, u32[]{:S(2)}, u32[]{:S(2)}) collective-permute-start(bf16[2,256,1024]{2,1,0:T(8,128)(2,1)S(1)} %get-tuple-element.103), channel_id=1, source_target_pairs={{0,2},{1,3},{2,0},{3,1},{4,6},{5,7},{6,4},{7,5},{8,10},{9,11},{10,... | collective-permute-start | bytes 3145736 | tf_op jit(solution)/shard_map/ppermute | solution.py:296
  171.3 2.5 collective-permute-start.13
  173.9 33.1 %collective-permute-start.14 = (bf16[64,1024]{1,0:T(8,128)(2,1)S(1)}, bf16[64,1024]{1,0:T(8,128)(2,1)S(1)}, u32[]{:S(2)}, u32[]{:S(2)}) collective-permute-start(bf16[64,1024]{1,0:T(8,128)(2,1)S(1)} %dynamic-slice_convert_fusion), channel_id=1, source_target_pairs={{0,2},{1,3},{2,0},{3,1},{4,6},{5,7},{6,4},{7,5},{8,10},{9,11},{10,... | collective-permute-start | bytes 393224 | tf_op jit(solution)/shard_map/ppermute | solution.py:296
  189.0 20.0 %copy-start.1 = (bf16[2048,1024]{1,0:T(8,128)(2,1)}, bf16[2048,1024]{1,0:T(8,128)(2,1)S(1)}, u32[]{:S(2)}) copy-start(bf16[2048,1024]{1,0:T(8,128)(2,1)S(1)} %pieces.1) | copy-start | bytes 12582916
  207.0 2.0 copy-start.5
  207.0 2.0 copy-start.7
  207.1 2.2 copy-start.9
  209.3 29.7 %collective-permute-start.22 = (bf16[4,256,1024]{2,1,0:T(8,128)(2,1)}, bf16[4,256,1024]{2,1,0:T(8,128)(2,1)}, u32[]{:S(2)}, u32[]{:S(2)}) collective-permute-start(bf16[4,256,1024]{2,1,0:T(8,128)(2,1)} %pad_maximum_fusion.1), channel_id=1, source_target_pairs={{0,1},{1,0},{2,3},{3,2},{4,5},{5,4},{6,7},{7,6},{8,9},{9,8},{10,11... | collective-permute-start | bytes 6291464 | tf_op jit(solution)/shard_map/ppermute | solution.py:296
  209.8 5.1 %collective-permute-start.15 = (bf16[64,1024]{1,0:T(8,128)(2,1)S(1)}, bf16[64,1024]{1,0:T(8,128)(2,1)S(1)}, u32[]{:S(2)}, u32[]{:S(2)}) collective-permute-start(bf16[64,1024]{1,0:T(8,128)(2,1)S(1)} %fusion.11), channel_id=1, source_target_pairs={{0,4},{1,5},{2,6},{3,7},{4,0},{5,1},{6,2},{7,3},{8,12},{9,13},{10,... | collective-permute-start | bytes 393224 | tf_op jit(solution)/shard_map/ppermute | solution.py:296
  215.0 2.1 collective-permute-start.16
  222.6 16.4 %all-to-all-start.1 = ((bf16[8,256,128]{2,1,0:T(8,128)(2,1)}), bf16[8,256,128]{2,1,0:T(8,128)(2,1)S(1)}, u32[]{:S(2)}, u32[]{:S(2)}) async-start(bf16[8,256,128]{2,1,0:T(8,128)(2,1)} %get-tuple-element.76), calls=%async_computation.1 | async-start | bytes 1048576 | tf_op jit(solution)/shard_map/all_to_all | solution.py:293
  229.3 6.0 %collective-permute-start.17 = (f32[]{:T(128)}, f32[]{:T(128)}, u32[]{:S(2)}, u32[]{:S(2)}) collective-permute-start(f32[]{:T(128)} %add.247), channel_id=1, source_target_pairs={{0,8},{1,9},{2,10},{3,11},{4,12},{5,13},{6,14},{7,15},{8,0},{9,1},... | collective-permute-start | bytes 20 | tf_op jit(solution)/shard_map/ppermute | solution.py:296
  236.0 2.4 collective-permute-start.18
  239.8 6.8 %copy-start.21 = (s32[128,1]{0,1:T(1,128)S(1)}, s32[128,1]{0,1:T(1,128)}, u32[]{:S(2)}) copy-start(s32[128,1]{0,1:T(1,128)} %param.15) | copy-start | bytes 1540
  239.8 25.7 %copy-start.6 = (bf16[2,256,1024]{2,1,0:T(8,128)(2,1)S(1)}, bf16[2,256,1024]{2,1,0:T(8,128)(2,1)}, u32[]{:S(2)}) copy-start(bf16[2,256,1024]{2,1,0:T(8,128)(2,1)} %copy-done.5) | copy-start | bytes 3145732
  239.8 25.7 %copy-start.8 = (bf16[2,256,1024]{2,1,0:T(8,128)(2,1)S(1)}, bf16[2,256,1024]{2,1,0:T(8,128)(2,1)}, u32[]{:S(2)}) copy-start(bf16[2,256,1024]{2,1,0:T(8,128)(2,1)} %copy-done.7) | copy-start | bytes 3145732
  239.8 25.7 %copy-start.10 = (bf16[2,256,1024]{2,1,0:T(8,128)(2,1)S(1)}, bf16[2,256,1024]{2,1,0:T(8,128)(2,1)}, u32[]{:S(2)}) copy-start(bf16[2,256,1024]{2,1,0:T(8,128)(2,1)} %copy-done.9) | copy-start | bytes 3145732
  239.8 99.3 %all-to-all-start.2 = ((bf16[16,128,1024]{2,1,0:T(8,128)(2,1)}), bf16[16,128,1024]{2,1,0:T(8,128)(2,1)}, u32[]{:S(2)}, u32[]{:S(2)}) async-start(bf16[16,128,1024]{2,1,0:T(8,128)(2,1)} %bitcast.74), calls=%async_computation.2 | async-start | bytes 8388608 | tf_op jit(solution)/shard_map/all_to_all | solution.py:285
  246.9 1.4 collective-permute-start.23
  248.9 15.9 %collective-permute-start.24 = (f32[]{:T(128)}, f32[]{:T(128)}, u32[]{:S(2)}, u32[]{:S(2)}) collective-permute-start(f32[]{:T(128)} %add.250), channel_id=1, source_target_pairs={{0,2},{1,3},{2,0},{3,1},{4,6},{5,7},{6,4},{7,5},{8,10},{9,11},{10,... | collective-permute-start | bytes 20 | tf_op jit(solution)/shard_map/ppermute | solution.py:296
  265.5 3.4 copy-start
  268.9 3.4 copy-start.2
  273.3 17.6 %copy-start.15 = (bf16[8,256,128]{2,1,0:T(8,128)(2,1)S(1)}, bf16[8,256,128]{2,1,0:T(8,128)(2,1)}, u32[]{:S(2)}) copy-start(bf16[8,256,128]{2,1,0:T(8,128)(2,1)} %copy-done.14) | copy-start | bytes 1572868
  291.0 1.2 copy-start.12
  (2 other events, 1.8 us)

commit v4 on v3

--- a/solution.py
+++ b/solution.py
@@ -124,39 +124,41 @@
 
 def gradient(units, ids, lanes, right, scale, parts, depth):
     rows, span = right.shape
-    cols = scale.shape[0]
+    cols = scale.shape[0] * depth
     size = cols // parts
 
-    def kernel(units_ref, ids_ref, lanes_ref, right_ref, scale_ref, out_ref, square_ref, wide):
+    def kernel(units_ref, scale_ref, ids_ref, lanes_ref, right_ref, out_ref, square_ref, wide):
         b = pl.program_id(0)
         twice = 2 * ids_ref[...]
         for u in range(size // depth):
             wide[u * depth : (u + 1) * depth, :] = spread(
                 units_ref[b * (size // depth) + u], twice, lanes_ref[...], depth
             )
-        grad = scale_ref[...] * jnp.dot(wide[...], right_ref[...], preferred_element_type=jnp.float32)
-        out_ref[0] = grad.astype(out_ref.dtype)
+        total = jnp.dot(wide[...], right_ref[...], preferred_element_type=jnp.float32)
 
         @pl.when(b == 0)
         def _():
             square_ref[...] = jnp.zeros_like(square_ref)
 
-        square_ref[...] += jnp.sum(grad * grad, axis=0, keepdims=True)
+        for u in range(size // depth):
+            part = slice(u * depth, (u + 1) * depth)
+            grad = scale_ref[b * (size // depth) + u] * total[part]
+            out_ref[0, part, :] = grad.astype(out_ref.dtype)
+            square_ref[...] += jnp.sum(grad * grad, axis=0, keepdims=True)
 
     return pl.pallas_call(
         kernel,
         grid_spec=pltpu.PrefetchScalarGridSpec(
-            num_scalar_prefetch=1,
+            num_scalar_prefetch=2,
             grid=(parts,),
             in_specs=[
                 whole(ids),
                 whole(lanes),
                 whole(right),
-                pl.BlockSpec((size, 1), lambda i, _: (i, 0)),
             ],
             out_specs=[
-                pl.BlockSpec((1, size, span), lambda i, _: (i, 0, 0)),
-                pl.BlockSpec((1, span), lambda i, _: (0, 0)),
+                pl.BlockSpec((1, size, span), lambda i, *_: (i, 0, 0)),
+                pl.BlockSpec((1, span), lambda i, *_: (0, 0)),
             ],
             scratch_shapes=[pltpu.VMEM((size, rows), jnp.bfloat16)],
         ),
@@ -167,7 +169,7 @@
         compiler_params=ROOM,
         cost_estimate=cost(2 * rows * cols * span, 2 * (rows + cols) * span),
         name="gradient",
-    )(units, ids, lanes, right, scale.reshape(cols, 1))
+    )(units, scale, ids, lanes, right)
 
 
 def update_slots(params, moment, second, stacks, places, columns, clip_factor):
@@ -343,11 +345,10 @@
     tall = rows + id_block.shape[0]
     g_mine = jnp.concatenate([grad_out, jnp.tile(id_block, (1, team))], axis=0)
     g_other = lax.ppermute(g_mine, "dp", [(i, (i + team) % devices) for i in range(devices)])
+    acts_send = jnp.tile(sliced(acts, team), (halves, 1, 1))
+    g_other, acts_send = lax.optimization_barrier((g_other, acts_send))
     g_and_b = jnp.concatenate([g_mine, g_other, up16], axis=0)
-    _, stacks = swap([columns_of(g_and_b, peer, out_cut) for peer in peers], ())
-    acts_send = jnp.tile(sliced(acts, team), (halves, 1, 1))
-    acts_send, early = lax.optimization_barrier((acts_send, stacks[:3]))
-    stacks = early + stacks[3:]
+    acts_send, stacks = swap([columns_of(g_and_b, peer, out_cut) for peer in peers], acts_send, True)
     x_cut = to_all(acts_send).reshape(all_rows, cut)
     blocks = [stacks[stack][place] for stack, place in places]
     mine = jnp.zeros((team, tall, out_cut), bf16)
@@ -371,8 +372,8 @@
     pair_seats = jnp.arange(team, dtype=jnp.int32) ^ seat
     pair_units = jnp.take(half_unit.reshape(team, own), pair_seats, axis=0).reshape(-1)
     pair_rank = jnp.take(half_rank.reshape(team, own), pair_seats, axis=0).reshape(-1)
-    pair_scale = adapter_alpha_value / jnp.repeat(pair_rank, depth).astype(f32)
-    half_scale = adapter_alpha_value / jnp.repeat(half_rank, depth).astype(f32)
+    pair_scale = adapter_alpha_value / pair_rank.astype(f32)
+    half_scale = adapter_alpha_value / half_rank.astype(f32)
 
     alone = [(0, k) for k in range(team)]
     low_chip = chip_sum(narrow(units, ids, g_cut, [b_cut], alone, depth))
@@ -391,7 +392,7 @@
     up_parts, up_squares = gradient(half_unit, ids, hidden, g_cut, half_scale, team, depth)
     up_home = to_team(up_parts)
     far_steps = [2**k for k in range(2, devices.bit_length() - 1)][::-1]
-    squares = sum_over(jnp.sum(down_squares) + jnp.sum(up_squares), far_steps)
+    squares = sum_over(jnp.sum(jnp.concatenate([down_squares, up_squares], axis=1)), far_steps)
     piece, squares, down_stacks, up_home = lax.optimization_barrier((piece, squares, down_stacks, up_home))
     squares = sum_over(squares, [1, 2])
     clip_factor = jnp.minimum(1.0, clip_limit / (jnp.sqrt(squares) + norm_eps))

time: 345 us -> 344 us (level)
  waiting for transfers between devices: 152 us -> 136 us
  starting transfers between devices: 59.9 us -> 74.7 us
    ppermute x24, starting transfers between devices: 38.7 us -> 53.5 us  [send(): return lax.ppermute(array, 'dp', [(i, i ^ apart) for i in range(devices)])]
    ppermute x24, waiting for transfers between devices: 100 us -> 87.7 us  [send(): return lax.ppermute(array, 'dp', [(i, i ^ apart) for i in range(devices)])]
    unnamed x53 -> x56, local copies, waits for them, and re-layouts: 13.8 us -> 16.6 us
    another operation x7 -> x6, other arithmetic: 11.3 us -> 10.6 us  [swap(): pairs = [jnp.stack([blocks[k], got[k]]) for k in range(1, count)]]
  transfers between devices with their start and end apart: 28 -> 28, of which waited for: 14 -> 17; matrix products, arithmetic and copies ran while one was open for 11% -> 10% of each run, Pallas kernels for 19% -> 19%
where the time goes in v4:
time: 344 us; the launch traced here: 343 us
  waiting for transfers between devices  136 us (40%)
  starting transfers between devices  74.7 us (22%)
  Pallas kernels  70.9 us (21%)
  local copies, waits for them, and re-layouts  29.9 us (9%)
  other arithmetic  26.4 us (8%)
  between operations  5.31 us (2%)
    ppermute x24, waiting for transfers between devices, send(): return lax.ppermute(array, 'dp', [(i, i ^ apart) for i in range(devices)])  87.7 us
    ppermute x24, starting transfers between devices, send(): return lax.ppermute(array, 'dp', [(i, i ^ apart) for i in range(devices)])  53.5 us
    all_to_all x2, waiting for transfers between devices, to_all(): return lax.all_to_all(array, 'dp', split_axis=0, concat_axis=0, tiled=True)  42.2 us
    pallas_call x2, Pallas kernels, gradient(): pl.pallas_call(kernel, grid_spec=pltpu.PrefetchScalarGridSpec(num_scalar_...  20 us
    pallas_call x2, Pallas kernels, narrow(): pl.pallas_call(kernel, grid_spec=pltpu.PrefetchScalarGridSpec(num_scalar_...  17.4 us
    pallas_call x1, Pallas kernels, update_slots(): pl.pallas_call(kernel, grid_spec=pltpu.PrefetchScalarGridSpec(num_scalar_...  16.8 us
    unnamed x56, local copies, waits for them, and re-layouts  16.6 us
    all_to_all x2, starting transfers between devices, to_all(): return lax.all_to_all(array, 'dp', split_axis=0, concat_axis=0, tiled=True)  14 us
  transfers between devices with their start and end apart: 28, of which 17 were waited for; matrix products, arithmetic and copies ran while one was open for 10% of the time, Pallas kernels for 19%

profile of v4, /device:TPU:15, one launch (start us, length us, event | category | flops | bytes accessed | tf_op | source)
XLA Modules:
  0.0 343.0 jit_solution(14445373962355600153)
XLA Ops:
  1.3 1.7 pad_maximum_fusion.8
  3.0 2.3 collective-permute-start
  8.3 3.0 copy.49
  11.3 1.2 copy.37
  12.7 5.9 %collective-permute-done = bf16[144,1024]{1,0:T(8,128)(2,1)S(1)} collective-permute-done((bf16[144,1024]{1,0:T(8,128)(2,1)}, bf16[144,1024]{1,0:T(8,128)(2,1)S(1)}, u32[]{:S(2)}, u32[]{:S(2)}) %collective-permute-start) | collective-permute-done | bytes 294944 | tf_op jit(solution)/shard_map/ppermute | solution.py:347
  18.6 2.6 tile.20
  27.8 1.5 collective-permute-start.4
  29.3 7.8 %all-to-all-start = ((bf16[16,128,1024]{2,1,0:T(8,128)(2,1)}), bf16[16,128,1024]{2,1,0:T(8,128)(2,1)}, u32[]{:S(2)}, u32[]{:S(2)}) async-start(bf16[16,128,1024]{2,1,0:T(8,128)(2,1)} %bitcast.92), calls=%async_computation | async-start | bytes 8388608 | tf_op jit(solution)/shard_map/all_to_all | solution.py:287
  37.9 9.9 %collective-permute-done.4 = bf16[2,544,128]{2,1,0:T(8,128)(2,1)S(1)} collective-permute-done((bf16[2,544,128]{2,1,0:T(8,128)(2,1)}, bf16[2,544,128]{2,1,0:T(8,128)(2,1)S(1)}, u32[]{:S(2)}, u32[]{:S(2)}) %collective-permute-start.4) | collective-permute-done | bytes 278560 | tf_op jit(solution)/shard_map/ppermute | solution.py:298
  48.8 2.4 dynamic_update_slice.63
  53.5 4.4 %narrow.2 = f32[64,2048]{1,0:T(8,128)S(1)} custom-call(s32[64]{0:T(128)S(1)} %reshape.254.units_ref, s32[1,2048]{1,0:T(1,128)S(1)} %bitcast.87, bf16[2048,128]{1,0:T(8,128)(2,1)S(1)} %bitcast.85, bf16[8,256,128]{2,1,0:T(8,128)(2,1)S(1)} %slice_dynamic-update-slice_fusion.refs_0_), custom_call_target="tpu_custom_call" | custom-call | flops 262144 | bytes 128 | tf_op jit(solution)/shard_map/narrow/pallas_call | solution.py:63
  57.8 3.6 %collective-permute-start.5 = (f32[64,2048]{1,0:T(8,128)S(1)}, f32[64,2048]{1,0:T(8,128)S(1)}, u32[]{:S(2)}, u32[]{:S(2)}) collective-permute-start(f32[64,2048]{1,0:T(8,128)S(1)} %narrow.2), channel_id=1, source_target_pairs={{0,1},{1,0},{2,3},{3,2},{4,5},{5,4},{6,7},{7,6},{8,9},{9,8},{10,11... | collective-permute-start | bytes 1572872 | tf_op jit(solution)/shard_map/ppermute | solution.py:298
  61.4 1.5 collective-permute-done.5
  63.0 5.8 %fusion.9 = (bf16[1,256,1024]{2,1,0:T(8,128)(2,1)}, bf16[1,256,1024]{2,1,0:T(8,128)(2,1)}, bf16[1,256,1024]{2,1,0:T(8,128)(2,1)}, bf16[1,256,1024]{2,1,0:T(8,128...) fusion(f32[256,8192]{1,0:T(8,128)} %bitcast.81, ...), kind=kLoop, calls=%fused_computation.32 | loop fusion | flops 2097152 | bytes 8388896 | tf_op jit(solution)/shard_map/stack | solution.py:303
  68.8 1.6 pad_maximum_fusion
  72.3 2.5 collective-permute-done.6.refs_1_
  76.0 7.7 %collective-permute-start.7 = (bf16[2,256,1024]{2,1,0:T(8,128)(2,1)}, bf16[2,256,1024]{2,1,0:T(8,128)(2,1)}, u32[]{:S(2)}, u32[]{:S(2)}) collective-permute-start(bf16[2,256,1024]{2,1,0:T(8,128)(2,1)} %pad_maximum_fusion.3), channel_id=1, source_target_pairs={{0,2},{1,3},{2,0},{3,1},{4,6},{5,7},{6,4},{7,5},{8,10},{9,11},{10,... | collective-permute-start | bytes 3145736 | tf_op jit(solution)/shard_map/ppermute | solution.py:298
  84.8 3.3 collective-permute-start.8
  88.1 37.9 %collective-permute-done.10 = bf16[64,1024]{1,0:T(8,128)(2,1)S(1)} collective-permute-done((bf16[64,1024]{1,0:T(8,128)(2,1)S(1)}, bf16[64,1024]{1,0:T(8,128)(2,1)S(1)}, u32[]{:S(2)}, u32[]{:S(2)}) %collective-permute-start.10) | collective-permute-done | bytes 131104 | tf_op jit(solution)/shard_map/ppermute | solution.py:298
  128.2 2.5 collective-permute-start.9
  130.7 4.0 %collective-permute-done.11 = bf16[64,1024]{1,0:T(8,128)(2,1)S(1)} collective-permute-done((bf16[64,1024]{1,0:T(8,128)(2,1)S(1)}, bf16[64,1024]{1,0:T(8,128)(2,1)S(1)}, u32[]{:S(2)}, u32[]{:S(2)}) %collective-permute-start.11) | collective-permute-done | bytes 131104 | tf_op jit(solution)/shard_map/ppermute | solution.py:298
  134.8 2.7 collective-permute-start.12
  138.6 14.5 %gradient.2 = (bf16[8,256,1024]{2,1,0:T(8,128)(2,1)S(1)}, f32[1,1024]{1,0:T(1,128)S(1)}) custom-call(s32[64]{0:T(128)S(1)} %reshape.260.units_ref, f32[64]{0:T(128)S(1)} %div.80.scale_ref, s32[1,2048]{1,0:T(1,128)S(1)} %bitcast.88, f32[64,2048]{1,0:T(8,128)S(1)} %maximum_convert_fusion.lanes_ref, bf16[2048,1024]{1,0:T(8,128)(2,1)} %bitcast.22.right_ref.left_ref), custom_call_target="tpu_custom_call" | custom-call | flops 2097152 | bytes 2048 | tf_op jit(solution)/shard_map/gradient/pallas_call | solution.py:149
  154.9 1.4 collective-permute-start.19
  157.1 13.0 %narrow.3 = f32[64,2048]{1,0:T(8,128)S(1)} custom-call(s32[64]{0:T(128)S(1)} %reshape.254.units_ref, s32[1,2048]{1,0:T(1,128)S(1)} %bitcast.89, bf16[2048,1024]{1,0:T(8,128)(2,1)} %bitcast.22.right_ref.left_ref, bf16[1,256,1024]{2,1,0:T(8,128)(2,1)S(1)} %copy-done.3, bf16[4,256,1024]{2,1,0:T(8,128)(2,1)S(1)} %collective-permute-done.6.refs_1_, ...), custom_call_target="tpu_custom_call" | custom-call | flops 2097152 | bytes 1024 | tf_op jit(solution)/shard_map/narrow/pallas_call | solution.py:63
  170.1 2.4 collective-permute-start.13
  172.5 1.5 collective-permute-done.13
  174.1 1.9 collective-permute-start.14
  176.9 12.3 %pieces.1 = bf16[2048,1024]{1,0:T(8,128)(2,1)S(1)} custom-call(s32[64]{0:T(128)S(1)} %reshape.254.units_ref, s32[1,2048]{1,0:T(1,128)S(1)} %bitcast.90, f32[64,2048]{1,0:T(8,128)S(1)} %maximum_convert_fusion.lanes_ref, bf16[1,256,1024]{2,1,0:T(8,128)(2,1)S(1)} %copy-done.3, bf16[4,256,1024]{2,1,0:T(8,128)(2,1)S(1)} %collective-permute-done.6.refs_1_, ...), custom_call_target="tpu_custom_call" | custom-call | flops 2097152 | bytes 1024 | tf_op jit(solution)/shard_map/pieces/pallas_call | solution.py:105
  189.2 16.6 %collective-permute-done.14 = bf16[64,1024]{1,0:T(8,128)(2,1)S(1)} collective-permute-done((bf16[64,1024]{1,0:T(8,128)(2,1)S(1)}, bf16[64,1024]{1,0:T(8,128)(2,1)S(1)}, u32[]{:S(2)}, u32[]{:S(2)}) %collective-permute-start.14) | collective-permute-done | bytes 131104 | tf_op jit(solution)/shard_map/ppermute | solution.py:298
  205.9 1.8 pad_maximum_fusion.1
  209.4 4.4 %collective-permute-done.15 = bf16[64,1024]{1,0:T(8,128)(2,1)S(1)} collective-permute-done((bf16[64,1024]{1,0:T(8,128)(2,1)S(1)}, bf16[64,1024]{1,0:T(8,128)(2,1)S(1)}, u32[]{:S(2)}, u32[]{:S(2)}) %collective-permute-start.15) | collective-permute-done | bytes 131104 | tf_op jit(solution)/shard_map/ppermute | solution.py:298
  215.8 5.5 %gradient.3 = (bf16[8,256,128]{2,1,0:T(8,128)(2,1)}, f32[1,128]{1,0:T(1,128)S(1)}) custom-call(s32[64]{0:T(128)S(1)} %select_reduce_fusion.2.units_ref, f32[64]{0:T(128)S(1)} %convert_divide_fusion.scale_ref, s32[1,2048]{1,0:T(1,128)S(1)} %bitcast.91, f32[64,2048]{1,0:T(8,128)S(1)} %maximum_convert_fusion.1.lanes_ref, bf16[2048,128]{1,0:T(8,128)(2,1)S(1)} %bitcast.86), custom_call_target="tpu_custom_call" | custom-call | flops 262144 | bytes 256 | tf_op jit(solution)/shard_map/gradient/pallas_call | solution.py:149
  221.3 4.9 %all-to-all-start.1 = ((bf16[8,256,128]{2,1,0:T(8,128)(2,1)}), bf16[8,256,128]{2,1,0:T(8,128)(2,1)S(1)}, u32[]{:S(2)}, u32[]{:S(2)}) async-start(bf16[8,256,128]{2,1,0:T(8,128)(2,1)} %get-tuple-element.84), calls=%async_computation.1 | async-start | bytes 1048576 | tf_op jit(solution)/shard_map/all_to_all | solution.py:295
  228.7 2.8 collective-permute-start.17
  231.5 3.0 collective-permute-done.17
  236.0 1.8 collective-permute-done.18
  238.5 1.3 copy-done.11
  239.9 6.2 %all-to-all-start.2 = ((bf16[16,128,1024]{2,1,0:T(8,128)(2,1)}), bf16[16,128,1024]{2,1,0:T(8,128)(2,1)}, u32[]{:S(2)}, u32[]{:S(2)}) async-start(bf16[16,128,1024]{2,1,0:T(8,128)(2,1)} %bitcast.83), calls=%async_computation.2 | async-start | bytes 8388608 | tf_op jit(solution)/shard_map/all_to_all | solution.py:287
  246.3 1.5 collective-permute-start.23
  248.5 14.8 %collective-permute-start.24 = (f32[]{:T(128)}, f32[]{:T(128)}, u32[]{:S(2)}, u32[]{:S(2)}) collective-permute-start(f32[]{:T(128)} %add.246), channel_id=1, source_target_pairs={{0,2},{1,3},{2,0},{3,1},{4,6},{5,7},{6,4},{7,5},{8,10},{9,11},{10,... | collective-permute-start | bytes 20 | tf_op jit(solution)/shard_map/ppermute | solution.py:298
  265.0 3.4 copy-done
  268.4 3.4 copy-done.2
  272.8 1.6 copy-done.12
  274.4 16.8 %update.1 = (f32[256,8192]{1,0:T(8,128)}, f32[256,8192]{1,0:T(8,128)}, f32[256,8192]{1,0:T(8,128)}) custom-call(s32[8]{0:T(128)S(1)} %stack.126.columns_ref, f32[1,1]{1,0:T(1,128)} %bitcast.37.clip_ref, f32[256,8192]{1,0:T(8,128)S(1)} %bitcast.82, f32[256,8192]{1,0:T(8,128)S(1)} %bitcast.84, f32[256,8192]{1,0:T(8,128)} %bitcast.93, ...), custom_call_target="tpu_custom_call" | custom-call | flops 10240 | bytes 13312 | tf_op jit(solution)/shard_map/update/pallas_call | solution.py:196
  292.5 3.9 %multiply_subtract_fusion = (f32[8,32,1024]{2,1,0:T(8,128)}, f32[8,32,1024]{2,1,0:T(8,128)}, f32[8,32,1024]{2,1,0:T(8,128)}) fusion(f32[8,32,1024]{2,1,0:T(8,128)S(1)} %copy-done.14, f32[8,32,1024]{2,1,0:T(8,128)S(1)} %mul.142, f32[8,32,1024]{2,1,0:T(8,128)} %param.22, f32[8,32,1024]{2,1,0:T(8,128)} %param.23), kind=kLoop, calls=%fused_computation.13 | loop fusion | flops 3932160 | bytes 7340032 | tf_op jit(solution)/shard_map/sub | solution.py:24
  296.4 42.2 %all-to-all-done.2.back_ref = bf16[16,128,1024]{2,1,0:T(8,128)(2,1)} async-done(((bf16[16,128,1024]{2,1,0:T(8,128)(2,1)}), bf16[16,128,1024]{2,1,0:T(8,128)(2,1)}, u32[]{:S(2)}, u32[]{:S(2)}) %all-to-all-start.2) | async-done | bytes 4194336 | tf_op jit(solution)/shard_map/all_to_all | solution.py:287
  338.6 4.4 %join.1 = bf16[128,8192]{1,0:T(8,128)(2,1)} custom-call(bf16[16,128,1024]{2,1,0:T(8,128)(2,1)} %all-to-all-done.2.back_ref, f32[128,1]{1,0:T(8,128)S(1)} %copy.45.scale_ref), custom_call_target="tpu_custom_call" | custom-call | flops 768 | bytes 1536 | tf_op jit(solution)/shard_map/join/pallas_call | solution.py:222
  (164 shorter events, 34.7 us)
Async XLA Ops:
  3.0 15.6 %collective-permute-start = (bf16[144,1024]{1,0:T(8,128)(2,1)}, bf16[144,1024]{1,0:T(8,128)(2,1)S(1)}, u32[]{:S(2)}, u32[]{:S(2)}) collective-permute-start(bf16[144,1024]{1,0:T(8,128)(2,1)} %pad_maximum_fusion.8), channel_id=1, source_target_pairs={{0,8},{1,9},{2,10},{3,11},{4,12},{5,13},{6,14},{7,15},{8,0},{9,1},... | collective-permute-start | bytes 884744 | tf_op jit(solution)/shard_map/ppermute | solution.py:347
  12.7 8.5 %copy-start.20 = (bf16[128,1024]{1,0:T(8,128)(2,1)S(1)}, bf16[128,1024]{1,0:T(8,128)(2,1)}, u32[]{:S(2)}) copy-start(bf16[128,1024]{1,0:T(8,128)(2,1)} %param.14) | copy-start | bytes 786436
  22.4 2.3 collective-permute-start.1
  26.3 10.8 %collective-permute-start.2 = (bf16[2,544,128]{2,1,0:T(8,128)(2,1)}, bf16[2,544,128]{2,1,0:T(8,128)(2,1)S(1)}, u32[]{:S(2)}, u32[]{:S(2)}) collective-permute-start(bf16[2,544,128]{2,1,0:T(8,128)(2,1)} %get-tuple-element.56), channel_id=1, source_target_pairs={{0,2},{1,3},{2,0},{3,1},{4,6},{5,7},{6,4},{7,5},{8,10},{9,11},{10,... | collective-permute-start | bytes 835592 | tf_op jit(solution)/shard_map/ppermute | solution.py:298
  26.7 10.4 %collective-permute-start.3 = (bf16[2,544,128]{2,1,0:T(8,128)(2,1)}, bf16[2,544,128]{2,1,0:T(8,128)(2,1)}, u32[]{:S(2)}, u32[]{:S(2)}) collective-permute-start(bf16[2,544,128]{2,1,0:T(8,128)(2,1)} %get-tuple-element.57), channel_id=1, source_target_pairs={{0,4},{1,5},{2,6},{3,7},{4,0},{5,1},{6,2},{7,3},{8,12},{9,13},{10,... | collective-permute-start | bytes 835592 | tf_op jit(solution)/shard_map/ppermute | solution.py:298
  27.8 20.0 %collective-permute-start.4 = (bf16[2,544,128]{2,1,0:T(8,128)(2,1)}, bf16[2,544,128]{2,1,0:T(8,128)(2,1)S(1)}, u32[]{:S(2)}, u32[]{:S(2)}) collective-permute-start(bf16[2,544,128]{2,1,0:T(8,128)(2,1)} %pad_maximum_fusion.11), channel_id=1, source_target_pairs={{0,6},{1,7},{2,4},{3,5},{4,2},{5,3},{6,0},{7,1},{8,14},{9,15},{10,... | collective-permute-start | bytes 835592 | tf_op jit(solution)/shard_map/ppermute | solution.py:298
  29.3 109.3 %all-to-all-start = ((bf16[16,128,1024]{2,1,0:T(8,128)(2,1)}), bf16[16,128,1024]{2,1,0:T(8,128)(2,1)}, u32[]{:S(2)}, u32[]{:S(2)}) async-start(bf16[16,128,1024]{2,1,0:T(8,128)(2,1)} %bitcast.92), calls=%async_computation | async-start | bytes 8388608 | tf_op jit(solution)/shard_map/all_to_all | solution.py:287
  57.8 5.1 %collective-permute-start.5 = (f32[64,2048]{1,0:T(8,128)S(1)}, f32[64,2048]{1,0:T(8,128)S(1)}, u32[]{:S(2)}, u32[]{:S(2)}) collective-permute-start(f32[64,2048]{1,0:T(8,128)S(1)} %narrow.2), channel_id=1, source_target_pairs={{0,1},{1,0},{2,3},{3,2},{4,5},{5,4},{6,7},{7,6},{8,9},{9,8},{10,11... | collective-permute-start | bytes 1572872 | tf_op jit(solution)/shard_map/ppermute | solution.py:298
  68.8 2.5 copy-start.21
  70.4 4.4 %collective-permute-start.6 = (bf16[4,256,1024]{2,1,0:T(8,128)(2,1)}, bf16[4,256,1024]{2,1,0:T(8,128)(2,1)S(1)}, u32[]{:S(2)}, u32[]{:S(2)}) collective-permute-start(bf16[4,256,1024]{2,1,0:T(8,128)(2,1)} %pad_maximum_fusion), channel_id=1, source_target_pairs={{0,1},{1,0},{2,3},{3,2},{4,5},{5,4},{6,7},{7,6},{8,9},{9,8},{10,11... | collective-permute-start | bytes 6291464 | tf_op jit(solution)/shard_map/ppermute | solution.py:298
  72.2 2.7 copy-start.19
  72.3 11.5 %copy-start.18 = (bf16[1,256,1024]{2,1,0:T(8,128)(2,1)S(1)}, bf16[1,256,1024]{2,1,0:T(8,128)(2,1)}, u32[]{:S(2)}) copy-start(bf16[1,256,1024]{2,1,0:T(8,128)(2,1)} %get-tuple-element.100) | copy-start | bytes 1572868
  74.9 52.3 %copy-start.17 = (bf16[1,256,1024]{2,1,0:T(8,128)(2,1)S(1)}, bf16[1,256,1024]{2,1,0:T(8,128)(2,1)}, u32[]{:S(2)}) copy-start(bf16[1,256,1024]{2,1,0:T(8,128)(2,1)} %get-tuple-element.99) | copy-start | bytes 1572868
  76.0 79.0 %collective-permute-start.7 = (bf16[2,256,1024]{2,1,0:T(8,128)(2,1)}, bf16[2,256,1024]{2,1,0:T(8,128)(2,1)}, u32[]{:S(2)}, u32[]{:S(2)}) collective-permute-start(bf16[2,256,1024]{2,1,0:T(8,128)(2,1)} %pad_maximum_fusion.3), channel_id=1, source_target_pairs={{0,2},{1,3},{2,0},{3,1},{4,6},{5,7},{6,4},{7,5},{8,10},{9,11},{10,... | collective-permute-start | bytes 3145736 | tf_op jit(solution)/shard_map/ppermute | solution.py:298
  83.7 42.3 %collective-permute-start.10 = (bf16[64,1024]{1,0:T(8,128)(2,1)S(1)}, bf16[64,1024]{1,0:T(8,128)(2,1)S(1)}, u32[]{:S(2)}, u32[]{:S(2)}) collective-permute-start(bf16[64,1024]{1,0:T(8,128)(2,1)S(1)} %dynamic-slice_convert_fusion.1), channel_id=1, source_target_pairs={{0,2},{1,3},{2,0},{3,1},{4,6},{5,7},{6,4},{7,5},{8,10},{9,11},{10,... | collective-permute-start | bytes 393224 | tf_op jit(solution)/shard_map/ppermute | solution.py:298
  84.8 71.5 %collective-permute-start.8 = (bf16[2,256,1024]{2,1,0:T(8,128)(2,1)}, bf16[2,256,1024]{2,1,0:T(8,128)(2,1)}, u32[]{:S(2)}, u32[]{:S(2)}) collective-permute-start(bf16[2,256,1024]{2,1,0:T(8,128)(2,1)} %pad_maximum_fusion.4), channel_id=1, source_target_pairs={{0,4},{1,5},{2,6},{3,7},{4,0},{5,1},{6,2},{7,3},{8,12},{9,13},{10,... | collective-permute-start | bytes 3145736 | tf_op jit(solution)/shard_map/ppermute | solution.py:298
  126.1 8.7 %collective-permute-start.11 = (bf16[64,1024]{1,0:T(8,128)(2,1)S(1)}, bf16[64,1024]{1,0:T(8,128)(2,1)S(1)}, u32[]{:S(2)}, u32[]{:S(2)}) collective-permute-start(bf16[64,1024]{1,0:T(8,128)(2,1)S(1)} %fusion.10), channel_id=1, source_target_pairs={{0,4},{1,5},{2,6},{3,7},{4,0},{5,1},{6,2},{7,3},{8,12},{9,13},{10,... | collective-permute-start | bytes 393224 | tf_op jit(solution)/shard_map/ppermute | solution.py:298
  128.2 28.9 %collective-permute-start.9 = (bf16[2,256,1024]{2,1,0:T(8,128)(2,1)}, bf16[2,256,1024]{2,1,0:T(8,128)(2,1)}, u32[]{:S(2)}, u32[]{:S(2)}) collective-permute-start(bf16[2,256,1024]{2,1,0:T(8,128)(2,1)} %pad_maximum_fusion.5), channel_id=1, source_target_pairs={{0,6},{1,7},{2,4},{3,5},{4,2},{5,3},{6,0},{7,1},{8,14},{9,15},{10,... | collective-permute-start | bytes 3145736 | tf_op jit(solution)/shard_map/ppermute | solution.py:298
  134.8 3.7 %collective-permute-start.12 = (bf16[64,1024]{1,0:T(8,128)(2,1)S(1)}, bf16[64,1024]{1,0:T(8,128)(2,1)S(1)}, u32[]{:S(2)}, u32[]{:S(2)}) collective-permute-start(bf16[64,1024]{1,0:T(8,128)(2,1)S(1)} %add_convert_fusion.1), channel_id=1, source_target_pairs={{0,1},{1,0},{2,3},{3,2},{4,5},{5,4},{6,7},{7,6},{8,9},{9,8},{10,11... | collective-permute-start | bytes 393224 | tf_op jit(solution)/shard_map/ppermute | solution.py:298
  153.0 4.0 %copy-start.3 = (bf16[1,256,1024]{2,1,0:T(8,128)(2,1)S(1)}, bf16[1,256,1024]{2,1,0:T(8,128)(2,1)}, u32[]{:S(2)}) copy-start(bf16[1,256,1024]{2,1,0:T(8,128)(2,1)} %get-tuple-element.73.refs_0_) | copy-start | bytes 1572868
  153.6 52.1 %collective-permute-start.21 = (bf16[2,256,1024]{2,1,0:T(8,128)(2,1)S(1)}, bf16[2,256,1024]{2,1,0:T(8,128)(2,1)S(1)}, u32[]{:S(2)}, u32[]{:S(2)}) collective-permute-start(bf16[2,256,1024]{2,1,0:T(8,128)(2,1)S(1)} %get-tuple-element.109), channel_id=1, source_target_pairs={{0,6},{1,7},{2,4},{3,5},{4,2},{5,3},{6,0},{7,1},{8,14},{9,15},{10,... | collective-permute-start | bytes 3145736 | tf_op jit(solution)/shard_map/ppermute | solution.py:298
  154.2 51.6 %collective-permute-start.20 = (bf16[2,256,1024]{2,1,0:T(8,128)(2,1)S(1)}, bf16[2,256,1024]{2,1,0:T(8,128)(2,1)S(1)}, u32[]{:S(2)}, u32[]{:S(2)}) collective-permute-start(bf16[2,256,1024]{2,1,0:T(8,128)(2,1)S(1)} %get-tuple-element.110), channel_id=1, source_target_pairs={{0,4},{1,5},{2,6},{3,7},{4,0},{5,1},{6,2},{7,3},{8,12},{9,13},{10,... | collective-permute-start | bytes 3145736 | tf_op jit(solution)/shard_map/ppermute | solution.py:298
  154.9 50.9 %collective-permute-start.19 = (bf16[2,256,1024]{2,1,0:T(8,128)(2,1)S(1)}, bf16[2,256,1024]{2,1,0:T(8,128)(2,1)S(1)}, u32[]{:S(2)}, u32[]{:S(2)}) collective-permute-start(bf16[2,256,1024]{2,1,0:T(8,128)(2,1)S(1)} %get-tuple-element.111), channel_id=1, source_target_pairs={{0,2},{1,3},{2,0},{3,1},{4,6},{5,7},{6,4},{7,5},{8,10},{9,11},{10,... | collective-permute-start | bytes 3145736 | tf_op jit(solution)/shard_map/ppermute | solution.py:298
  170.1 3.9 %collective-permute-start.13 = (f32[64,2048]{1,0:T(8,128)S(1)}, f32[64,2048]{1,0:T(8,128)S(1)}, u32[]{:S(2)}, u32[]{:S(2)}) collective-permute-start(f32[64,2048]{1,0:T(8,128)S(1)} %narrow.3), channel_id=1, source_target_pairs={{0,1},{1,0},{2,3},{3,2},{4,5},{5,4},{6,7},{7,6},{8,9},{9,8},{10,11... | collective-permute-start | bytes 1572872 | tf_op jit(solution)/shard_map/ppermute | solution.py:298
  174.1 31.6 %collective-permute-start.14 = (bf16[64,1024]{1,0:T(8,128)(2,1)S(1)}, bf16[64,1024]{1,0:T(8,128)(2,1)S(1)}, u32[]{:S(2)}, u32[]{:S(2)}) collective-permute-start(bf16[64,1024]{1,0:T(8,128)(2,1)S(1)} %dynamic-slice_convert_fusion), channel_id=1, source_target_pairs={{0,2},{1,3},{2,0},{3,1},{4,6},{5,7},{6,4},{7,5},{8,10},{9,11},{10,... | collective-permute-start | bytes 393224 | tf_op jit(solution)/shard_map/ppermute | solution.py:298
  189.2 18.6 %copy-start.1 = (bf16[2048,1024]{1,0:T(8,128)(2,1)}, bf16[2048,1024]{1,0:T(8,128)(2,1)S(1)}, u32[]{:S(2)}) copy-start(bf16[2048,1024]{1,0:T(8,128)(2,1)S(1)} %pieces.1) | copy-start | bytes 12582916
  205.7 2.0 copy-start.4
  205.8 2.0 copy-start.6
  205.9 2.2 copy-start.8
  208.1 30.3 %collective-permute-start.22 = (bf16[4,256,1024]{2,1,0:T(8,128)(2,1)}, bf16[4,256,1024]{2,1,0:T(8,128)(2,1)S(1)}, u32[]{:S(2)}, u32[]{:S(2)}) collective-permute-start(bf16[4,256,1024]{2,1,0:T(8,128)(2,1)} %pad_maximum_fusion.1), channel_id=1, source_target_pairs={{0,1},{1,0},{2,3},{3,2},{4,5},{5,4},{6,7},{7,6},{8,9},{9,8},{10,11... | collective-permute-start | bytes 6291464 | tf_op jit(solution)/shard_map/ppermute | solution.py:298
  208.6 5.2 %collective-permute-start.15 = (bf16[64,1024]{1,0:T(8,128)(2,1)S(1)}, bf16[64,1024]{1,0:T(8,128)(2,1)S(1)}, u32[]{:S(2)}, u32[]{:S(2)}) collective-permute-start(bf16[64,1024]{1,0:T(8,128)(2,1)S(1)} %fusion.11), channel_id=1, source_target_pairs={{0,4},{1,5},{2,6},{3,7},{4,0},{5,1},{6,2},{7,3},{8,12},{9,13},{10,... | collective-permute-start | bytes 393224 | tf_op jit(solution)/shard_map/ppermute | solution.py:298
  213.9 1.8 collective-permute-start.16
  221.3 17.1 %all-to-all-start.1 = ((bf16[8,256,128]{2,1,0:T(8,128)(2,1)}), bf16[8,256,128]{2,1,0:T(8,128)(2,1)S(1)}, u32[]{:S(2)}, u32[]{:S(2)}) async-start(bf16[8,256,128]{2,1,0:T(8,128)(2,1)} %get-tuple-element.84), calls=%async_computation.1 | async-start | bytes 1048576 | tf_op jit(solution)/shard_map/all_to_all | solution.py:295
  228.7 5.8 %collective-permute-start.17 = (f32[]{:T(128)}, f32[]{:T(128)}, u32[]{:S(2)}, u32[]{:S(2)}) collective-permute-start(f32[]{:T(128)} %reduce_sum.68), channel_id=1, source_target_pairs={{0,8},{1,9},{2,10},{3,11},{4,12},{5,13},{6,14},{7,15},{8,0},{9,1},... | collective-permute-start | bytes 20 | tf_op jit(solution)/shard_map/ppermute | solution.py:298
  235.2 2.6 collective-permute-start.18
  238.4 1.4 copy-start.15
  238.4 1.4 copy-start.11
  239.9 6.2 %copy-start.22 = (s32[128,1]{0,1:T(1,128)S(1)}, s32[128,1]{0,1:T(1,128)}, u32[]{:S(2)}) copy-start(s32[128,1]{0,1:T(1,128)} %param.15) | copy-start | bytes 1540
  239.9 25.1 %copy-start.5 = (bf16[2,256,1024]{2,1,0:T(8,128)(2,1)S(1)}, bf16[2,256,1024]{2,1,0:T(8,128)(2,1)}, u32[]{:S(2)}) copy-start(bf16[2,256,1024]{2,1,0:T(8,128)(2,1)} %copy-done.4) | copy-start | bytes 3145732
  239.9 25.1 %copy-start.7 = (bf16[2,256,1024]{2,1,0:T(8,128)(2,1)S(1)}, bf16[2,256,1024]{2,1,0:T(8,128)(2,1)}, u32[]{:S(2)}) copy-start(bf16[2,256,1024]{2,1,0:T(8,128)(2,1)} %copy-done.6) | copy-start | bytes 3145732
  239.9 25.1 %copy-start.9 = (bf16[2,256,1024]{2,1,0:T(8,128)(2,1)S(1)}, bf16[2,256,1024]{2,1,0:T(8,128)(2,1)}, u32[]{:S(2)}) copy-start(bf16[2,256,1024]{2,1,0:T(8,128)(2,1)} %copy-done.8) | copy-start | bytes 3145732
  239.9 98.7 %all-to-all-start.2 = ((bf16[16,128,1024]{2,1,0:T(8,128)(2,1)}), bf16[16,128,1024]{2,1,0:T(8,128)(2,1)}, u32[]{:S(2)}, u32[]{:S(2)}) async-start(bf16[16,128,1024]{2,1,0:T(8,128)(2,1)} %bitcast.83), calls=%async_computation.2 | async-start | bytes 8388608 | tf_op jit(solution)/shard_map/all_to_all | solution.py:287
  246.3 1.5 collective-permute-start.23
  248.5 15.7 %collective-permute-start.24 = (f32[]{:T(128)}, f32[]{:T(128)}, u32[]{:S(2)}, u32[]{:S(2)}) collective-permute-start(f32[]{:T(128)} %add.246), channel_id=1, source_target_pairs={{0,2},{1,3},{2,0},{3,1},{4,6},{5,7},{6,4},{7,5},{8,10},{9,11},{10,... | collective-permute-start | bytes 20 | tf_op jit(solution)/shard_map/ppermute | solution.py:298
  265.0 3.4 copy-start
  268.4 3.4 copy-start.2
  272.8 1.6 copy-start.12
  274.4 16.8 %copy-start.16 = (bf16[8,256,128]{2,1,0:T(8,128)(2,1)S(1)}, bf16[8,256,128]{2,1,0:T(8,128)(2,1)}, u32[]{:S(2)}) copy-start(bf16[8,256,128]{2,1,0:T(8,128)(2,1)} %copy-done.15) | copy-start | bytes 1572868
  (3 other events, 3.5 us)

commit v5 on v4

--- a/solution.py
+++ b/solution.py
@@ -212,7 +212,7 @@
 
 def join(back, scale, team):
     _, rows, cut = back.shape
-    tile = min(rows, 32)
+    tile = min(rows, 16)
 
     def kernel(back_ref, scale_ref, out_ref):
         for j in range(team):

time: 344 us -> 346 us (level)
  no operation moved by 1% of the time
where the time goes in v5:
time: 346 us; the launch traced here: 345 us
  waiting for transfers between devices  136 us (39%)
  starting transfers between devices  74.7 us (22%)
  Pallas kernels  72.8 us (21%)
  local copies, waits for them, and re-layouts  29.9 us (9%)
  other arithmetic  26.4 us (8%)
  between operations  5.31 us (2%)
    ppermute x24, waiting for transfers between devices, send(): return lax.ppermute(array, 'dp', [(i, i ^ apart) for i in range(devices)])  87.7 us
    ppermute x24, starting transfers between devices, send(): return lax.ppermute(array, 'dp', [(i, i ^ apart) for i in range(devices)])  53.5 us
    all_to_all x2, waiting for transfers between devices, to_all(): return lax.all_to_all(array, 'dp', split_axis=0, concat_axis=0, tiled=True)  42.2 us
    pallas_call x2, Pallas kernels, gradient(): pl.pallas_call(kernel, grid_spec=pltpu.PrefetchScalarGridSpec(num_scalar_...  20 us
    pallas_call x2, Pallas kernels, narrow(): pl.pallas_call(kernel, grid_spec=pltpu.PrefetchScalarGridSpec(num_scalar_...  17.4 us
    pallas_call x1, Pallas kernels, update_slots(): pl.pallas_call(kernel, grid_spec=pltpu.PrefetchScalarGridSpec(num_scalar_...  16.8 us
    unnamed x56, local copies, waits for them, and re-layouts  16.6 us
    all_to_all x2, starting transfers between devices, to_all(): return lax.all_to_all(array, 'dp', split_axis=0, concat_axis=0, tiled=True)  14 us
  transfers between devices with their start and end apart: 28, of which 17 were waited for; matrix products, arithmetic and copies ran while one was open for 10% of the time, Pallas kernels for 19%

profile of v5, /device:TPU:15, one launch (start us, length us, event | category | flops | bytes accessed | tf_op | source)
XLA Modules:
  0.0 345.0 jit_solution(4540445418731645468)
XLA Ops:
  1.3 1.7 pad_maximum_fusion.8
  3.0 2.3 collective-permute-start
  8.3 3.0 copy.49
  11.3 1.2 copy.37
  12.7 5.9 %collective-permute-done = bf16[144,1024]{1,0:T(8,128)(2,1)S(1)} collective-permute-done((bf16[144,1024]{1,0:T(8,128)(2,1)}, bf16[144,1024]{1,0:T(8,128)(2,1)S(1)}, u32[]{:S(2)}, u32[]{:S(2)}) %collective-permute-start) | collective-permute-done | bytes 294944 | tf_op jit(solution)/shard_map/ppermute | solution.py:347
  18.6 2.6 tile.20
  27.8 1.5 collective-permute-start.4
  29.3 7.8 %all-to-all-start = ((bf16[16,128,1024]{2,1,0:T(8,128)(2,1)}), bf16[16,128,1024]{2,1,0:T(8,128)(2,1)}, u32[]{:S(2)}, u32[]{:S(2)}) async-start(bf16[16,128,1024]{2,1,0:T(8,128)(2,1)} %bitcast.92), calls=%async_computation | async-start | bytes 8388608 | tf_op jit(solution)/shard_map/all_to_all | solution.py:287
  37.9 9.9 %collective-permute-done.4 = bf16[2,544,128]{2,1,0:T(8,128)(2,1)S(1)} collective-permute-done((bf16[2,544,128]{2,1,0:T(8,128)(2,1)}, bf16[2,544,128]{2,1,0:T(8,128)(2,1)S(1)}, u32[]{:S(2)}, u32[]{:S(2)}) %collective-permute-start.4) | collective-permute-done | bytes 278560 | tf_op jit(solution)/shard_map/ppermute | solution.py:298
  48.8 2.4 dynamic_update_slice.63
  53.5 4.4 %narrow.2 = f32[64,2048]{1,0:T(8,128)S(1)} custom-call(s32[64]{0:T(128)S(1)} %reshape.254.units_ref, s32[1,2048]{1,0:T(1,128)S(1)} %bitcast.87, bf16[2048,128]{1,0:T(8,128)(2,1)S(1)} %bitcast.85, bf16[8,256,128]{2,1,0:T(8,128)(2,1)S(1)} %slice_dynamic-update-slice_fusion.refs_0_), custom_call_target="tpu_custom_call" | custom-call | flops 262144 | bytes 128 | tf_op jit(solution)/shard_map/narrow/pallas_call | solution.py:63
  57.8 3.6 %collective-permute-start.5 = (f32[64,2048]{1,0:T(8,128)S(1)}, f32[64,2048]{1,0:T(8,128)S(1)}, u32[]{:S(2)}, u32[]{:S(2)}) collective-permute-start(f32[64,2048]{1,0:T(8,128)S(1)} %narrow.2), channel_id=1, source_target_pairs={{0,1},{1,0},{2,3},{3,2},{4,5},{5,4},{6,7},{7,6},{8,9},{9,8},{10,11... | collective-permute-start | bytes 1572872 | tf_op jit(solution)/shard_map/ppermute | solution.py:298
  61.4 1.5 collective-permute-done.5
  63.0 5.8 %fusion.9 = (bf16[1,256,1024]{2,1,0:T(8,128)(2,1)}, bf16[1,256,1024]{2,1,0:T(8,128)(2,1)}, bf16[1,256,1024]{2,1,0:T(8,128)(2,1)}, bf16[1,256,1024]{2,1,0:T(8,128...) fusion(f32[256,8192]{1,0:T(8,128)} %bitcast.81, ...), kind=kLoop, calls=%fused_computation.32 | loop fusion | flops 2097152 | bytes 8388896 | tf_op jit(solution)/shard_map/stack | solution.py:303
  68.8 1.6 pad_maximum_fusion
  72.3 2.5 collective-permute-done.6.refs_1_
  76.0 7.7 %collective-permute-start.7 = (bf16[2,256,1024]{2,1,0:T(8,128)(2,1)}, bf16[2,256,1024]{2,1,0:T(8,128)(2,1)}, u32[]{:S(2)}, u32[]{:S(2)}) collective-permute-start(bf16[2,256,1024]{2,1,0:T(8,128)(2,1)} %pad_maximum_fusion.3), channel_id=1, source_target_pairs={{0,2},{1,3},{2,0},{3,1},{4,6},{5,7},{6,4},{7,5},{8,10},{9,11},{10,... | collective-permute-start | bytes 3145736 | tf_op jit(solution)/shard_map/ppermute | solution.py:298
  84.8 3.3 collective-permute-start.8
  88.1 37.9 %collective-permute-done.10 = bf16[64,1024]{1,0:T(8,128)(2,1)S(1)} collective-permute-done((bf16[64,1024]{1,0:T(8,128)(2,1)S(1)}, bf16[64,1024]{1,0:T(8,128)(2,1)S(1)}, u32[]{:S(2)}, u32[]{:S(2)}) %collective-permute-start.10) | collective-permute-done | bytes 131104 | tf_op jit(solution)/shard_map/ppermute | solution.py:298
  128.2 2.5 collective-permute-start.9
  130.7 4.0 %collective-permute-done.11 = bf16[64,1024]{1,0:T(8,128)(2,1)S(1)} collective-permute-done((bf16[64,1024]{1,0:T(8,128)(2,1)S(1)}, bf16[64,1024]{1,0:T(8,128)(2,1)S(1)}, u32[]{:S(2)}, u32[]{:S(2)}) %collective-permute-start.11) | collective-permute-done | bytes 131104 | tf_op jit(solution)/shard_map/ppermute | solution.py:298
  134.8 2.7 collective-permute-start.12
  138.6 14.5 %gradient.2 = (bf16[8,256,1024]{2,1,0:T(8,128)(2,1)S(1)}, f32[1,1024]{1,0:T(1,128)S(1)}) custom-call(s32[64]{0:T(128)S(1)} %reshape.260.units_ref, f32[64]{0:T(128)S(1)} %div.80.scale_ref, s32[1,2048]{1,0:T(1,128)S(1)} %bitcast.88, f32[64,2048]{1,0:T(8,128)S(1)} %maximum_convert_fusion.lanes_ref, bf16[2048,1024]{1,0:T(8,128)(2,1)} %bitcast.22.right_ref.left_ref), custom_call_target="tpu_custom_call" | custom-call | flops 2097152 | bytes 2048 | tf_op jit(solution)/shard_map/gradient/pallas_call | solution.py:149
  154.9 1.4 collective-permute-start.19
  157.1 13.0 %narrow.3 = f32[64,2048]{1,0:T(8,128)S(1)} custom-call(s32[64]{0:T(128)S(1)} %reshape.254.units_ref, s32[1,2048]{1,0:T(1,128)S(1)} %bitcast.89, bf16[2048,1024]{1,0:T(8,128)(2,1)} %bitcast.22.right_ref.left_ref, bf16[1,256,1024]{2,1,0:T(8,128)(2,1)S(1)} %copy-done.3, bf16[4,256,1024]{2,1,0:T(8,128)(2,1)S(1)} %collective-permute-done.6.refs_1_, ...), custom_call_target="tpu_custom_call" | custom-call | flops 2097152 | bytes 1024 | tf_op jit(solution)/shard_map/narrow/pallas_call | solution.py:63
  170.1 2.4 collective-permute-start.13
  172.5 1.5 collective-permute-done.13
  174.1 1.9 collective-permute-start.14
  176.9 12.3 %pieces.1 = bf16[2048,1024]{1,0:T(8,128)(2,1)S(1)} custom-call(s32[64]{0:T(128)S(1)} %reshape.254.units_ref, s32[1,2048]{1,0:T(1,128)S(1)} %bitcast.90, f32[64,2048]{1,0:T(8,128)S(1)} %maximum_convert_fusion.lanes_ref, bf16[1,256,1024]{2,1,0:T(8,128)(2,1)S(1)} %copy-done.3, bf16[4,256,1024]{2,1,0:T(8,128)(2,1)S(1)} %collective-permute-done.6.refs_1_, ...), custom_call_target="tpu_custom_call" | custom-call | flops 2097152 | bytes 1024 | tf_op jit(solution)/shard_map/pieces/pallas_call | solution.py:105
  189.2 16.6 %collective-permute-done.14 = bf16[64,1024]{1,0:T(8,128)(2,1)S(1)} collective-permute-done((bf16[64,1024]{1,0:T(8,128)(2,1)S(1)}, bf16[64,1024]{1,0:T(8,128)(2,1)S(1)}, u32[]{:S(2)}, u32[]{:S(2)}) %collective-permute-start.14) | collective-permute-done | bytes 131104 | tf_op jit(solution)/shard_map/ppermute | solution.py:298
  205.9 1.8 pad_maximum_fusion.1
  209.4 4.4 %collective-permute-done.15 = bf16[64,1024]{1,0:T(8,128)(2,1)S(1)} collective-permute-done((bf16[64,1024]{1,0:T(8,128)(2,1)S(1)}, bf16[64,1024]{1,0:T(8,128)(2,1)S(1)}, u32[]{:S(2)}, u32[]{:S(2)}) %collective-permute-start.15) | collective-permute-done | bytes 131104 | tf_op jit(solution)/shard_map/ppermute | solution.py:298
  215.8 5.5 %gradient.3 = (bf16[8,256,128]{2,1,0:T(8,128)(2,1)}, f32[1,128]{1,0:T(1,128)S(1)}) custom-call(s32[64]{0:T(128)S(1)} %select_reduce_fusion.2.units_ref, f32[64]{0:T(128)S(1)} %convert_divide_fusion.scale_ref, s32[1,2048]{1,0:T(1,128)S(1)} %bitcast.91, f32[64,2048]{1,0:T(8,128)S(1)} %maximum_convert_fusion.1.lanes_ref, bf16[2048,128]{1,0:T(8,128)(2,1)S(1)} %bitcast.86), custom_call_target="tpu_custom_call" | custom-call | flops 262144 | bytes 256 | tf_op jit(solution)/shard_map/gradient/pallas_call | solution.py:149
  221.3 4.9 %all-to-all-start.1 = ((bf16[8,256,128]{2,1,0:T(8,128)(2,1)}), bf16[8,256,128]{2,1,0:T(8,128)(2,1)S(1)}, u32[]{:S(2)}, u32[]{:S(2)}) async-start(bf16[8,256,128]{2,1,0:T(8,128)(2,1)} %get-tuple-element.84), calls=%async_computation.1 | async-start | bytes 1048576 | tf_op jit(solution)/shard_map/all_to_all | solution.py:295
  228.7 2.8 collective-permute-start.17
  231.5 3.0 collective-permute-done.17
  236.0 1.8 collective-permute-done.18
  238.5 1.3 copy-done.11
  239.9 6.2 %all-to-all-start.2 = ((bf16[16,128,1024]{2,1,0:T(8,128)(2,1)}), bf16[16,128,1024]{2,1,0:T(8,128)(2,1)}, u32[]{:S(2)}, u32[]{:S(2)}) async-start(bf16[16,128,1024]{2,1,0:T(8,128)(2,1)} %bitcast.83), calls=%async_computation.2 | async-start | bytes 8388608 | tf_op jit(solution)/shard_map/all_to_all | solution.py:287
  246.3 1.5 collective-permute-start.23
  248.5 14.8 %collective-permute-start.24 = (f32[]{:T(128)}, f32[]{:T(128)}, u32[]{:S(2)}, u32[]{:S(2)}) collective-permute-start(f32[]{:T(128)} %add.246), channel_id=1, source_target_pairs={{0,2},{1,3},{2,0},{3,1},{4,6},{5,7},{6,4},{7,5},{8,10},{9,11},{10,... | collective-permute-start | bytes 20 | tf_op jit(solution)/shard_map/ppermute | solution.py:298
  265.0 3.4 copy-done
  268.4 3.4 copy-done.2
  272.8 1.6 copy-done.12
  274.4 16.8 %update.1 = (f32[256,8192]{1,0:T(8,128)}, f32[256,8192]{1,0:T(8,128)}, f32[256,8192]{1,0:T(8,128)}) custom-call(s32[8]{0:T(128)S(1)} %stack.126.columns_ref, f32[1,1]{1,0:T(1,128)} %bitcast.37.clip_ref, f32[256,8192]{1,0:T(8,128)S(1)} %bitcast.82, f32[256,8192]{1,0:T(8,128)S(1)} %bitcast.84, f32[256,8192]{1,0:T(8,128)} %bitcast.93, ...), custom_call_target="tpu_custom_call" | custom-call | flops 10240 | bytes 13312 | tf_op jit(solution)/shard_map/update/pallas_call | solution.py:196
  292.5 3.9 %multiply_subtract_fusion = (f32[8,32,1024]{2,1,0:T(8,128)}, f32[8,32,1024]{2,1,0:T(8,128)}, f32[8,32,1024]{2,1,0:T(8,128)}) fusion(f32[8,32,1024]{2,1,0:T(8,128)S(1)} %copy-done.14, f32[8,32,1024]{2,1,0:T(8,128)S(1)} %mul.142, f32[8,32,1024]{2,1,0:T(8,128)} %param.22, f32[8,32,1024]{2,1,0:T(8,128)} %param.23), kind=kLoop, calls=%fused_computation.13 | loop fusion | flops 3932160 | bytes 7340032 | tf_op jit(solution)/shard_map/sub | solution.py:24
  296.4 42.2 %all-to-all-done.2.back_ref = bf16[16,128,1024]{2,1,0:T(8,128)(2,1)} async-done(((bf16[16,128,1024]{2,1,0:T(8,128)(2,1)}), bf16[16,128,1024]{2,1,0:T(8,128)(2,1)}, u32[]{:S(2)}, u32[]{:S(2)}) %all-to-all-start.2) | async-done | bytes 4194336 | tf_op jit(solution)/shard_map/all_to_all | solution.py:287
  338.6 6.4 %join.1 = bf16[128,8192]{1,0:T(8,128)(2,1)} custom-call(bf16[16,128,1024]{2,1,0:T(8,128)(2,1)} %all-to-all-done.2.back_ref, f32[128,1]{1,0:T(8,128)S(1)} %copy.45.scale_ref), custom_call_target="tpu_custom_call" | custom-call | flops 768 | bytes 1536 | tf_op jit(solution)/shard_map/join/pallas_call | solution.py:222
  (164 shorter events, 34.7 us)
Async XLA Ops:
  3.0 15.6 %collective-permute-start = (bf16[144,1024]{1,0:T(8,128)(2,1)}, bf16[144,1024]{1,0:T(8,128)(2,1)S(1)}, u32[]{:S(2)}, u32[]{:S(2)}) collective-permute-start(bf16[144,1024]{1,0:T(8,128)(2,1)} %pad_maximum_fusion.8), channel_id=1, source_target_pairs={{0,8},{1,9},{2,10},{3,11},{4,12},{5,13},{6,14},{7,15},{8,0},{9,1},... | collective-permute-start | bytes 884744 | tf_op jit(solution)/shard_map/ppermute | solution.py:347
  12.7 8.5 %copy-start.20 = (bf16[128,1024]{1,0:T(8,128)(2,1)S(1)}, bf16[128,1024]{1,0:T(8,128)(2,1)}, u32[]{:S(2)}) copy-start(bf16[128,1024]{1,0:T(8,128)(2,1)} %param.14) | copy-start | bytes 786436
  22.4 2.3 collective-permute-start.1
  26.3 10.8 %collective-permute-start.2 = (bf16[2,544,128]{2,1,0:T(8,128)(2,1)}, bf16[2,544,128]{2,1,0:T(8,128)(2,1)S(1)}, u32[]{:S(2)}, u32[]{:S(2)}) collective-permute-start(bf16[2,544,128]{2,1,0:T(8,128)(2,1)} %get-tuple-element.56), channel_id=1, source_target_pairs={{0,2},{1,3},{2,0},{3,1},{4,6},{5,7},{6,4},{7,5},{8,10},{9,11},{10,... | collective-permute-start | bytes 835592 | tf_op jit(solution)/shard_map/ppermute | solution.py:298
  26.7 10.4 %collective-permute-start.3 = (bf16[2,544,128]{2,1,0:T(8,128)(2,1)}, bf16[2,544,128]{2,1,0:T(8,128)(2,1)}, u32[]{:S(2)}, u32[]{:S(2)}) collective-permute-start(bf16[2,544,128]{2,1,0:T(8,128)(2,1)} %get-tuple-element.57), channel_id=1, source_target_pairs={{0,4},{1,5},{2,6},{3,7},{4,0},{5,1},{6,2},{7,3},{8,12},{9,13},{10,... | collective-permute-start | bytes 835592 | tf_op jit(solution)/shard_map/ppermute | solution.py:298
  27.8 20.0 %collective-permute-start.4 = (bf16[2,544,128]{2,1,0:T(8,128)(2,1)}, bf16[2,544,128]{2,1,0:T(8,128)(2,1)S(1)}, u32[]{:S(2)}, u32[]{:S(2)}) collective-permute-start(bf16[2,544,128]{2,1,0:T(8,128)(2,1)} %pad_maximum_fusion.11), channel_id=1, source_target_pairs={{0,6},{1,7},{2,4},{3,5},{4,2},{5,3},{6,0},{7,1},{8,14},{9,15},{10,... | collective-permute-start | bytes 835592 | tf_op jit(solution)/shard_map/ppermute | solution.py:298
  29.3 109.3 %all-to-all-start = ((bf16[16,128,1024]{2,1,0:T(8,128)(2,1)}), bf16[16,128,1024]{2,1,0:T(8,128)(2,1)}, u32[]{:S(2)}, u32[]{:S(2)}) async-start(bf16[16,128,1024]{2,1,0:T(8,128)(2,1)} %bitcast.92), calls=%async_computation | async-start | bytes 8388608 | tf_op jit(solution)/shard_map/all_to_all | solution.py:287
  57.8 5.1 %collective-permute-start.5 = (f32[64,2048]{1,0:T(8,128)S(1)}, f32[64,2048]{1,0:T(8,128)S(1)}, u32[]{:S(2)}, u32[]{:S(2)}) collective-permute-start(f32[64,2048]{1,0:T(8,128)S(1)} %narrow.2), channel_id=1, source_target_pairs={{0,1},{1,0},{2,3},{3,2},{4,5},{5,4},{6,7},{7,6},{8,9},{9,8},{10,11... | collective-permute-start | bytes 1572872 | tf_op jit(solution)/shard_map/ppermute | solution.py:298
  68.8 2.5 copy-start.21
  70.4 4.4 %collective-permute-start.6 = (bf16[4,256,1024]{2,1,0:T(8,128)(2,1)}, bf16[4,256,1024]{2,1,0:T(8,128)(2,1)S(1)}, u32[]{:S(2)}, u32[]{:S(2)}) collective-permute-start(bf16[4,256,1024]{2,1,0:T(8,128)(2,1)} %pad_maximum_fusion), channel_id=1, source_target_pairs={{0,1},{1,0},{2,3},{3,2},{4,5},{5,4},{6,7},{7,6},{8,9},{9,8},{10,11... | collective-permute-start | bytes 6291464 | tf_op jit(solution)/shard_map/ppermute | solution.py:298
  72.2 2.7 copy-start.19
  72.3 11.5 %copy-start.18 = (bf16[1,256,1024]{2,1,0:T(8,128)(2,1)S(1)}, bf16[1,256,1024]{2,1,0:T(8,128)(2,1)}, u32[]{:S(2)}) copy-start(bf16[1,256,1024]{2,1,0:T(8,128)(2,1)} %get-tuple-element.100) | copy-start | bytes 1572868
  74.9 52.3 %copy-start.17 = (bf16[1,256,1024]{2,1,0:T(8,128)(2,1)S(1)}, bf16[1,256,1024]{2,1,0:T(8,128)(2,1)}, u32[]{:S(2)}) copy-start(bf16[1,256,1024]{2,1,0:T(8,128)(2,1)} %get-tuple-element.99) | copy-start | bytes 1572868
  76.0 79.0 %collective-permute-start.7 = (bf16[2,256,1024]{2,1,0:T(8,128)(2,1)}, bf16[2,256,1024]{2,1,0:T(8,128)(2,1)}, u32[]{:S(2)}, u32[]{:S(2)}) collective-permute-start(bf16[2,256,1024]{2,1,0:T(8,128)(2,1)} %pad_maximum_fusion.3), channel_id=1, source_target_pairs={{0,2},{1,3},{2,0},{3,1},{4,6},{5,7},{6,4},{7,5},{8,10},{9,11},{10,... | collective-permute-start | bytes 3145736 | tf_op jit(solution)/shard_map/ppermute | solution.py:298
  83.7 42.3 %collective-permute-start.10 = (bf16[64,1024]{1,0:T(8,128)(2,1)S(1)}, bf16[64,1024]{1,0:T(8,128)(2,1)S(1)}, u32[]{:S(2)}, u32[]{:S(2)}) collective-permute-start(bf16[64,1024]{1,0:T(8,128)(2,1)S(1)} %dynamic-slice_convert_fusion.1), channel_id=1, source_target_pairs={{0,2},{1,3},{2,0},{3,1},{4,6},{5,7},{6,4},{7,5},{8,10},{9,11},{10,... | collective-permute-start | bytes 393224 | tf_op jit(solution)/shard_map/ppermute | solution.py:298
  84.8 71.5 %collective-permute-start.8 = (bf16[2,256,1024]{2,1,0:T(8,128)(2,1)}, bf16[2,256,1024]{2,1,0:T(8,128)(2,1)}, u32[]{:S(2)}, u32[]{:S(2)}) collective-permute-start(bf16[2,256,1024]{2,1,0:T(8,128)(2,1)} %pad_maximum_fusion.4), channel_id=1, source_target_pairs={{0,4},{1,5},{2,6},{3,7},{4,0},{5,1},{6,2},{7,3},{8,12},{9,13},{10,... | collective-permute-start | bytes 3145736 | tf_op jit(solution)/shard_map/ppermute | solution.py:298
  126.1 8.7 %collective-permute-start.11 = (bf16[64,1024]{1,0:T(8,128)(2,1)S(1)}, bf16[64,1024]{1,0:T(8,128)(2,1)S(1)}, u32[]{:S(2)}, u32[]{:S(2)}) collective-permute-start(bf16[64,1024]{1,0:T(8,128)(2,1)S(1)} %fusion.10), channel_id=1, source_target_pairs={{0,4},{1,5},{2,6},{3,7},{4,0},{5,1},{6,2},{7,3},{8,12},{9,13},{10,... | collective-permute-start | bytes 393224 | tf_op jit(solution)/shard_map/ppermute | solution.py:298
  128.2 28.9 %collective-permute-start.9 = (bf16[2,256,1024]{2,1,0:T(8,128)(2,1)}, bf16[2,256,1024]{2,1,0:T(8,128)(2,1)}, u32[]{:S(2)}, u32[]{:S(2)}) collective-permute-start(bf16[2,256,1024]{2,1,0:T(8,128)(2,1)} %pad_maximum_fusion.5), channel_id=1, source_target_pairs={{0,6},{1,7},{2,4},{3,5},{4,2},{5,3},{6,0},{7,1},{8,14},{9,15},{10,... | collective-permute-start | bytes 3145736 | tf_op jit(solution)/shard_map/ppermute | solution.py:298
  134.8 3.7 %collective-permute-start.12 = (bf16[64,1024]{1,0:T(8,128)(2,1)S(1)}, bf16[64,1024]{1,0:T(8,128)(2,1)S(1)}, u32[]{:S(2)}, u32[]{:S(2)}) collective-permute-start(bf16[64,1024]{1,0:T(8,128)(2,1)S(1)} %add_convert_fusion.1), channel_id=1, source_target_pairs={{0,1},{1,0},{2,3},{3,2},{4,5},{5,4},{6,7},{7,6},{8,9},{9,8},{10,11... | collective-permute-start | bytes 393224 | tf_op jit(solution)/shard_map/ppermute | solution.py:298
  153.0 4.0 %copy-start.3 = (bf16[1,256,1024]{2,1,0:T(8,128)(2,1)S(1)}, bf16[1,256,1024]{2,1,0:T(8,128)(2,1)}, u32[]{:S(2)}) copy-start(bf16[1,256,1024]{2,1,0:T(8,128)(2,1)} %get-tuple-element.73.refs_0_) | copy-start | bytes 1572868
  153.6 52.1 %collective-permute-start.21 = (bf16[2,256,1024]{2,1,0:T(8,128)(2,1)S(1)}, bf16[2,256,1024]{2,1,0:T(8,128)(2,1)S(1)}, u32[]{:S(2)}, u32[]{:S(2)}) collective-permute-start(bf16[2,256,1024]{2,1,0:T(8,128)(2,1)S(1)} %get-tuple-element.109), channel_id=1, source_target_pairs={{0,6},{1,7},{2,4},{3,5},{4,2},{5,3},{6,0},{7,1},{8,14},{9,15},{10,... | collective-permute-start | bytes 3145736 | tf_op jit(solution)/shard_map/ppermute | solution.py:298
  154.2 51.6 %collective-permute-start.20 = (bf16[2,256,1024]{2,1,0:T(8,128)(2,1)S(1)}, bf16[2,256,1024]{2,1,0:T(8,128)(2,1)S(1)}, u32[]{:S(2)}, u32[]{:S(2)}) collective-permute-start(bf16[2,256,1024]{2,1,0:T(8,128)(2,1)S(1)} %get-tuple-element.110), channel_id=1, source_target_pairs={{0,4},{1,5},{2,6},{3,7},{4,0},{5,1},{6,2},{7,3},{8,12},{9,13},{10,... | collective-permute-start | bytes 3145736 | tf_op jit(solution)/shard_map/ppermute | solution.py:298
  154.9 50.9 %collective-permute-start.19 = (bf16[2,256,1024]{2,1,0:T(8,128)(2,1)S(1)}, bf16[2,256,1024]{2,1,0:T(8,128)(2,1)S(1)}, u32[]{:S(2)}, u32[]{:S(2)}) collective-permute-start(bf16[2,256,1024]{2,1,0:T(8,128)(2,1)S(1)} %get-tuple-element.111), channel_id=1, source_target_pairs={{0,2},{1,3},{2,0},{3,1},{4,6},{5,7},{6,4},{7,5},{8,10},{9,11},{10,... | collective-permute-start | bytes 3145736 | tf_op jit(solution)/shard_map/ppermute | solution.py:298
  170.1 3.9 %collective-permute-start.13 = (f32[64,2048]{1,0:T(8,128)S(1)}, f32[64,2048]{1,0:T(8,128)S(1)}, u32[]{:S(2)}, u32[]{:S(2)}) collective-permute-start(f32[64,2048]{1,0:T(8,128)S(1)} %narrow.3), channel_id=1, source_target_pairs={{0,1},{1,0},{2,3},{3,2},{4,5},{5,4},{6,7},{7,6},{8,9},{9,8},{10,11... | collective-permute-start | bytes 1572872 | tf_op jit(solution)/shard_map/ppermute | solution.py:298
  174.1 31.6 %collective-permute-start.14 = (bf16[64,1024]{1,0:T(8,128)(2,1)S(1)}, bf16[64,1024]{1,0:T(8,128)(2,1)S(1)}, u32[]{:S(2)}, u32[]{:S(2)}) collective-permute-start(bf16[64,1024]{1,0:T(8,128)(2,1)S(1)} %dynamic-slice_convert_fusion), channel_id=1, source_target_pairs={{0,2},{1,3},{2,0},{3,1},{4,6},{5,7},{6,4},{7,5},{8,10},{9,11},{10,... | collective-permute-start | bytes 393224 | tf_op jit(solution)/shard_map/ppermute | solution.py:298
  189.2 18.6 %copy-start.1 = (bf16[2048,1024]{1,0:T(8,128)(2,1)}, bf16[2048,1024]{1,0:T(8,128)(2,1)S(1)}, u32[]{:S(2)}) copy-start(bf16[2048,1024]{1,0:T(8,128)(2,1)S(1)} %pieces.1) | copy-start | bytes 12582916
  205.7 2.0 copy-start.4
  205.8 2.0 copy-start.6
  205.9 2.2 copy-start.8
  208.1 30.3 %collective-permute-start.22 = (bf16[4,256,1024]{2,1,0:T(8,128)(2,1)}, bf16[4,256,1024]{2,1,0:T(8,128)(2,1)S(1)}, u32[]{:S(2)}, u32[]{:S(2)}) collective-permute-start(bf16[4,256,1024]{2,1,0:T(8,128)(2,1)} %pad_maximum_fusion.1), channel_id=1, source_target_pairs={{0,1},{1,0},{2,3},{3,2},{4,5},{5,4},{6,7},{7,6},{8,9},{9,8},{10,11... | collective-permute-start | bytes 6291464 | tf_op jit(solution)/shard_map/ppermute | solution.py:298
  208.6 5.2 %collective-permute-start.15 = (bf16[64,1024]{1,0:T(8,128)(2,1)S(1)}, bf16[64,1024]{1,0:T(8,128)(2,1)S(1)}, u32[]{:S(2)}, u32[]{:S(2)}) collective-permute-start(bf16[64,1024]{1,0:T(8,128)(2,1)S(1)} %fusion.11), channel_id=1, source_target_pairs={{0,4},{1,5},{2,6},{3,7},{4,0},{5,1},{6,2},{7,3},{8,12},{9,13},{10,... | collective-permute-start | bytes 393224 | tf_op jit(solution)/shard_map/ppermute | solution.py:298
  213.9 1.8 collective-permute-start.16
  221.3 17.1 %all-to-all-start.1 = ((bf16[8,256,128]{2,1,0:T(8,128)(2,1)}), bf16[8,256,128]{2,1,0:T(8,128)(2,1)S(1)}, u32[]{:S(2)}, u32[]{:S(2)}) async-start(bf16[8,256,128]{2,1,0:T(8,128)(2,1)} %get-tuple-element.84), calls=%async_computation.1 | async-start | bytes 1048576 | tf_op jit(solution)/shard_map/all_to_all | solution.py:295
  228.7 5.8 %collective-permute-start.17 = (f32[]{:T(128)}, f32[]{:T(128)}, u32[]{:S(2)}, u32[]{:S(2)}) collective-permute-start(f32[]{:T(128)} %reduce_sum.68), channel_id=1, source_target_pairs={{0,8},{1,9},{2,10},{3,11},{4,12},{5,13},{6,14},{7,15},{8,0},{9,1},... | collective-permute-start | bytes 20 | tf_op jit(solution)/shard_map/ppermute | solution.py:298
  235.2 2.6 collective-permute-start.18
  238.4 1.4 copy-start.15
  238.4 1.4 copy-start.11
  239.9 6.2 %copy-start.22 = (s32[128,1]{0,1:T(1,128)S(1)}, s32[128,1]{0,1:T(1,128)}, u32[]{:S(2)}) copy-start(s32[128,1]{0,1:T(1,128)} %param.15) | copy-start | bytes 1540
  239.9 25.1 %copy-start.5 = (bf16[2,256,1024]{2,1,0:T(8,128)(2,1)S(1)}, bf16[2,256,1024]{2,1,0:T(8,128)(2,1)}, u32[]{:S(2)}) copy-start(bf16[2,256,1024]{2,1,0:T(8,128)(2,1)} %copy-done.4) | copy-start | bytes 3145732
  239.9 25.1 %copy-start.7 = (bf16[2,256,1024]{2,1,0:T(8,128)(2,1)S(1)}, bf16[2,256,1024]{2,1,0:T(8,128)(2,1)}, u32[]{:S(2)}) copy-start(bf16[2,256,1024]{2,1,0:T(8,128)(2,1)} %copy-done.6) | copy-start | bytes 3145732
  239.9 25.1 %copy-start.9 = (bf16[2,256,1024]{2,1,0:T(8,128)(2,1)S(1)}, bf16[2,256,1024]{2,1,0:T(8,128)(2,1)}, u32[]{:S(2)}) copy-start(bf16[2,256,1024]{2,1,0:T(8,128)(2,1)} %copy-done.8) | copy-start | bytes 3145732
  239.9 98.7 %all-to-all-start.2 = ((bf16[16,128,1024]{2,1,0:T(8,128)(2,1)}), bf16[16,128,1024]{2,1,0:T(8,128)(2,1)}, u32[]{:S(2)}, u32[]{:S(2)}) async-start(bf16[16,128,1024]{2,1,0:T(8,128)(2,1)} %bitcast.83), calls=%async_computation.2 | async-start | bytes 8388608 | tf_op jit(solution)/shard_map/all_to_all | solution.py:287
  246.3 1.5 collective-permute-start.23
  248.5 15.7 %collective-permute-start.24 = (f32[]{:T(128)}, f32[]{:T(128)}, u32[]{:S(2)}, u32[]{:S(2)}) collective-permute-start(f32[]{:T(128)} %add.246), channel_id=1, source_target_pairs={{0,2},{1,3},{2,0},{3,1},{4,6},{5,7},{6,4},{7,5},{8,10},{9,11},{10,... | collective-permute-start | bytes 20 | tf_op jit(solution)/shard_map/ppermute | solution.py:298
  265.0 3.4 copy-start
  268.4 3.4 copy-start.2
  272.8 1.6 copy-start.12
  274.4 16.8 %copy-start.16 = (bf16[8,256,128]{2,1,0:T(8,128)(2,1)S(1)}, bf16[8,256,128]{2,1,0:T(8,128)(2,1)}, u32[]{:S(2)}) copy-start(bf16[8,256,128]{2,1,0:T(8,128)(2,1)} %copy-done.15) | copy-start | bytes 1572868
  (3 other events, 3.5 us)
